TPU v7x, 128 devices: a whole 4x4x4 slice. The times are simulated.
128 devices in a mesh: section: 8 (over z_lo, x), peer: 16 (over z_hi, y, core).
Axes of the slice: x: 4, y: 4, z: 4 (z_hi: 2, z_lo: 2; z = z_hi * 2 + z_lo), core: 2. Of those that a mesh axis runs over, the one named last changes fastest.
Arguments:
- acts: bfloat16 [8, 256, 5120], P('section', 'peer'), may hold values from -6 to 6
- cotangent: bfloat16 [8, 256, 5120], P('section', 'peer'), may hold values from -6 to 6
- gain: float32 [8, 5120], P('section'), may hold values from 0.25 to 1.75
- w_up: bfloat16 [8, 6912, 5120], P('section', 'peer'), may hold values from -0.078125 to 0.078125
- w_down: bfloat16 [8, 6912, 5120], P('section', 'peer'), may hold values from -0.078125 to 0.078125
- matching: int32 [8, 16], replicated, may hold values from 0 to 15, each once within a row
Outputs:
- grad_acts: bfloat16 [8, 256, 5120], P('section', 'peer')
- second_out: bfloat16 [8, 256, 5120], P('section', 'peer')
- grad_up: bfloat16 [8, 6912, 5120], P('section', 'peer')
- grad_down: bfloat16 [8, 6912, 5120], P('section', 'peer')
- grad_gain: float32 [8, 5120], P('section')
Inputs may be any that keep to these rules, and one draw needn't show every extreme that they name: Each row of matching is a permutation of the peers 0 to 15.
All inputs are finite; a program needn't handle non-finite values.
Results may differ from a plain program's by a relative error of at most 0.025.
Values may be sent and summed in bfloat16 or wider, within the bound.
No kernel may reach another device: no remote copies, remote signals or barrier semaphores. Data moves between devices by JAX's collectives and lax.ppermute only.
A program may use at most 128 MiB of HBM per device.

v0:
```python
import jax
import jax.numpy as jnp
from jax import lax
from jax.sharding import PartitionSpec as P


def passed_along(value, axis, steps):
    count = lax.axis_size(axis)
    leading, last = (max(0, -steps), min(count, count - steps))
    return lax.ppermute(value, axis, [(source, source + steps) for source in range(leading, last)])


def norm_rows(rows, gain_row):
    vf = rows.astype(jnp.float32)
    scale = lax.rsqrt(jnp.mean(vf * vf, axis=-1, keepdims=True) + 1e-05)
    vhat = vf * scale
    normed = (vhat * gain_row).astype(jnp.bfloat16)
    return (vf, scale, vhat, normed)


def gather_rows(local_rows):
    return lax.all_gather(local_rows, "peer", axis=0, tiled=True)


def sum_rows(left, right):
    return lax.psum_scatter(
        jnp.dot(left, right, preferred_element_type=jnp.float32).astype(jnp.bfloat16),
        "peer",
        scatter_dimension=0,
        tiled=True,
    ).astype(jnp.float32)


def hidden_of(normed_all, up):
    act = lax.dot_general(
        normed_all, up, (((1,), (1,)), ((), ())), preferred_element_type=jnp.float32
    )
    return (act, jax.nn.silu(act).astype(jnp.bfloat16))


def forward_rows(vf, scale, vhat, normed_all, up, down):
    act, hidden = hidden_of(normed_all, up)
    proj = sum_rows(hidden, down)
    return ((vf + proj).astype(jnp.bfloat16), (scale, vhat, normed_all, act, hidden))


def backward_rows(incoming, gain_row, up, down, saved):
    scale, vhat, normed_all, act, hidden = saved
    incoming_all = gather_rows(incoming)
    d_hidden = lax.dot_general(
        incoming_all, down, (((1,), (1,)), ((), ())), preferred_element_type=jnp.float32
    )
    sigma = jax.nn.sigmoid(act)
    d_act = (d_hidden * sigma * (1.0 + act * (1.0 - sigma))).astype(jnp.bfloat16)
    d_normed = sum_rows(d_act, up)
    gain_term = jnp.sum(d_normed * vhat, axis=0)
    spread = d_normed * gain_row
    d_rows = incoming.astype(jnp.float32) + scale * (
        spread - vhat * jnp.mean(spread * vhat, axis=-1, keepdims=True)
    )
    dims = (((0,), (0,)), ((), ()))
    up_term = lax.dot_general(d_act, normed_all, dims, preferred_element_type=jnp.float32)
    down_term = lax.dot_general(hidden, incoming_all, dims, preferred_element_type=jnp.float32)
    return (d_rows.astype(jnp.bfloat16), gain_term, up_term, down_term)


def local(acts, cotangent, gain, w_up, w_down, matching):
    peers = lax.axis_size("peer")
    section_id = lax.axis_index("section")
    peer_id = lax.axis_index("peer")
    rows_in = acts[0]
    count_rows = rows_in.shape[0]
    block = count_rows // peers
    width = rows_in.shape[1]
    gain_row = gain[0]
    up = w_up[0]
    down = w_down[0]
    my_match = lax.dynamic_index_in_dim(matching, section_id, 0, keepdims=False)[peer_id]
    slot_order = jnp.bitwise_xor(jnp.arange(peers, dtype=jnp.int32), my_match)
    vf_one, scale_one, vhat_one, normed_one = norm_rows(rows_in, gain_row)
    first, saved_one = forward_rows(vf_one, scale_one, vhat_one, gather_rows(normed_one), up, down)
    outgoing = first.reshape(peers, block, width)[slot_order]
    matched = lax.all_to_all(outgoing, "peer", split_axis=0, concat_axis=0, tiled=True)
    arrived = passed_along(matched, "section", 1)
    arrived = arrived.reshape(count_rows, width)
    vf_two, scale_two, vhat_two, normed_two = norm_rows(arrived, gain_row)
    normed_two_all = gather_rows(normed_two)
    second, saved_two = forward_rows(vf_two, scale_two, vhat_two, normed_two_all, up, down)
    d_two, gain_two, up_two, down_two = backward_rows(cotangent[0], gain_row, up, down, saved_two)
    returning = d_two.reshape(peers, block, width)
    sorted_back = lax.all_to_all(returning, "peer", split_axis=0, concat_axis=0, tiled=True)
    landed = passed_along(sorted_back, "section", -1)
    back_first = landed[slot_order].reshape(count_rows, width)
    d_one, gain_one, up_one, down_one = backward_rows(back_first, gain_row, up, down, saved_one)
    grad_up = (up_one + up_two).astype(jnp.bfloat16)
    grad_down = (down_one + down_two).astype(jnp.bfloat16)
    grad_gain = lax.psum(gain_one + gain_two, "peer")
    return (d_one[None], second[None], grad_up[None], grad_down[None], grad_gain[None])


def solution(mesh):
    in_specs = (
        P("section", "peer", None),
        P("section", "peer", None),
        P("section", None),
        P("section", "peer", None),
        P("section", "peer", None),
        P(),
    )
    out_specs = (
        P("section", "peer", None),
        P("section", "peer", None),
        P("section", "peer", None),
        P("section", "peer", None),
        P("section", None),
    )
    return jax.shard_map(local, mesh=mesh, in_specs=in_specs, out_specs=out_specs, check_vma=False)
```

profile of v0, /device:TPU:7, one launch (start us, length us, event | category | flops | bytes accessed | tf_op | source)
XLA Modules:
  0.0 656.6 jit_solution(1095513230101594623)
XLA Ops:
  8.3 1.7 fusion.57
  10.1 54.2 %all-gather.7.cloned.1.call-done = bf16[256,5120]{1,0:T(8,128)(2,1)} async-done(((bf16[16,5120]{1,0:T(8,128)(2,1)}), bf16[256,5120]{1,0:T(8,128)(2,1)}) %all-gather.7.cloned.1.call-update) | async-done | bytes 2621456 | tf_op jit(solution)/shard_map/all_gather | solution.py:22
  64.3 4.4 fusion.12
  68.7 5.4 convolution_convert_fusion.3
  74.1 1.3 dynamic_slice.5
  76.1 68.4 %reduce-scatter.5.cloned.1.call-done = bf16[16,5120]{1,0:T(8,128)(2,1)} async-done(((bf16[256,5120]{1,0:T(8,128)(2,1)}), bf16[16,5120]{1,0:T(8,128)(2,1)}) %reduce-scatter.5.cloned.1.call-update) | async-done | bytes 163856 | tf_op jit(solution)/shard_map/reduce_scatter | solution.py:26
  147.4 14.1 %all_to_all.10 = bf16[16,2,2560]{2,1,0:T(2,128)(2,1)S(1)} all-to-all(bf16[16,2,2560]{2,1,0:T(2,128)(2,1)S(1)} %reshape.98), channel_id=1, replica_groups=mesh['section'=8,'peer'=16] {'peer'}, dimensions={0} | all-to-all | bytes 327680 | tf_op jit(solution)/shard_map/all_to_all | solution.py:83
  161.7 2.3 collective-permute-start
  164.0 4.8 collective-permute-done
  170.4 48.3 %all-gather.9.cloned.1.call-done = bf16[256,5120]{1,0:T(8,128)(2,1)} async-done(((bf16[16,5120]{1,0:T(8,128)(2,1)}), bf16[256,5120]{1,0:T(8,128)(2,1)}) %all-gather.9.cloned.1.call-update) | async-done | bytes 2621456 | tf_op jit(solution)/shard_map/all_gather | solution.py:22
  218.7 4.4 fusion.10
  223.1 47.3 %all-gather.11.cloned.1.call-done = bf16[1,256,5120]{2,1,0:T(8,128)(2,1)} async-done(((bf16[1,16,5120]{2,1,0:T(8,128)(2,1)}), bf16[1,256,5120]{2,1,0:T(8,128)(2,1)}) %all-gather.11.cloned.1.call-update) | async-done | bytes 2621456 | tf_op jit(solution)/shard_map/all_gather | solution.py:22
  270.4 4.4 fusion.33
  274.8 5.3 convolution_convert_fusion.2
  280.2 5.4 convolution_convert_fusion
  285.6 64.9 %reduce-scatter.7.cloned.1.call-done = bf16[16,5120]{1,0:T(8,128)(2,1)} async-done(((bf16[256,5120]{1,0:T(8,128)(2,1)}), bf16[16,5120]{1,0:T(8,128)(2,1)}) %reduce-scatter.7.cloned.1.call-update) | async-done | bytes 163856 | tf_op jit(solution)/shard_map/reduce_scatter | solution.py:26
  350.5 76.6 %reduce-scatter.11.cloned.1.call-done = bf16[16,5120]{1,0:T(8,128)(2,1)} async-done(((bf16[256,5120]{1,0:T(8,128)(2,1)}), bf16[16,5120]{1,0:T(8,128)(2,1)}) %reduce-scatter.11.cloned.1.call-update) | async-done | bytes 163856 | tf_op jit(solution)/shard_map/reduce_scatter | solution.py:26
  427.1 1.9 fusion.64
  430.8 14.0 %all_to_all.11 = bf16[16,2,2560]{2,1,0:T(2,128)(2,1)S(1)} all-to-all(bf16[16,2,2560]{2,1,0:T(2,128)(2,1)S(1)} %reshape.100), channel_id=1, replica_groups=mesh['section'=8,'peer'=16] {'peer'}, dimensions={0} | all-to-all | bytes 327680 | tf_op jit(solution)/shard_map/all_to_all | solution.py:91
  445.1 2.5 collective-permute-start.1
  447.6 6.7 %collective-permute-done.1 = bf16[16,1,5120]{2,0,1:T(8,128)(2,1)S(1)} collective-permute-done((bf16[16,1,5120]{2,0,1:T(8,128)(2,1)S(1)}, bf16[16,1,5120]{2,0,1:T(8,128)(2,1)S(1)}, u32[]{:S(2)}, u32[]{:S(2)}) %collective-permute-start.1) | collective-permute-done | bytes 163872 | tf_op jit(solution)/shard_map/ppermute | solution.py:10
  454.3 1.3 gather_fusion.1
  455.9 48.4 %all-gather.13.cloned.1.call-done = bf16[256,5120]{1,0:T(8,128)(2,1)} async-done(((bf16[16,5120]{1,0:T(8,128)(2,1)}), bf16[256,5120]{1,0:T(8,128)(2,1)}) %all-gather.13.cloned.1.call-update) | async-done | bytes 2621456 | tf_op jit(solution)/shard_map/all_gather | solution.py:22
  504.3 4.4 fusion.38
  509.4 5.5 convolution_convert_fusion.1
  514.9 2.5 fusion.14
  517.5 1.3 fusion.71
  519.2 3.5 fusion
  522.7 3.5 fusion.1
  526.1 59.2 %reduce-scatter.9.cloned.1.call-done = bf16[16,5120]{1,0:T(8,128)(2,1)} async-done(((bf16[256,5120]{1,0:T(8,128)(2,1)}), bf16[16,5120]{1,0:T(8,128)(2,1)}) %reduce-scatter.9.cloned.1.call-update) | async-done | bytes 163856 | tf_op jit(solution)/shard_map/reduce_scatter | solution.py:26
  586.5 61.5 %psum.7 = f32[1,5120]{1,0:T(1,128)} all-reduce(f32[1,5120]{1,0:T(1,128)S(1)} %bitcast.95), channel_id=1, replica_groups=mesh['section'=8,'peer'=16] {'peer'}, use_global_device_ids=true, to_apply=%region_10.11 | all-reduce | flops 5120 | bytes 40960 | tf_op jit(solution)/shard_map/psum | solution.py:97
  648.0 1.7 fusion.69
  (61 shorter events, 11.3 us)
Async XLA Ops:
  7.2 57.1 %all-gather.7.cloned.1.call-start = ((), (), s32[]{:S(2)}) async-start(), calls=%async_computation.6 | async-start | bytes 2785280 | tf_op jit(solution)/shard_map/all_gather | solution.py:22
  10.0 134.4 %reduce-scatter.5.cloned.1.call-start = ((), (), s32[]{:S(2)}) async-start(), calls=%async_computation.7 | async-start | bytes 2785280 | tf_op jit(solution)/shard_map/reduce_scatter | solution.py:26
  68.7 75.8 %copy-start = (bf16[1,16,5120]{2,1,0:T(8,128)(2,1)S(1)}, bf16[1,16,5120]{2,1,0:T(8,128)(2,1)}, u32[]{:S(2)}) copy-start(bf16[1,16,5120]{2,1,0:T(8,128)(2,1)} %param.6) | copy-start | bytes 491524
  74.0 94.9 %copy-start.9 = (f32[1,5120]{1,0:T(1,128)S(1)}, f32[1,5120]{1,0:T(1,128)}, u32[]{:S(2)}) copy-start(f32[1,5120]{1,0:T(1,128)} %param.8) | copy-start | bytes 61444
  74.1 144.6 %all-gather.9.cloned.1.call-start = ((), (), s32[]{:S(2)}) async-start(), calls=%async_computation.8 | async-start | bytes 2785280 | tf_op jit(solution)/shard_map/all_gather | solution.py:22
  161.7 7.1 %collective-permute-start = (bf16[16,1,5120]{2,0,1:T(8,128)(2,1)S(1)}, bf16[16,1,5120]{2,0,1:T(8,128)(2,1)S(1)}, u32[]{:S(2)}, u32[]{:S(2)}) collective-permute-start(bf16[16,1,5120]{2,0,1:T(8,128)(2,1)S(1)} %copy.12), channel_id=1, source_target_pairs={{0,16},{16,32},{32,48},{48,64},{64,80},{80,96},{96,112},{1,17},{17... | collective-permute-start | bytes 491528 | tf_op jit(solution)/shard_map/ppermute | solution.py:10
  169.8 100.6 %all-gather.11.cloned.1.call-start = ((), (), s32[]{:S(2)}) async-start(), calls=%async_computation.12 | async-start | bytes 2785280 | tf_op jit(solution)/shard_map/all_gather | solution.py:22
  170.4 180.1 %reduce-scatter.7.cloned.1.call-start = ((), (), s32[]{:S(2)}) async-start(), calls=%async_computation.9 | async-start | bytes 2785280 | tf_op jit(solution)/shard_map/reduce_scatter | solution.py:26
  223.1 57.1 %copy-start.5 = (f32[256,432]{0,1:T(8,128)}, f32[256,432]{0,1:T(8,128)S(1)}, u32[]{:S(2)}) copy-start(f32[256,432]{0,1:T(8,128)S(1)} %fusion.10) | copy-start | bytes 1327108
  280.1 148.9 %copy-start.10 = (bf16[1,16,5120]{2,1,0:T(8,128)(2,1)S(1)}, bf16[1,16,5120]{2,1,0:T(8,128)(2,1)}, u32[]{:S(2)}) copy-start(bf16[1,16,5120]{2,1,0:T(8,128)(2,1)} %param.7) | copy-start | bytes 491524
  280.1 147.0 %reduce-scatter.11.cloned.1.call-start = ((), (), s32[]{:S(2)}) async-start(), calls=%async_computation.11 | async-start | bytes 2785280 | tf_op jit(solution)/shard_map/reduce_scatter | solution.py:26
  285.5 218.8 %all-gather.13.cloned.1.call-start = ((), (), s32[]{:S(2)}) async-start(), calls=%async_computation.13 | async-start | bytes 2785280 | tf_op jit(solution)/shard_map/all_gather | solution.py:22
  445.1 9.3 %collective-permute-start.1 = (bf16[16,1,5120]{2,0,1:T(8,128)(2,1)S(1)}, bf16[16,1,5120]{2,0,1:T(8,128)(2,1)S(1)}, u32[]{:S(2)}, u32[]{:S(2)}) collective-permute-start(bf16[16,1,5120]{2,0,1:T(8,128)(2,1)S(1)} %copy.14), channel_id=1, source_target_pairs={{16,0},{32,16},{48,32},{64,48},{80,64},{96,80},{112,96},{17,1},{33... | collective-permute-start | bytes 491528 | tf_op jit(solution)/shard_map/ppermute | solution.py:10
  455.7 129.6 %reduce-scatter.9.cloned.1.call-start = ((), (), s32[]{:S(2)}) async-start(), calls=%async_computation.10 | async-start | bytes 2785280 | tf_op jit(solution)/shard_map/reduce_scatter | solution.py:26
  508.7 0.7 copy-start.7
  509.4 5.5 copy-start.2
  514.9 2.5 copy-start.1
  514.9 2.5 copy-start.8
  517.5 1.7 copy-start.3
  519.2 3.5 copy-start.4
  522.7 125.4 %copy-start.6 = (bf16[16,5120]{1,0:T(8,128)(2,1)S(1)}, bf16[16,5120]{1,0:T(8,128)(2,1)}, u32[]{:S(2)}) copy-start(bf16[16,5120]{1,0:T(8,128)(2,1)} %gather_fusion.1) | copy-start | bytes 491524
Sparse Core Ops, SparseCore 0:
  11.0 53.2 all-gather.6
  74.2 70.2 reduce-scatter.4
  169.9 48.7 all-gather.8
  221.3 49.0 all-gather.10
  280.2 70.2 reduce-scatter.6
  354.9 72.1 reduce-scatter.10
  455.8 48.4 all-gather.12
  515.0 70.2 reduce-scatter.8
where the time goes:
time: 663 us; the launch traced here: 657 us
  waiting for transfers between devices  479 us (72%)
  blocking collectives  89.6 us (14%)
  matrix products  49.8 us (8%)
  between operations  14.4 us (2%)
  other arithmetic  12.6 us (2%)
    reduce_scatter x4, waiting for transfers between devices, sum_rows(): lax.psum_scatter(jnp.dot(left, right, preferred_element_type=jnp.float32)...  269 us
    all_gather x4, waiting for transfers between devices, gather_rows(): return lax.all_gather(local_rows, 'peer', axis=0, tiled=True)  198 us
    psum x1, blocking collectives, local(): grad_gain = lax.psum(gain_one + gain_two, 'peer')  61.5 us
    dot_general x4, matrix products, sum_rows(): jnp.dot(left, right, preferred_element_type=jnp.float32)  21.5 us
    all_to_all x1, blocking collectives, local(): lax.all_to_all(outgoing, 'peer', split_axis=0, concat_axis=0, tiled=True)  14.1 us
    all_to_all x1, blocking collectives, local(): lax.all_to_all(returning, 'peer', split_axis=0, concat_axis=0, tiled=True)  14 us
  transfers between devices with their start and end apart: 10, of which 10 were waited for; matrix products, arithmetic and copies ran while one was open for 3% of the time, Pallas kernels for 0%

commit v1 on v0

v1 whole, which is shorter than its diff:
```python
import functools

import jax
import jax.numpy as jnp
from jax import lax
from jax.experimental import pallas as pl
from jax.experimental.pallas import tpu as pltpu
from jax.sharding import PartitionSpec as P

BF = jnp.bfloat16
F32 = jnp.float32
ROWS = 16
CHIPS = 8
TALL = CHIPS * ROWS
CHUNK = 1024
VMEM_MB = 1024 * 1024

SAME_CORE = [[2 * chip + core for chip in range(CHIPS)] for core in range(2)]
ALONG_Y = [[z * 8 + y * 2 + core for y in range(4)] for z in range(2) for core in range(2)]
ALONG_Z = [[z * 8 + y * 2 + core for z in range(2)] for y in range(4) for core in range(2)]
SIBLING = [(peer, peer ^ 1) for peer in range(16)]

VM = pl.BlockSpec(memory_space=pltpu.VMEM)
SM = pl.BlockSpec(memory_space=pltpu.SMEM)
ANY = pl.BlockSpec(memory_space=pl.ANY)


def dot_nt(left, right):
    return lax.dot_general(left, right, (((1,), (1,)), ((), ())), preferred_element_type=F32)


def dot_nn(left, right):
    return jnp.dot(left, right, preferred_element_type=F32)


def chunks(width):
    return [slice(at, at + CHUNK) for at in range(0, width, CHUNK)]


def row_scale(x_ref):
    rows, width = x_ref.shape
    total = jnp.zeros((rows, 128), F32)
    for at in range(0, width, 128):
        piece = x_ref[:, at : at + 128].astype(F32)
        total = total + piece * piece
    mean = jnp.sum(total, axis=-1, keepdims=True) * (1.0 / width)
    return lax.rsqrt(mean + 1e-05)


class Weights:
    def __init__(self, sources, buffer, sems):
        self.copies = {}
        for at, cols in enumerate(chunks(sources[0].shape[1])):
            for which, source in enumerate(sources):
                copy = pltpu.make_async_copy(source.at[:, cols], buffer.at[which, :, cols], sems.at[at, which])
                copy.start()
                self.copies[at, which] = copy

    def wait(self, at):
        for which in range(2):
            self.copies[at, which].wait()


def silu_parts(act):
    sigma = jax.nn.sigmoid(act)
    return act * sigma, sigma * (1.0 + act * (1.0 - sigma))


def one_hot(index, width):
    lanes = lax.broadcasted_iota(jnp.int32, (index.shape[0], width), 1)
    return jnp.where(lanes == index, 1.0, 0.0).astype(BF)


def forward_kernel(x, gain, up_a, up_b, down_a, down_b, proj, normed, act, hidden, scale_out, wu, wd, su, sd):
    width = x.shape[1]
    ups = Weights((up_a, up_b), wu, su)
    downs = Weights((down_a, down_b), wd, sd)
    scale = row_scale(x)
    scale_out[...] = jnp.broadcast_to(scale, scale_out.shape)
    total = [None, None]
    for at, cols in enumerate(chunks(width)):
        piece = (x[:, cols].astype(F32) * scale * gain[:, cols]).astype(BF)
        normed[:, cols] = piece
        ups.wait(at)
        for half in range(2):
            term = dot_nt(piece, wu[half, :, cols])
            total[half] = term if at == 0 else total[half] + term
    for half in range(2):
        act[half] = total[half]
        hidden[half] = silu_parts(total[half])[0].astype(BF)
    for at, cols in enumerate(chunks(width)):
        downs.wait(at)
        proj[:, cols] = (dot_nn(hidden[0], wd[0, :, cols]) + dot_nn(hidden[1], wd[1, :, cols])).astype(BF)


def cot_kernel(cot_all, pick, down_a, down_b, cot, d_hidden, wd, sd):
    width = cot_all.shape[1]
    downs = Weights((down_a, down_b), wd, sd)
    choose = one_hot(pick[...], cot_all.shape[0])
    total = [None, None]
    for at, cols in enumerate(chunks(width)):
        piece = dot_nn(choose, cot_all[:, cols]).astype(BF)
        cot[:, cols] = piece
        downs.wait(at)
        for half in range(2):
            term = dot_nt(piece, wd[half, :, cols])
            total[half] = term if at == 0 else total[half] + term
    for half in range(2):
        d_hidden[half] = total[half]


def second_kernel(
    x, gain, d_hidden, to_target, own_target, up_a, up_b, down_a, down_b,
    d_normed, proj, normed, d_act, hidden, gain_term, own_rows, wu, wd, su, sd,
):
    width = x.shape[1]
    ups = Weights((up_a, up_b), wu, su)
    downs = Weights((down_a, down_b), wd, sd)
    scale = row_scale(x)
    total = [None, None]
    for at, cols in enumerate(chunks(width)):
        piece = (x[:, cols].astype(F32) * scale * gain[:, cols]).astype(BF)
        normed[:, cols] = piece
        ups.wait(at)
        for half in range(2):
            term = dot_nt(piece, wu[half, :, cols])
            total[half] = term if at == 0 else total[half] + term
    sort = one_hot(to_target[...], TALL)
    own = one_hot(own_target[...], TALL)
    moved = []
    for half in range(2):
        value, slope = silu_parts(total[half])
        rounded = value.astype(BF)
        hidden[half] = rounded
        moved.append(dot_nn(sort, rounded).astype(BF))
        d_act[half] = (d_hidden[half] * slope).astype(BF)
    for at, cols in enumerate(chunks(width)):
        term = dot_nn(d_act[0], wu[0, :, cols]) + dot_nn(d_act[1], wu[1, :, cols])
        d_normed[:, cols] = term.astype(BF)
        gain_term[:, cols] = jnp.sum(term * (x[:, cols].astype(F32) * scale), axis=0, keepdims=True)
    for at, cols in enumerate(chunks(width)):
        downs.wait(at)
        proj[:, cols] = (dot_nn(moved[0], wd[0, :, cols]) + dot_nn(moved[1], wd[1, :, cols])).astype(BF)
        own_rows[:, cols] = dot_nn(own, x[:, cols]).astype(BF)


def first_back_kernel(
    c, x, scale_in, act, gain_two, up_a, up_b, down_a, down_b, d_normed, d_act, wu, wd, su, sd
):
    width = x.shape[1]
    downs = Weights((down_a, down_b), wd, sd)
    ups = Weights((up_a, up_b), wu, su)
    scale = scale_in[:, :1]
    total = [None, None]
    for at, cols in enumerate(chunks(width)):
        downs.wait(at)
        for half in range(2):
            term = dot_nt(c[:, cols], wd[half, :, cols])
            total[half] = term if at == 0 else total[half] + term
    for half in range(2):
        d_act[half] = (total[half] * silu_parts(act[half])[1]).astype(BF)
    gain_pieces = []
    for at, cols in enumerate(chunks(width)):
        ups.wait(at)
        term = dot_nn(d_act[0], wu[0, :, cols]) + dot_nn(d_act[1], wu[1, :, cols])
        d_normed[:, cols] = term.astype(BF)
        gain_pieces.append(
            jnp.sum(term * (x[:, cols].astype(F32) * scale), axis=0, keepdims=True) + gain_two[:, cols]
        )
    line = jnp.concatenate(gain_pieces, axis=1)
    lanes = width // 8
    grid = jnp.concatenate([line[:, lanes * at : lanes * (at + 1)] for at in range(8)], axis=0)
    high = grid.astype(BF)
    low = (grid - high.astype(F32)).astype(BF)
    both = jnp.concatenate([high.astype(F32), low.astype(F32)], axis=0).astype(BF)
    for block in range(CHIPS):
        d_normed[block * ROWS : (block + 1) * ROWS, width:] = both


def add_blocks(blocks, cols):
    total = blocks[0:ROWS, cols].astype(F32)
    for block in range(1, CHIPS):
        total = total + blocks[block * ROWS : (block + 1) * ROWS, cols].astype(F32)
    return total


def add_kernel(blocks, x, out):
    for cols in chunks(x.shape[1]):
        out[:, cols] = (x[:, cols].astype(F32) + add_blocks(blocks, cols)).astype(BF)


def rows_back_kernel(blocks, x, c, gain, *rest):
    out, spread = rest[0], rest[-1]
    width = x.shape[1]
    scale = row_scale(x)
    along = jnp.zeros((ROWS, 128), F32)
    for cols in chunks(width):
        piece = add_blocks(blocks, cols) * gain[:, cols]
        spread[:, cols] = piece
        product = piece * (x[:, cols].astype(F32) * scale)
        for at in range(0, CHUNK, 128):
            along = along + product[:, at : at + 128]
    mean = jnp.sum(along, axis=-1, keepdims=True) * (1.0 / width)
    for cols in chunks(width):
        vhat = x[:, cols].astype(F32) * scale
        out[:, cols] = (c[:, cols].astype(F32) + scale * (spread[:, cols] - vhat * mean)).astype(BF)
    if len(rest) == 3:
        extra = add_blocks(blocks, slice(width, blocks.shape[1]))
        rest[1][...] = extra[:8] + extra[8:]


def grads_kernel(*refs):
    normed, c, d_act, hidden = refs[0:4], refs[4:8], refs[8:12], refs[12:16]
    out_up, out_down, left_up, left_down = refs[16:20]

    @pl.when(pl.program_id(0) == 0)
    def _():
        for at in range(4):
            rows = slice(at * TALL, (at + 1) * TALL)
            left_up[:, rows] = d_act[at][...].T
            left_down[:, rows] = hidden[at][...].T

    right = jnp.concatenate([ref[...] for ref in normed], axis=0)
    out_up[...] = dot_nn(left_up[...], right).astype(BF)
    right = jnp.concatenate([ref[...] for ref in c], axis=0)
    out_down[...] = dot_nn(left_down[...], right).astype(BF)


def shape(*dims, dtype=BF):
    return jax.ShapeDtypeStruct(dims, dtype)


def call(kernel, outs, ins, scratch=(), limit=48, flops=0, moved=0):
    return pl.pallas_call(
        kernel,
        out_shape=outs,
        in_specs=ins,
        out_specs=jax.tree.map(lambda _: VM, outs),
        scratch_shapes=scratch,
        compiler_params=pltpu.CompilerParams(vmem_limit_bytes=limit * VMEM_MB),
        cost_estimate=pl.CostEstimate(flops=flops, bytes_accessed=moved, transcendentals=0),
    )


def weight_scratch(units, width, count):
    steps = width // CHUNK
    return [pltpu.VMEM((2, units, width), BF)] * count + [pltpu.SemaphoreType.DMA((steps, 2))] * count


def to_chips(blocks):
    return lax.all_to_all(
        blocks, "peer", split_axis=0, concat_axis=0, tiled=True, axis_index_groups=SAME_CORE
    )


def from_chips(rows):
    spread = jnp.broadcast_to(rows[None], (CHIPS,) + rows.shape).reshape(TALL, rows.shape[1])
    return to_chips(spread)


def swap(value):
    return lax.ppermute(value, "peer", SIBLING)


def passed_along(value, steps):
    count = lax.axis_size("section")
    leading, last = (max(0, -steps), min(count, count - steps))
    return lax.ppermute(value, "section", [(source, source + steps) for source in range(leading, last)])


def local(acts, cotangent, gain, w_up, w_down, matching):
    section = lax.axis_index("section")
    peer = lax.axis_index("peer")
    core = peer % 2
    chip = peer // 2
    rows_in, up, down = acts[0], w_up[0], w_down[0]
    units, width = up.shape
    flops = 2 * TALL * units * 2 * width
    moved = 2 * units * width * 2

    up_b, down_b = swap(up), swap(down)
    cot_all = lax.all_gather(cotangent[0], "peer", axis=0, tiled=True)

    before = lax.dynamic_index_in_dim(matching, jnp.maximum(section - 1, 0), 0, keepdims=False)
    mine = jnp.where(core == 0, before[0::2], before[1::2])
    chips = jnp.arange(CHIPS, dtype=jnp.int32)
    slots = jnp.arange(ROWS, dtype=jnp.int32)
    pick = (slots[None, :] ^ mine[:, None]) * ROWS + (2 * chips + core)[:, None]
    owner = jnp.array([z * 4 + y for y in range(4) for z in range(2)], jnp.int32)
    to_target = (owner[:, None, None] * 2 + jnp.arange(2, dtype=jnp.int32)[None, :, None]) ^ mine[None, None, :]
    to_target = (to_target + chips[None, None, :] * ROWS).reshape(TALL, 1)
    own_target = (chip * 2 + jnp.arange(2, dtype=jnp.int32))[:, None] ^ mine[None, :]
    own_target = (own_target + chips[None, :] * ROWS).reshape(ROWS, 1)
    pick = pick.reshape(TALL, 1)

    x_one = from_chips(rows_in)
    proj, normed_one, act_one, hidden_one, scale_one = call(
        forward_kernel,
        [shape(TALL, width), shape(TALL, width), shape(2, TALL, units, dtype=F32), shape(2, TALL, units),
         shape(TALL, 128, dtype=F32)],
        [VM, VM, ANY, ANY, ANY, ANY],
        weight_scratch(units, width, 2), flops=2 * flops, moved=2 * moved,
    )(x_one, gain, up, up_b, down, down_b)
    blocks = to_chips(proj)
    first = call(add_kernel, shape(ROWS, width), [VM, VM])(blocks, rows_in)
    arrived = passed_along(first, 1)
    cot, d_hidden = call(
        cot_kernel,
        [shape(TALL, width), shape(2, TALL, units, dtype=F32)],
        [VM, VM, ANY, ANY],
        weight_scratch(units, width, 1), flops=flops, moved=moved,
    )(cot_all, pick, down, down_b)
    x_two = from_chips(arrived)
    d_normed, proj, normed_two, d_act_two, hidden_two, gain_two, own_rows = call(
        second_kernel,
        [shape(TALL, width), shape(TALL, width), shape(TALL, width), shape(2, TALL, units), shape(2, TALL, units),
         shape(1, width, dtype=F32), shape(ROWS, width)],
        [VM] * 5 + [ANY] * 4,
        weight_scratch(units, width, 2), flops=3 * flops, moved=2 * moved,
    )(x_two, gain, d_hidden, to_target, own_target, up, up_b, down, down_b)

    half = lax.psum_scatter(proj, "peer", scatter_dimension=0, tiled=True, axis_index_groups=ALONG_Y)
    total = lax.psum_scatter(half, "peer", scatter_dimension=0, tiled=True, axis_index_groups=ALONG_Z)
    second = (own_rows.astype(F32) + total.astype(F32)).astype(BF).reshape(2, ROWS // 2, width)
    kept = lax.dynamic_index_in_dim(second, core, 0, keepdims=False)
    given = swap(lax.dynamic_index_in_dim(second, 1 - core, 0, keepdims=False))
    even = jnp.where(core == 0, kept, given)
    odd = jnp.where(core == 0, given, kept)
    second = jnp.stack([even, odd], axis=1).reshape(ROWS, width)

    blocks = to_chips(d_normed)
    cot_own = lax.dynamic_slice_in_dim(cot, chip * ROWS, ROWS, 0)
    d_two = call(
        rows_back_kernel, [shape(ROWS, width)], [VM] * 4, [pltpu.VMEM((ROWS, width), F32)]
    )(blocks, arrived, cot_own, gain)[0]
    landed = passed_along(d_two, -1)
    c_one = from_chips(landed)
    d_normed, d_act_one = call(
        first_back_kernel,
        [shape(TALL, width + width // 8), shape(2, TALL, units)],
        [VM] * 5 + [ANY] * 4,
        weight_scratch(units, width, 2), flops=2 * flops, moved=2 * moved,
    )(c_one, x_one, scale_one, act_one, gain_two, up, up_b, down, down_b)
    blocks = to_chips(d_normed)
    d_one, gain_sum = call(
        rows_back_kernel, [shape(ROWS, width), shape(8, width // 8, dtype=F32)], [VM] * 4,
        [pltpu.VMEM((ROWS, width), F32)],
    )(blocks, rows_in, landed, gain)
    grad_gain = (gain_sum + swap(gain_sum)).reshape(1, width)

    wide = [normed_one, swap(normed_one), normed_two, swap(normed_two)]
    wide += [c_one, swap(c_one), cot, swap(cot)]
    slim = [d_act_one[0], swap(d_act_one[1]), d_act_two[0], swap(d_act_two[1])]
    slim += [hidden_one[0], swap(hidden_one[1]), hidden_two[0], swap(hidden_two[1])]
    step = 512
    grad_up, grad_down = pl.pallas_call(
        grads_kernel,
        grid=(width // step,),
        out_shape=[shape(units, width)] * 2,
        in_specs=[pl.BlockSpec((TALL, step), lambda i: (0, i))] * 8 + [VM] * 8,
        out_specs=[pl.BlockSpec((units, step), lambda i: (0, i))] * 2,
        scratch_shapes=[pltpu.VMEM((units, 4 * TALL), BF)] * 2,
        compiler_params=pltpu.CompilerParams(vmem_limit_bytes=32 * VMEM_MB),
        cost_estimate=pl.CostEstimate(flops=4 * flops, bytes_accessed=4 * moved, transcendentals=0),
    )(*wide, *slim)
    return (d_one[None], second[None], grad_up[None], grad_down[None], grad_gain)


def solution(mesh):
    wide = P("section", "peer", None)
    in_specs = (wide, wide, P("section", None), wide, wide, P())
    out_specs = (wide, wide, wide, wide, P("section", None))
    return jax.shard_map(local, mesh=mesh, in_specs=in_specs, out_specs=out_specs, check_vma=False)
```

time: 663 us -> 255 us (0.38)
  waiting for transfers between devices: 479 us -> 98.3 us
  blocking collectives: 89.6 us -> 27.9 us
  matrix products: 49.8 us -> 0 us
  Pallas kernels: 0 us -> 49.5 us
  starting transfers between devices: 5.3 us -> 33.6 us
  local copies, waits for them, and re-layouts: 5.45 us -> 29 us
  other arithmetic: 12.6 us -> 1.38 us
    reduce_scatter x4 -> x2, waiting for transfers between devices: 269 us -> 0.02 us  [the longest x1 0.02 us: local(): lax.psum_scatter(half, 'peer', scatter_dimension=0, tiled=True, axis_inde...]
    all_gather x4 -> x1, waiting for transfers between devices: 198 us -> 0.01 us  [local(): cot_all = lax.all_gather(cotangent[0], 'peer', axis=0, tiled=True)]
    all_to_all x0 -> x5, waiting for transfers between devices: none -> 87.4 us  [to_chips(): lax.all_to_all(blocks, 'peer', split_axis=0, concat_axis=0, tiled=True, a...]
    psum x1 -> x0, blocking collectives: 61.5 us -> none  [local(): grad_gain = lax.psum(gain_one + gain_two, 'peer')]
    dot_general x12 -> x0, matrix products: 49.8 us -> none  [the longest x4 21.5 us: sum_rows(): jnp.dot(left, right, preferred_element_type=jnp.float32)]
    pallas_call x0 -> x8, Pallas kernels: none -> 49.5 us  [the longest x1 13 us: local(): call(second_kernel, [shape(TALL, width), shape(TALL, width), shape(TALL,...]
    all_to_all x0 -> x5, starting transfers between devices: none -> 21.4 us  [to_chips(): lax.all_to_all(blocks, 'peer', split_axis=0, concat_axis=0, tiled=True, a...]
    unnamed x26 -> x53, local copies, waits for them, and re-layouts: 1.59 us -> 17.9 us
  transfers between devices with their start and end apart: 10 -> 22, of which waited for: 10 -> 8; matrix products, arithmetic and copies ran while one was open for 3% -> 5% of each run, Pallas kernels for 0% -> 14%
where the time goes in v1:
time: 255 us; the launch traced here: 254 us
  waiting for transfers between devices  98.3 us (39%)
  Pallas kernels  49.5 us (19%)
  starting transfers between devices  33.6 us (13%)
  local copies, waits for them, and re-layouts  29 us (11%)
  blocking collectives  27.9 us (11%)
  between operations  14.2 us (6%)
    all_to_all x5, waiting for transfers between devices, to_chips(): lax.all_to_all(blocks, 'peer', split_axis=0, concat_axis=0, tiled=True, a...  87.4 us
    all_to_all x1, blocking collectives, to_chips(): lax.all_to_all(blocks, 'peer', split_axis=0, concat_axis=0, tiled=True, a...  27.9 us
    all_to_all x5, starting transfers between devices, to_chips(): lax.all_to_all(blocks, 'peer', split_axis=0, concat_axis=0, tiled=True, a...  21.4 us
    unnamed x53, local copies, waits for them, and re-layouts  17.9 us
    pallas_call x1, Pallas kernels, local(): call(second_kernel, [shape(TALL, width), shape(TALL, width), shape(TALL,...  13 us
    pallas_call x1, Pallas kernels, local(): pl.pallas_call(grads_kernel, grid=(width // step,), out_shape=[shape(unit...  11.3 us
    ppermute x2, waiting for transfers between devices, passed_along(): lax.ppermute(value, 'section', [(source, source + steps) for source in ra...  10.5 us
    pallas_call x1, Pallas kernels, local(): call(first_back_kernel, [shape(TALL, width + width // 8), shape(2, TALL,...  9.06 us
  transfers between devices with their start and end apart: 22, of which 8 were waited for; matrix products, arithmetic and copies ran while one was open for 5% of the time, Pallas kernels for 14%

profile of v1, /device:TPU:7, one launch (start us, length us, event | category | flops | bytes accessed | tf_op | source)
XLA Modules:
  0.0 253.7 jit_solution(717938788677774345)
XLA Ops:
  9.2 27.9 %all_to_all.57 = bf16[8,16,5120]{2,1,0:T(8,128)(2,1)S(1)} all-to-all(bf16[8,16,5120]{2,1,0:T(8,128)(2,1)S(1)} %broadcast_in_dim.15), channel_id=1, replica_groups={{0,2,4,6,8,10,12,14},{1,3,5,7,9,11,13,15},{16,18,20,22,24,26,28,30},{17..., dimensions={0} | all-to-all | bytes 2621440 | tf_op jit(solution)/shard_map/all_to_all | solution.py:251
  37.1 8.9 %shard_map.110 = (bf16[128,5120]{1,0:T(8,128)(2,1)S(1)}, bf16[128,5120]{1,0:T(8,128)(2,1)S(1)}, f32[2,128,432]{2,1,0:T(8,128)S(1)}, bf16[2,128,432]{2,1,0:T(8,128)(2,1)S(1)}, f32[128,128]{1,0:T(8,128)S(1)}) custom-call(bf16[128,5120]{1,0:T(8,128)(2,1)S(1)} %bitcast.53, f32[1,5120]{1,0:T(1,128)S(1)} %copy-done.8, bf16[432,5120]{1,0:T(8,128)(2,1)} %bitcast.74, ...), custom_call_target="tpu_custom_call" | custom-call | flops 2264924160 | bytes 17694720 | tf_op jit(solution)/shard_map/pallas_call | solution.py:297
  47.5 1.1 copy-done.21
  49.7 3.7 %all-to-all-start.1 = ((bf16[8,16,5120]{2,1,0:T(8,128)(2,1)}), bf16[8,16,5120]{2,1,0:T(8,128)(2,1)S(1)}, u32[]{:S(2)}, u32[]{:S(2)}) async-start(bf16[8,16,5120]{2,1,0:T(8,128)(2,1)} %bitcast.66), calls=%async_computation.1 | async-start | bytes 2621440 | tf_op jit(solution)/shard_map/all_to_all | solution.py:251
  53.6 22.7 %all-to-all-done.1 = bf16[8,16,5120]{2,1,0:T(8,128)(2,1)S(1)} async-done(((bf16[8,16,5120]{2,1,0:T(8,128)(2,1)}), bf16[8,16,5120]{2,1,0:T(8,128)(2,1)S(1)}, u32[]{:S(2)}, u32[]{:S(2)}) %all-to-all-start.1) | async-done | bytes 1310752 | tf_op jit(solution)/shard_map/all_to_all | solution.py:251
  76.5 2.2 collective-permute-start.2
  78.7 4.6 %collective-permute-done.2.x = bf16[16,5120]{1,0:T(8,128)(2,1)S(1)} collective-permute-done((bf16[16,5120]{1,0:T(8,128)(2,1)S(1)}, bf16[16,5120]{1,0:T(8,128)(2,1)S(1)}, u32[]{:S(2)}, u32[]{:S(2)}) %collective-permute-start.2) | collective-permute-done | bytes 163872 | tf_op jit(solution)/shard_map/ppermute | solution.py:268
  83.4 1.2 broadcast_in_dim.16
  84.5 4.4 %all-to-all-start.2 = ((bf16[8,16,5120]{2,1,0:T(8,128)(2,1)}), bf16[8,16,5120]{2,1,0:T(8,128)(2,1)}, u32[]{:S(2)}, u32[]{:S(2)}) async-start(bf16[8,16,5120]{2,1,0:T(8,128)(2,1)} %broadcast_in_dim.16), calls=%async_computation.2 | async-start | bytes 2621440 | tf_op jit(solution)/shard_map/all_to_all | solution.py:251
  89.8 1.7 copy-done.1
  91.5 5.4 %shard_map.112 = (bf16[128,5120]{1,0:T(8,128)(2,1)S(1)}, f32[2,128,432]{2,1,0:T(8,128)S(1)}) custom-call(bf16[256,5120]{1,0:T(8,128)(2,1)S(1)} %bitcast.61, s32[128,1]{1,0:T(8,128)S(1)} %add.143.pick, bf16[432,5120]{1,0:T(8,128)(2,1)} %bitcast.70, bf16[432,5120]{1,0:T(8,128)(2,1)} %collective-permute-done.1.down_b), custom_call_target="tpu_custom_call" | custom-call | flops 1132462080 | bytes 8847360 | tf_op jit(solution)/shard_map/pallas_call | solution.py:307
  98.0 11.0 %all-to-all-done.2 = bf16[8,16,5120]{2,1,0:T(8,128)(2,1)} async-done(((bf16[8,16,5120]{2,1,0:T(8,128)(2,1)}), bf16[8,16,5120]{2,1,0:T(8,128)(2,1)}, u32[]{:S(2)}, u32[]{:S(2)}) %all-to-all-start.2) | async-done | bytes 1310752 | tf_op jit(solution)/shard_map/all_to_all | solution.py:251
  109.1 13.0 %shard_map.113 = (bf16[128,5120]{1,0:T(8,128)(2,1)S(1)}, bf16[128,5120]{1,0:T(8,128)(2,1)}, bf16[128,5120]{1,0:T(8,128)(2,1)S(1)}, bf16[2,128,432]{2,1,0:T(8,128...) custom-call(bf16[128,5120]{1,0:T(8,128)(2,1)} %bitcast.6.x, ...), custom_call_target="tpu_custom_call" | custom-call | flops 3397386240 | bytes 17694720 | tf_op jit(solution)/shard_map/pallas_call | solution.py:314
  125.3 1.1 copy-done.23
  126.4 3.6 %all-to-all-start.3 = ((bf16[8,16,5120]{2,1,0:T(8,128)(2,1)}), bf16[8,16,5120]{2,1,0:T(8,128)(2,1)S(1)}, u32[]{:S(2)}, u32[]{:S(2)}) async-start(bf16[8,16,5120]{2,1,0:T(8,128)(2,1)} %bitcast.67), calls=%async_computation.3 | async-start | bytes 2621440 | tf_op jit(solution)/shard_map/all_to_all | solution.py:251
  130.9 25.3 %all-to-all-done.3 = bf16[8,16,5120]{2,1,0:T(8,128)(2,1)S(1)} async-done(((bf16[8,16,5120]{2,1,0:T(8,128)(2,1)}), bf16[8,16,5120]{2,1,0:T(8,128)(2,1)S(1)}, u32[]{:S(2)}, u32[]{:S(2)}) %all-to-all-start.3) | async-done | bytes 1310752 | tf_op jit(solution)/shard_map/all_to_all | solution.py:251
  156.6 2.3 collective-permute-start.3
  158.9 5.9 %collective-permute-done.3.c = bf16[16,5120]{1,0:T(8,128)(2,1)S(1)} collective-permute-done((bf16[16,5120]{1,0:T(8,128)(2,1)S(1)}, bf16[16,5120]{1,0:T(8,128)(2,1)S(1)}, u32[]{:S(2)}, u32[]{:S(2)}) %collective-permute-start.3) | collective-permute-done | bytes 163872 | tf_op jit(solution)/shard_map/ppermute | solution.py:268
  164.8 1.2 broadcast_in_dim.17
  165.9 6.1 %all-to-all-start.4 = ((bf16[8,16,5120]{2,1,0:T(8,128)(2,1)}), bf16[8,16,5120]{2,1,0:T(8,128)(2,1)S(1)}, u32[]{:S(2)}, u32[]{:S(2)}) async-start(bf16[8,16,5120]{2,1,0:T(8,128)(2,1)} %broadcast_in_dim.17), calls=%async_computation.4 | async-start | bytes 2621440 | tf_op jit(solution)/shard_map/all_to_all | solution.py:251
  172.1 3.1 %collective-permute-start.5 = (bf16[128,5120]{1,0:T(8,128)(2,1)}, bf16[128,5120]{1,0:T(8,128)(2,1)}, u32[]{:S(2)}, u32[]{:S(2)}) collective-permute-start(bf16[128,5120]{1,0:T(8,128)(2,1)} %copy-done.21), channel_id=1, source_target_pairs={{0,1},{1,0},{2,3},{3,2},{4,5},{5,4},{6,7},{7,6},{8,9},{9,8},{10,11... | collective-permute-start | bytes 3932168 | tf_op jit(solution)/shard_map/ppermute | solution.py:262
  176.5 1.7 slice_bitcast_fusion.4
  178.9 13.3 %all-to-all-done.4 = bf16[8,16,5120]{2,1,0:T(8,128)(2,1)S(1)} async-done(((bf16[8,16,5120]{2,1,0:T(8,128)(2,1)}), bf16[8,16,5120]{2,1,0:T(8,128)(2,1)S(1)}, u32[]{:S(2)}, u32[]{:S(2)}) %all-to-all-start.4) | async-done | bytes 1310752 | tf_op jit(solution)/shard_map/all_to_all | solution.py:251
  193.2 9.1 %shard_map.115 = (bf16[128,5760]{1,0:T(8,128)(2,1)S(1)}, bf16[2,128,432]{2,1,0:T(8,128)(2,1)S(1)}) custom-call(bf16[128,5120]{1,0:T(8,128)(2,1)S(1)} %bitcast.56, bf16[128,5120]{1,0:T(8,128)(2,1)S(1)} %bitcast.54, f32[128,128]{1,0:T(8,128)S(1)} %copy-done.18, f32[2,128,432]{2,1,0:T(8,128)S(1)} %copy-done.7, f32[1,5120]{1,0:T(1,128)S(1)} %get-tuple-element.31.gain_two, ...), custom_call_target="tpu_custom_call" | custom-call | flops 2264924160 | bytes 17694720 | tf_op jit(solution)/shard_map/pallas_call | solution.py:338
  202.3 1.1 copy-done.2
  203.4 3.6 %all-to-all-start.5 = ((bf16[8,16,5760]{2,1,0:T(8,128)(2,1)}), bf16[8,16,5760]{2,1,0:T(8,128)(2,1)S(1)}, u32[]{:S(2)}, u32[]{:S(2)}) async-start(bf16[8,16,5760]{2,1,0:T(8,128)(2,1)} %bitcast.62), calls=%async_computation.5 | async-start | bytes 2949120 | tf_op jit(solution)/shard_map/all_to_all | solution.py:251
  212.1 1.6 broadcast_in_dim_reshape.3
  213.7 15.1 %all-to-all-done.5 = bf16[8,16,5760]{2,1,0:T(8,128)(2,1)S(1)} async-done(((bf16[8,16,5760]{2,1,0:T(8,128)(2,1)}), bf16[8,16,5760]{2,1,0:T(8,128)(2,1)S(1)}, u32[]{:S(2)}, u32[]{:S(2)}) %all-to-all-start.5) | async-done | bytes 1474592 | tf_op jit(solution)/shard_map/all_to_all | solution.py:251
  228.8 1.1 shard_map.116
  232.6 1.3 copy-done.22
  233.9 1.3 copy-done.24
  235.2 11.3 %shard_map.117 = (bf16[432,5120]{1,0:T(8,128)(2,1)}, bf16[432,5120]{1,0:T(8,128)(2,1)}) custom-call(bf16[128,5120]{1,0:T(8,128)(2,1)S(1)} %copy-done.22, bf16[128,5120]{1,0:T(8,128)(2,1)} %collective-permute-done.5.refs_1_, bf16[128,5120]{1,0:T(8,128)(2,1)S(1)} %copy-done.24, bf16[128,5120]{1,0:T(8,128)(2,1)} %collective-permute-done.6.refs_3_, ...), custom_call_target="tpu_custom_call" | custom-call | flops 4529848320 | bytes 35389440 | tf_op jit(solution)/shard_map/pallas_call | solution.py:356
  (105 shorter events, 22.5 us)
Async XLA Ops:
  7.2 46.2 %copy-start = (s32[8,16]{1,0:T(8,128)S(1)}, s32[8,16]{1,0:T(8,128)}, u32[]{:S(2)}) copy-start(s32[8,16]{1,0:T(8,128)} %param.12) | copy-start | bytes 1540
  7.2 82.6 %all-gather.3.cloned.1.call-start = ((), (), s32[]{:S(2)}) async-start(), calls=%async_computation.10 | async-start | bytes 2785280 | tf_op jit(solution)/shard_map/all_gather | solution.py:282
  7.2 29.8 %collective-permute-start = (bf16[432,5120]{1,0:T(8,128)(2,1)}, bf16[432,5120]{1,0:T(8,128)(2,1)}, u32[]{:S(2)}, u32[]{:S(2)}) collective-permute-start(bf16[432,5120]{1,0:T(8,128)(2,1)} %bitcast.73), channel_id=1, source_target_pairs={{0,1},{1,0},{2,3},{3,2},{4,5},{5,4},{6,7},{7,6},{8,9},{9,8},{10,11... | collective-permute-start | bytes 13271048 | tf_op jit(solution)/shard_map/ppermute | solution.py:262
  8.0 29.1 %collective-permute-start.1 = (bf16[432,5120]{1,0:T(8,128)(2,1)}, bf16[432,5120]{1,0:T(8,128)(2,1)}, u32[]{:S(2)}, u32[]{:S(2)}) collective-permute-start(bf16[432,5120]{1,0:T(8,128)(2,1)} %bitcast.68), channel_id=1, source_target_pairs={{0,1},{1,0},{2,3},{3,2},{4,5},{5,4},{6,7},{7,6},{8,9},{9,8},{10,11... | collective-permute-start | bytes 13271048 | tf_op jit(solution)/shard_map/ppermute | solution.py:262
  9.1 27.9 %copy-start.8 = (f32[1,5120]{1,0:T(1,128)S(1)}, f32[1,5120]{1,0:T(1,128)}, u32[]{:S(2)}) copy-start(f32[1,5120]{1,0:T(1,128)} %gain.7) | copy-start | bytes 61444
  49.7 26.7 %copy-start.3 = (bf16[1,16,5120]{2,1,0:T(8,128)(2,1)S(1)}, bf16[1,16,5120]{2,1,0:T(8,128)(2,1)}, u32[]{:S(2)}) copy-start(bf16[1,16,5120]{2,1,0:T(8,128)(2,1)} %param.7) | copy-start | bytes 491524
  49.7 26.7 %all-to-all-start.1 = ((bf16[8,16,5120]{2,1,0:T(8,128)(2,1)}), bf16[8,16,5120]{2,1,0:T(8,128)(2,1)S(1)}, u32[]{:S(2)}, u32[]{:S(2)}) async-start(bf16[8,16,5120]{2,1,0:T(8,128)(2,1)} %bitcast.66), calls=%async_computation.1 | async-start | bytes 2621440 | tf_op jit(solution)/shard_map/all_to_all | solution.py:251
  76.5 6.8 %collective-permute-start.2 = (bf16[16,5120]{1,0:T(8,128)(2,1)S(1)}, bf16[16,5120]{1,0:T(8,128)(2,1)S(1)}, u32[]{:S(2)}, u32[]{:S(2)}) collective-permute-start(bf16[16,5120]{1,0:T(8,128)(2,1)S(1)} %shard_map.111), channel_id=1, source_target_pairs={{0,16},{16,32},{32,48},{48,64},{64,80},{80,96},{96,112},{1,17},{17... | collective-permute-start | bytes 491528 | tf_op jit(solution)/shard_map/ppermute | solution.py:268
  84.5 4.8 %copy-start.25 = (s32[8]{0:T(128)S(1)}, s32[8]{0:T(128)}, u32[]{:S(2)}) copy-start(s32[8]{0:T(128)} %constant.66) | copy-start | bytes 100
  84.5 24.5 %all-to-all-start.2 = ((bf16[8,16,5120]{2,1,0:T(8,128)(2,1)}), bf16[8,16,5120]{2,1,0:T(8,128)(2,1)}, u32[]{:S(2)}, u32[]{:S(2)}) async-start(bf16[8,16,5120]{2,1,0:T(8,128)(2,1)} %broadcast_in_dim.16), calls=%async_computation.2 | async-start | bytes 2621440 | tf_op jit(solution)/shard_map/all_to_all | solution.py:251
  88.9 87.5 %reduce-scatter.3.cloned.1.call-start = ((), (), s32[]{:S(2)}) async-start(), calls=%async_computation.8 | async-start | bytes 1638400 | tf_op jit(solution)/shard_map/reduce_scatter | solution.py:322
  89.8 1.7 copy-start.1
  126.4 29.8 %all-to-all-start.3 = ((bf16[8,16,5120]{2,1,0:T(8,128)(2,1)}), bf16[8,16,5120]{2,1,0:T(8,128)(2,1)S(1)}, u32[]{:S(2)}, u32[]{:S(2)}) async-start(bf16[8,16,5120]{2,1,0:T(8,128)(2,1)} %bitcast.67), calls=%async_computation.3 | async-start | bytes 2621440 | tf_op jit(solution)/shard_map/all_to_all | solution.py:251
  156.6 8.2 %collective-permute-start.3 = (bf16[16,5120]{1,0:T(8,128)(2,1)S(1)}, bf16[16,5120]{1,0:T(8,128)(2,1)S(1)}, u32[]{:S(2)}, u32[]{:S(2)}) collective-permute-start(bf16[16,5120]{1,0:T(8,128)(2,1)S(1)} %shard_map.114), channel_id=1, source_target_pairs={{16,0},{32,16},{48,32},{64,48},{80,64},{96,80},{112,96},{17,1},{33... | collective-permute-start | bytes 491528 | tf_op jit(solution)/shard_map/ppermute | solution.py:268
  165.9 26.2 %all-to-all-start.4 = ((bf16[8,16,5120]{2,1,0:T(8,128)(2,1)}), bf16[8,16,5120]{2,1,0:T(8,128)(2,1)S(1)}, u32[]{:S(2)}, u32[]{:S(2)}) async-start(bf16[8,16,5120]{2,1,0:T(8,128)(2,1)} %broadcast_in_dim.17), calls=%async_computation.4 | async-start | bytes 2621440 | tf_op jit(solution)/shard_map/all_to_all | solution.py:251
  172.1 6.1 %copy-start.10 = (bf16[2,128,432]{2,1,0:T(8,128)(2,1)S(1)}, bf16[2,128,432]{2,1,0:T(8,128)(2,1)}, u32[]{:S(2)}) copy-start(bf16[2,128,432]{2,1,0:T(8,128)(2,1)} %copy-done.9) | copy-start | bytes 663556
  172.1 34.9 %reduce-scatter.5.cloned.1.call-start = ((), (), s32[]{:S(2)}) async-start(), calls=%async_computation.9 | async-start | bytes 491520 | tf_op jit(solution)/shard_map/reduce_scatter | solution.py:323
  172.1 38.6 %collective-permute-start.5 = (bf16[128,5120]{1,0:T(8,128)(2,1)}, bf16[128,5120]{1,0:T(8,128)(2,1)}, u32[]{:S(2)}, u32[]{:S(2)}) collective-permute-start(bf16[128,5120]{1,0:T(8,128)(2,1)} %copy-done.21), channel_id=1, source_target_pairs={{0,1},{1,0},{2,3},{3,2},{4,5},{5,4},{6,7},{7,6},{8,9},{9,8},{10,11... | collective-permute-start | bytes 3932168 | tf_op jit(solution)/shard_map/ppermute | solution.py:262
  175.9 16.3 %copy-start.18 = (f32[128,128]{1,0:T(8,128)S(1)}, f32[128,128]{1,0:T(8,128)}, u32[]{:S(2)}) copy-start(f32[128,128]{1,0:T(8,128)} %copy-done.17) | copy-start | bytes 196612
  175.9 34.5 %collective-permute-start.11 = (bf16[128,432]{1,0:T(8,128)(2,1)}, bf16[128,432]{1,0:T(8,128)(2,1)}, u32[]{:S(2)}, u32[]{:S(2)}) collective-permute-start(bf16[128,432]{1,0:T(8,128)(2,1)} %get-tuple-element.47), channel_id=1, source_target_pairs={{0,1},{1,0},{2,3},{3,2},{4,5},{5,4},{6,7},{7,6},{8,9},{9,8},{10,11... | collective-permute-start | bytes 331784 | tf_op jit(solution)/shard_map/ppermute | solution.py:262
  175.9 35.1 %collective-permute-start.8 = (bf16[128,5120]{1,0:T(8,128)(2,1)}, bf16[128,5120]{1,0:T(8,128)(2,1)}, u32[]{:S(2)}, u32[]{:S(2)}) collective-permute-start(bf16[128,5120]{1,0:T(8,128)(2,1)} %copy-done.19), channel_id=1, source_target_pairs={{0,1},{1,0},{2,3},{3,2},{4,5},{5,4},{6,7},{7,6},{8,9},{9,8},{10,11... | collective-permute-start | bytes 3932168 | tf_op jit(solution)/shard_map/ppermute | solution.py:262
  176.4 54.3 %collective-permute-start.6 = (bf16[128,5120]{1,0:T(8,128)(2,1)}, bf16[128,5120]{1,0:T(8,128)(2,1)}, u32[]{:S(2)}, u32[]{:S(2)}) collective-permute-start(bf16[128,5120]{1,0:T(8,128)(2,1)} %copy-done.23), channel_id=1, source_target_pairs={{0,1},{1,0},{2,3},{3,2},{4,5},{5,4},{6,7},{7,6},{8,9},{9,8},{10,11... | collective-permute-start | bytes 3932168 | tf_op jit(solution)/shard_map/ppermute | solution.py:262
  203.4 25.4 %all-to-all-start.5 = ((bf16[8,16,5760]{2,1,0:T(8,128)(2,1)}), bf16[8,16,5760]{2,1,0:T(8,128)(2,1)S(1)}, u32[]{:S(2)}, u32[]{:S(2)}) async-start(bf16[8,16,5760]{2,1,0:T(8,128)(2,1)} %bitcast.62), calls=%async_computation.5 | async-start | bytes 2949120 | tf_op jit(solution)/shard_map/all_to_all | solution.py:251
  208.1 2.0 collective-permute-start.4
  210.1 20.7 %collective-permute-start.7 = (bf16[128,5120]{1,0:T(8,128)(2,1)S(1)}, bf16[128,5120]{1,0:T(8,128)(2,1)}, u32[]{:S(2)}, u32[]{:S(2)}) collective-permute-start(bf16[128,5120]{1,0:T(8,128)(2,1)S(1)} %bitcast.57), channel_id=1, source_target_pairs={{0,1},{1,0},{2,3},{3,2},{4,5},{5,4},{6,7},{7,6},{8,9},{9,8},{10,11... | collective-permute-start | bytes 3932168 | tf_op jit(solution)/shard_map/ppermute | solution.py:262
  210.4 19.4 %collective-permute-start.10 = (bf16[128,432]{1,0:T(8,128)(2,1)}, bf16[128,432]{1,0:T(8,128)(2,1)}, u32[]{:S(2)}, u32[]{:S(2)}) collective-permute-start(bf16[128,432]{1,0:T(8,128)(2,1)} %get-tuple-element.49), channel_id=1, source_target_pairs={{0,1},{1,0},{2,3},{3,2},{4,5},{5,4},{6,7},{7,6},{8,9},{9,8},{10,11... | collective-permute-start | bytes 331784 | tf_op jit(solution)/shard_map/ppermute | solution.py:262
  210.7 20.0 %collective-permute-start.12 = (bf16[128,432]{1,0:T(8,128)(2,1)}, bf16[128,432]{1,0:T(8,128)(2,1)}, u32[]{:S(2)}, u32[]{:S(2)}) collective-permute-start(bf16[128,432]{1,0:T(8,128)(2,1)} %get-tuple-element.45), channel_id=1, source_target_pairs={{0,1},{1,0},{2,3},{3,2},{4,5},{5,4},{6,7},{7,6},{8,9},{9,8},{10,11... | collective-permute-start | bytes 331784 | tf_op jit(solution)/shard_map/ppermute | solution.py:262
  211.0 19.7 %collective-permute-start.9 = (bf16[128,432]{1,0:T(8,128)(2,1)}, bf16[128,432]{1,0:T(8,128)(2,1)}, u32[]{:S(2)}, u32[]{:S(2)}) collective-permute-start(bf16[128,432]{1,0:T(8,128)(2,1)} %get-tuple-element.51), channel_id=1, source_target_pairs={{0,1},{1,0},{2,3},{3,2},{4,5},{5,4},{6,7},{7,6},{8,9},{9,8},{10,11... | collective-permute-start | bytes 331784 | tf_op jit(solution)/shard_map/ppermute | solution.py:262
  211.2 19.5 %copy-start.13 = (bf16[128,432]{1,0:T(8,128)(2,1)S(1)}, bf16[128,432]{1,0:T(8,128)(2,1)}, u32[]{:S(2)}) copy-start(bf16[128,432]{1,0:T(8,128)(2,1)} %get-tuple-element.48.refs_12_) | copy-start | bytes 331780
  211.2 19.5 %copy-start.14 = (bf16[128,432]{1,0:T(8,128)(2,1)S(1)}, bf16[128,432]{1,0:T(8,128)(2,1)}, u32[]{:S(2)}) copy-start(bf16[128,432]{1,0:T(8,128)(2,1)} %get-tuple-element.50.refs_10_) | copy-start | bytes 331780
  228.8 2.0 copy-start.20
  229.9 16.7 %collective-permute-start.13 = (f32[8,640]{1,0:T(8,128)S(1)}, f32[8,640]{1,0:T(8,128)S(1)}, u32[]{:S(2)}, u32[]{:S(2)}) collective-permute-start(f32[8,640]{1,0:T(8,128)S(1)} %get-tuple-element.44), channel_id=1, source_target_pairs={{0,1},{1,0},{2,3},{3,2},{4,5},{5,4},{6,7},{7,6},{8,9},{9,8},{10,11... | collective-permute-start | bytes 61448 | tf_op jit(solution)/shard_map/ppermute | solution.py:262
  (16 other events, 15.5 us)
Sparse Core Ops, SparseCore 0:
  10.4 69.0 all-gather.2
  126.5 33.0 reduce-scatter.2
  176.6 20.3 reduce-scatter.4

commit v2 on v1

v2 whole, which is shorter than its diff:
```python
import jax
import jax.numpy as jnp
from jax import lax
from jax.experimental import pallas as pl
from jax.experimental.pallas import tpu as pltpu
from jax.sharding import PartitionSpec as P

BF = jnp.bfloat16
F32 = jnp.float32
ROWS = 16
CHIPS = 8
TALL = CHIPS * ROWS
CHUNK = 1024
VMEM_MB = 1024 * 1024

SAME_CORE = [[2 * chip + core for chip in range(CHIPS)] for core in range(2)]
SIBLING = [(peer, peer ^ 1) for peer in range(16)]
ACROSS_Z = [(peer, peer ^ 8) for peer in range(16)]
ALONG_Y = [[(peer, peer // 8 * 8 + (peer + 2 * apart) % 8) for peer in range(16)] for apart in range(4)]

VM = pl.BlockSpec(memory_space=pltpu.VMEM)
HBM = pl.BlockSpec(memory_space=pltpu.HBM)


def dot_nt(left, right):
    return lax.dot_general(left, right, (((1,), (1,)), ((), ())), preferred_element_type=F32)


def dot_nn(left, right):
    return jnp.dot(left, right, preferred_element_type=F32)


def chunks(width):
    return [slice(at, at + CHUNK) for at in range(0, width, CHUNK)]


def row_scale(x_ref):
    rows, width = x_ref.shape
    total = jnp.zeros((rows, 128), F32)
    for at in range(0, width, 128):
        piece = x_ref[:, at : at + 128].astype(F32)
        total = total + piece * piece
    mean = jnp.sum(total, axis=-1, keepdims=True) * (1.0 / width)
    return lax.rsqrt(mean + 1e-05)


def silu_parts(act):
    sigma = jax.nn.sigmoid(act)
    return act * sigma, sigma * (1.0 + act * (1.0 - sigma))


def one_hot(index, width):
    lanes = lax.broadcasted_iota(jnp.int32, (index.shape[0], width), 1)
    return jnp.where(lanes == index, 1.0, 0.0).astype(BF)


class Weights:
    def __init__(self, sources, buffer, sems):
        self.copies = []
        for at, cols in enumerate(chunks(sources[0].shape[1])):
            self.copies.append(
                [
                    pltpu.make_async_copy(source.at[:, cols], buffer.at[which, :, cols], sems.at[at, which])
                    for which, source in enumerate(sources)
                ]
            )

    def start(self, at):
        for copy in self.copies[at]:
            copy.start()

    def start_all(self):
        for at in range(len(self.copies)):
            self.start(at)

    def wait(self, at):
        for copy in self.copies[at]:
            copy.wait()


class Stores:
    def __init__(self, sems):
        self.sems = sems
        self.copies = []

    def add(self, source, target):
        copy = pltpu.make_async_copy(source, target, self.sems.at[len(self.copies)])
        copy.start()
        self.copies.append(copy)

    def finish(self):
        for copy in self.copies:
            copy.wait()


def normed_times_up(x, scale, gain, normed, normed_out, stores, ups, wu, following=None):
    total = [None, None]
    for at, cols in enumerate(chunks(x.shape[1])):
        piece = (x[:, cols].astype(F32) * scale * gain[:, cols]).astype(BF)
        normed[:, cols] = piece
        stores.add(normed.at[:, cols], normed_out.at[:, cols])
        ups.wait(at)
        if following is not None:
            following.start(at)
        for half in range(2):
            term = dot_nt(piece, wu[half, :, cols])
            total[half] = term if at == 0 else total[half] + term
    return total


def forward_kernel(
    x, gain, up_a, up_b, down_a, down_b,
    proj, normed_out, slope_out, hidden_a_out, hidden_b_out,
    wu, wd, su, sd, normed, slope, hidden, so,
):
    ups = Weights((up_a, up_b), wu, su)
    downs = Weights((down_a, down_b), wd, sd)
    ups.start_all()
    stores = Stores(so)
    scale = row_scale(x)
    total = normed_times_up(x, scale, gain, normed, normed_out, stores, ups, wu, downs)
    for half in range(2):
        value, slant = silu_parts(total[half])
        slope[half] = slant
        hidden[half] = value.astype(BF)
    stores.add(slope, slope_out)
    stores.add(hidden.at[0], hidden_a_out)
    stores.add(hidden.at[1], hidden_b_out)
    for at, cols in enumerate(chunks(x.shape[1])):
        downs.wait(at)
        proj[:, cols] = (dot_nn(hidden[0], wd[0, :, cols]) + dot_nn(hidden[1], wd[1, :, cols])).astype(BF)
    stores.finish()


def pick_kernel(*refs):
    sources, index, out = refs[:-2], refs[-2], refs[-1]
    choose = one_hot(index[...], len(sources) * ROWS)
    for cols in chunks(out.shape[1]):
        rows = jnp.concatenate([source[:, cols] for source in sources], axis=0)
        out[:, cols] = dot_nn(choose, rows).astype(BF)


def join_kernel(own, even, odd, third, fourth, first_pair, second_pair):
    first_pair[:ROWS, :] = own[...]
    first_pair[ROWS:, :] = even[...] + odd[...]
    second_pair[:ROWS, :] = third[...]
    second_pair[ROWS:, :] = fourth[...]


def spread_kernel(rows, out):
    for at in range(0, out.shape[0], ROWS):
        out[at : at + ROWS, :] = rows[...]


def cot_kernel(*refs):
    sources, (pick, own_pick, down_a, down_b) = refs[:4], refs[4:8]
    cot_own, cot_out, d_hidden_out, wd, sd, cot, d_hidden, so = refs[8:]
    downs = Weights((down_a, down_b), wd, sd)
    downs.start_all()
    stores = Stores(so)
    choose = one_hot(pick[...], TALL)
    own = one_hot(own_pick[...], TALL)
    total = [None, None]
    for at, cols in enumerate(chunks(cot.shape[1])):
        rows = jnp.concatenate([source[:, cols] for source in sources], axis=0)
        piece = dot_nn(choose, rows).astype(BF)
        cot[:, cols] = piece
        stores.add(cot.at[:, cols], cot_out.at[:, cols])
        cot_own[:, cols] = dot_nn(own, piece).astype(BF)
        downs.wait(at)
        for half in range(2):
            term = dot_nt(piece, wd[half, :, cols])
            total[half] = term if at == 0 else total[half] + term
    for half in range(2):
        d_hidden[half] = total[half]
    stores.add(d_hidden, d_hidden_out)
    stores.finish()


def second_kernel(
    x, gain, own_target, d_hidden_in, up_a, up_b,
    gain_term, own_rows, dn, normed_out, d_act_a_out, d_act_b_out, hidden_a_out, hidden_b_out,
    wu, su, normed, d_act, hidden, d_hidden, sh, so,
):
    ups = Weights((up_a, up_b), wu, su)
    ups.start_all()
    fetch = pltpu.make_async_copy(d_hidden_in, d_hidden, sh)
    fetch.start()
    stores = Stores(so)
    scale = row_scale(x)
    total = normed_times_up(x, scale, gain, normed, normed_out, stores, ups, wu)
    fetch.wait()
    for half in range(2):
        value, slope = silu_parts(total[half])
        hidden[half] = value.astype(BF)
        d_act[half] = (d_hidden[half] * slope).astype(BF)
    stores.add(d_act.at[0], d_act_a_out)
    stores.add(d_act.at[1], d_act_b_out)
    stores.add(hidden.at[0], hidden_a_out)
    stores.add(hidden.at[1], hidden_b_out)
    own = one_hot(own_target[...], TALL)
    for cols in chunks(x.shape[1]):
        term = dot_nn(d_act[0], wu[0, :, cols]) + dot_nn(d_act[1], wu[1, :, cols])
        dn[:, cols] = term.astype(BF)
        gain_term[:, cols] = jnp.sum(term * normed[:, cols].astype(F32), axis=0, keepdims=True) / gain[:, cols]
        own_rows[:, cols] = dot_nn(own, x[:, cols]).astype(BF)
    stores.finish()


def target_kernel(to_target, hidden_a, hidden_b, down_a, down_b, near, second, third, fourth, wd, sd, hidden, sh):
    fetches = [pltpu.make_async_copy(ref, hidden.at[at], sh.at[at]) for at, ref in enumerate((hidden_a, hidden_b))]
    for fetch in fetches:
        fetch.start()
    downs = Weights((down_a, down_b), wd, sd)
    downs.start_all()
    sort = one_hot(to_target[...], TALL)
    left = []
    for half, fetch in enumerate(fetches):
        fetch.wait()
        left.append(dot_nn(sort, hidden[half]).astype(BF))
    for at, cols in enumerate(chunks(near.shape[1])):
        downs.wait(at)
        term = (dot_nn(left[0], wd[0, :, cols]) + dot_nn(left[1], wd[1, :, cols])).astype(BF)
        for part, out in enumerate((near, second, third, fourth)):
            out[:, cols] = term[2 * ROWS * part : 2 * ROWS * (part + 1)]


def sum_kernel(near, second, third, fourth, mine, other):
    for cols in chunks(near.shape[1]):
        total = near[:, cols].astype(F32) + second[:, cols].astype(F32)
        total = total + (third[:, cols].astype(F32) + fourth[:, cols].astype(F32))
        mine[:, cols] = total[:ROWS]
        other[:, cols] = total[ROWS:].astype(BF)


def second_out_kernel(own_rows, mine, given, out):
    for cols in chunks(out.shape[1]):
        out[:, cols] = (own_rows[:, cols].astype(F32) + (mine[:, cols] + given[:, cols].astype(F32))).astype(BF)


def first_back_kernel(
    c, gain, gain_two, slope_in, normed_in, up_a, up_b, down_a, down_b,
    dn, c_out, d_act_a_out, d_act_b_out,
    wu, wd, su, sd, d_act, slope, normed, sh, so,
):
    width = c.shape[1]
    downs = Weights((down_a, down_b), wd, sd)
    ups = Weights((up_a, up_b), wu, su)
    downs.start_all()
    fetches = [pltpu.make_async_copy(slope_in, slope, sh.at[0]), pltpu.make_async_copy(normed_in, normed, sh.at[1])]
    stores = Stores(so)
    stores.add(c, c_out)
    total = [None, None]
    for at, cols in enumerate(chunks(width)):
        downs.wait(at)
        if at == 0:
            for fetch in fetches:
                fetch.start()
        ups.start(at)
        for half in range(2):
            term = dot_nt(c[:, cols], wd[half, :, cols])
            total[half] = term if at == 0 else total[half] + term
    for fetch in fetches:
        fetch.wait()
    for half in range(2):
        d_act[half] = (total[half] * slope[half]).astype(BF)
    stores.add(d_act.at[0], d_act_a_out)
    stores.add(d_act.at[1], d_act_b_out)
    gain_pieces = []
    for at, cols in enumerate(chunks(width)):
        ups.wait(at)
        term = dot_nn(d_act[0], wu[0, :, cols]) + dot_nn(d_act[1], wu[1, :, cols])
        dn[:, cols] = term.astype(BF)
        product = jnp.sum(term * normed[:, cols].astype(F32), axis=0, keepdims=True)
        gain_pieces.append(product / gain[:, cols] + gain_two[:, cols])
    line = jnp.concatenate(gain_pieces, axis=1)
    lanes = width // 8
    grid = jnp.concatenate([line[:, lanes * at : lanes * (at + 1)] for at in range(8)], axis=0)
    high = grid.astype(BF).astype(F32)
    both = jnp.concatenate([high, grid - high], axis=0).astype(BF)
    for block in range(CHIPS):
        dn[block * ROWS : (block + 1) * ROWS, width:] = both
    stores.finish()


def add_blocks(blocks, cols):
    total = blocks[0:ROWS, cols].astype(F32)
    for at in range(ROWS, blocks.shape[0], ROWS):
        total = total + blocks[at : at + ROWS, cols].astype(F32)
    return total


def add_kernel(blocks, x, out):
    for cols in chunks(x.shape[1]):
        out[:, cols] = (x[:, cols].astype(F32) + add_blocks(blocks, cols)).astype(BF)


def rows_back_kernel(blocks, x, c, gain, *rest):
    out, spread = rest[0], rest[-1]
    width = x.shape[1]
    scale = row_scale(x)
    along = jnp.zeros((ROWS, 128), F32)
    for cols in chunks(width):
        piece = add_blocks(blocks, cols) * gain[:, cols]
        spread[:, cols] = piece
        product = piece * (x[:, cols].astype(F32) * scale)
        for at in range(0, CHUNK, 128):
            along = along + product[:, at : at + 128]
    mean = jnp.sum(along, axis=-1, keepdims=True) * (1.0 / width)
    for cols in chunks(width):
        vhat = x[:, cols].astype(F32) * scale
        out[:, cols] = (c[:, cols].astype(F32) + scale * (spread[:, cols] - vhat * mean)).astype(BF)
    if len(rest) == 3:
        extra = add_blocks(blocks, slice(width, blocks.shape[1]))
        line = extra[:8] + extra[8:]
        rest[1][...] = jnp.concatenate([line[at : at + 1] for at in range(8)], axis=1)


def grads_kernel(*refs):
    normed, c, slim = refs[0:4], refs[4:8], refs[8:16]
    out_up, out_down, left_up, left_down, held, sems = refs[16:22]

    @pl.when(pl.program_id(0) == 0)
    def _():
        copies = [pltpu.make_async_copy(ref, held.at[at], sems.at[at]) for at, ref in enumerate(slim)]
        for copy in copies:
            copy.start()
        for at in range(4):
            rows = slice(at * TALL, (at + 1) * TALL)
            copies[at].wait()
            left_up[:, rows] = held[at].T
            copies[4 + at].wait()
            left_down[:, rows] = held[4 + at].T

    right = jnp.concatenate([ref[...] for ref in normed], axis=0)
    out_up[...] = dot_nn(left_up[...], right).astype(BF)
    right = jnp.concatenate([ref[...] for ref in c], axis=0)
    out_down[...] = dot_nn(left_down[...], right).astype(BF)


def in_vmem(*dims, dtype=BF):
    return pltpu.VMEM(dims, dtype)


def shape(*dims, dtype=BF):
    return jax.ShapeDtypeStruct(dims, dtype)


def in_hbm(value):
    return pltpu.with_memory_space_constraint(value, pltpu.HBM)


def call(kernel, outs, args, from_hbm=(), hbm_outs=(), scratch=(), limit=16, flops=0, moved=0):
    return pl.pallas_call(
        kernel,
        out_shape=list(outs) + [pltpu.HBM(out.shape, out.dtype) for out in hbm_outs],
        in_specs=[VM] * len(args) + [HBM] * len(from_hbm),
        out_specs=[VM] * len(outs) + [HBM] * len(hbm_outs),
        scratch_shapes=scratch,
        compiler_params=pltpu.CompilerParams(vmem_limit_bytes=limit * VMEM_MB),
        cost_estimate=pl.CostEstimate(flops=flops, bytes_accessed=moved, transcendentals=0),
    )(*args, *[in_hbm(value) for value in from_hbm])


def kept(*dims, dtype=BF):
    return pltpu.VMEM(dims, dtype)


def dma(*dims):
    return pltpu.SemaphoreType.DMA(dims)


def weight_scratch(units, width, count):
    return [kept(2, units, width)] * count + [dma(width // CHUNK, 2)] * count


def to_chips(blocks):
    return lax.all_to_all(
        blocks, "peer", split_axis=0, concat_axis=0, tiled=True, axis_index_groups=SAME_CORE
    )


def from_chips(rows):
    width = rows.shape[1]
    return to_chips(call(spread_kernel, [in_vmem(TALL, width)], [rows], limit=4, moved=TALL * width * 4)[0])


def swap(value):
    return lax.ppermute(value, "peer", SIBLING)


def after(value, *earlier):
    return lax.optimization_barrier((value,) + earlier)[0]


def together(*values):
    return lax.optimization_barrier(values)


def passed_along(value, steps):
    count = lax.axis_size("section")
    leading, last = (max(0, -steps), min(count, count - steps))
    return lax.ppermute(value, "section", [(source, source + steps) for source in range(leading, last)])


def local(acts, cotangent, gain, w_up, w_down, matching):
    section = lax.axis_index("section")
    peer = lax.axis_index("peer")
    core = peer % 2
    chip = peer // 2
    rows_in, cot_in, up, down = acts[0], cotangent[0], w_up[0], w_down[0]
    units, width = up.shape
    flops = 4 * TALL * units * width
    moved = 2 * TALL * width * 2
    steps = width // CHUNK
    tall, block, slim = shape(TALL, width), shape(ROWS, width), shape(TALL, units)
    pair_f32 = shape(2, TALL, units, dtype=F32)

    cot_b = swap(cot_in)
    up_b, down_b = swap(after(up, cot_b)), swap(after(down, cot_b))

    before = lax.dynamic_index_in_dim(matching, jnp.maximum(section - 1, 0), 0, keepdims=False)
    mine = jnp.where(core == 0, before[0::2], before[1::2])
    chips = jnp.arange(CHIPS, dtype=jnp.int32)
    slots = jnp.arange(ROWS, dtype=jnp.int32)
    pair = jnp.arange(2, dtype=jnp.int32)
    wanted = slots[None, :] ^ mine[:, None]
    apart_y, apart_z = (wanted // 2 - chip) % 4, (wanted // 8) ^ (chip // 4)
    pick = ((apart_z * 4 + apart_y) * ROWS + (wanted % 2) * CHIPS + chips[:, None]).reshape(TALL, 1)
    cot_index = (jnp.where(pair == core, 0, ROWS)[:, None] + 2 * chips[None, :] + core).reshape(ROWS, 1)
    owner = (((chip // 4) ^ pair) * 4)[None, :] + ((chip + jnp.arange(4, dtype=jnp.int32)) % 4)[:, None]
    to_target = (owner.reshape(CHIPS, 1, 1) * 2 + pair[None, :, None]) ^ mine[None, None, :]
    to_target = (to_target + chips[None, None, :] * ROWS).reshape(TALL, 1)
    own_target = to_target[:ROWS]
    own_pick = (chip * ROWS + slots).reshape(ROWS, 1)
    out_index = (jnp.where(slots % 2 == core, 0, ROWS) + core * CHIPS + slots // 2).reshape(ROWS, 1)

    cot_half = call(pick_kernel, [block], [cot_in, cot_b, cot_index], moved=moved // 4)[0]
    even = lax.ppermute(cot_half, "peer", ALONG_Y[3][0::2])
    x_one = from_chips(after(rows_in, even))
    rest = after(cot_half, even)
    cot_y = [lax.ppermute(rest, "peer", pairs) for pairs in (ALONG_Y[3][1::2], ALONG_Y[2], ALONG_Y[1])]
    cot_a, cot_b = call(join_kernel, [shape(2 * ROWS, width)] * 2, [cot_half, even] + cot_y, moved=moved)
    x_one, cot_a, cot_b = together(x_one, cot_a, cot_b)
    cot_za = lax.ppermute(cot_a, "peer", ACROSS_Z)
    proj, normed_one, slope_one, hidden_one, hidden_one_b = call(
        forward_kernel, [in_vmem(TALL, width)], [x_one, gain], [up, up_b, down, down_b], [tall, pair_f32, slim, slim],
        weight_scratch(units, width, 2)
        + [kept(TALL, width), kept(2, TALL, units, dtype=F32), kept(2, TALL, units), dma(steps + 3)],
        limit=36, flops=3 * flops, moved=6 * moved,
    )
    proj, cot_za = together(proj, cot_za)
    blocks = to_chips(proj)
    first = call(add_kernel, [block], [blocks, rows_in], moved=moved)[0]
    arrived = passed_along(first, 1)
    cot_zb = lax.ppermute(after(cot_b, first), "peer", ACROSS_Z)
    arrived, cot_zb = together(arrived, cot_zb)
    cot_all = [cot_a, cot_b, cot_za, cot_zb]
    x_two = from_chips(arrived)
    cot_own, cot, d_hidden = call(
        cot_kernel, [block], cot_all + [pick, own_pick], [down, down_b], [tall, pair_f32],
        weight_scratch(units, width, 1) + [kept(TALL, width), kept(2, TALL, units, dtype=F32), dma(steps + 1)],
        limit=20, flops=3 * flops, moved=3 * moved,
    )
    gain_two, own_rows, d_normed, normed_two, d_act_two, d_act_two_b, hidden_two, hidden_two_b = call(
        second_kernel, [shape(1, width, dtype=F32), block, in_vmem(TALL, width)],
        [x_two, gain, own_target], [d_hidden, up, up_b], [tall, slim, slim, slim, slim],
        weight_scratch(units, width, 1)
        + [kept(TALL, width), kept(2, TALL, units), kept(2, TALL, units), kept(2, TALL, units, dtype=F32),
           pltpu.SemaphoreType.DMA, dma(steps + 4)],
        limit=28, flops=3 * flops, moved=4 * moved,
    )
    blocks = to_chips(d_normed)
    parts = call(
        target_kernel, [shape(2 * ROWS, width)] * 4, [to_target], [hidden_two, hidden_two_b, down, down_b], [],
        weight_scratch(units, width, 1) + [kept(2, TALL, units), dma(2)],
        limit=20, flops=2 * flops, moved=3 * moved,
    )
    d_two = call(
        rows_back_kernel, [block], [blocks, arrived, cot_own, gain], scratch=[kept(ROWS, width, dtype=F32)], moved=moved
    )[0]
    landed = passed_along(d_two, -1)
    near = together(*parts, d_two)
    part_up, part_down = lax.ppermute(near[1], "peer", ALONG_Y[1]), lax.ppermute(near[3], "peer", ALONG_Y[3])
    landed, part_up, part_down = together(landed, part_up, part_down)
    c_all = from_chips(landed)
    c_all, far = together(c_all, parts[2])
    part_far = lax.ppermute(far, "peer", ALONG_Y[2])
    d_normed, c_one, d_act_one, d_act_one_b = call(
        first_back_kernel, [in_vmem(TALL, width + width // 8)], [c_all, gain, gain_two],
        [slope_one, normed_one, up, up_b, down, down_b], [tall, slim, slim],
        weight_scratch(units, width, 2)
        + [kept(2, TALL, units), kept(2, TALL, units, dtype=F32), kept(TALL, width), dma(2), dma(3)],
        limit=36, flops=3 * flops, moved=6 * moved,
    )
    d_normed, part_far = together(d_normed, part_far)
    blocks = to_chips(d_normed)
    own_part, other_part = call(
        sum_kernel, [shape(ROWS, width, dtype=F32), block], [parts[0], part_up, part_far, part_down], moved=moved
    )
    given = lax.ppermute(after(other_part, d_normed), "peer", ACROSS_Z)
    wide, thin = [], []
    for value in (normed_one, normed_two, c_one, cot):
        wide += [value, swap(after(value, d_normed))]
    for own, other in ((d_act_one, d_act_one_b), (d_act_two, d_act_two_b), (hidden_one, hidden_one_b), (hidden_two, hidden_two_b)):
        thin += [own, swap(after(other, d_normed))]
    step = 1024
    grad_up, grad_down = pl.pallas_call(
        grads_kernel,
        grid=(width // step,),
        out_shape=[shape(units, width)] * 2,
        in_specs=[pl.BlockSpec((TALL, step), lambda i: (0, i))] * 8 + [HBM] * 8,
        out_specs=[pl.BlockSpec((units, step), lambda i: (0, i))] * 2,
        scratch_shapes=[kept(units, 4 * TALL)] * 2 + [kept(8, TALL, units), dma(8)],
        compiler_params=pltpu.CompilerParams(vmem_limit_bytes=24 * VMEM_MB),
        cost_estimate=pl.CostEstimate(flops=4 * flops, bytes_accessed=8 * moved, transcendentals=0),
    )(*[in_hbm(value) for value in wide], *[in_hbm(value) for value in thin])

    d_one, gain_sum = call(
        rows_back_kernel, [block, shape(1, width, dtype=F32)], [after(blocks, grad_up), rows_in, landed, gain],
        scratch=[kept(ROWS, width, dtype=F32)], moved=moved,
    )
    second = call(second_out_kernel, [block], [after(own_rows, grad_up), own_part, given], moved=moved // 4)[0]
    second = call(pick_kernel, [block], [second, swap(second), out_index])[0]
    grad_gain = gain_sum + swap(gain_sum)
    return (d_one[None], second[None], grad_up[None], grad_down[None], grad_gain)


def solution(mesh):
    wide = P("section", "peer", None)
    in_specs = (wide, wide, P("section", None), wide, wide, P())
    out_specs = (wide, wide, wide, wide, P("section", None))
    return jax.shard_map(local, mesh=mesh, in_specs=in_specs, out_specs=out_specs, check_vma=False)
```

time: 255 us -> 211 us (0.83)
  waiting for transfers between devices: 98.3 us -> 60 us
  starting transfers between devices: 33.6 us -> 67.3 us
  local copies, waits for them, and re-layouts: 29 us -> 3.3 us
  between operations: 14.2 us -> 0.97 us
  blocking collectives: 27.9 us -> 17.6 us
  Pallas kernels: 49.5 us -> 57 us
    all_to_all x5, waiting for transfers between devices: 87.4 us -> 24.5 us  [to_chips(): lax.all_to_all(blocks, 'peer', split_axis=0, concat_axis=0, tiled=True, a...]
    ppermute x0 -> x10, waiting for transfers between devices: none -> 18 us  [the longest x3 10.1 us: local(): lax.ppermute(rest, 'peer', pairs)]
    ppermute x0 -> x10, starting transfers between devices: none -> 17.3 us  [the longest x3 6.93 us: local(): lax.ppermute(rest, 'peer', pairs)]
    unnamed x53 -> x24, local copies, waits for them, and re-layouts: 17.9 us -> 2.59 us
    ppermute x12 -> x13, starting transfers between devices: 7.47 us -> 21.9 us  [swap(): return lax.ppermute(value, 'peer', SIBLING)]
    all_to_all x1, blocking collectives: 27.9 us -> 17.6 us  [to_chips(): lax.all_to_all(blocks, 'peer', split_axis=0, concat_axis=0, tiled=True, a...]
    ppermute x12 -> x13, waiting for transfers between devices: 0.24 us -> 7.41 us  [swap(): return lax.ppermute(value, 'peer', SIBLING)]
    pallas_call x7 -> x16, Pallas kernels: 38.1 us -> 45.1 us  [call(): pl.pallas_call(kernel, out_shape=list(outs) + [pltpu.HBM(out.shape, out.d...]
  transfers between devices with their start and end apart: 22 -> 30, of which waited for: 8 -> 16; matrix products, arithmetic and copies ran while one was open for 5% -> 1% of each run, Pallas kernels for 14% -> 22%
where the time goes in v2:
time: 211 us; the launch traced here: 207 us
  starting transfers between devices  67.3 us (32%)
  waiting for transfers between devices  60 us (28%)
  Pallas kernels  57 us (27%)
  blocking collectives  17.6 us (8%)
  local copies, waits for them, and re-layouts  3.3 us (2%)
    pallas_call x16, Pallas kernels, call(): pl.pallas_call(kernel, out_shape=list(outs) + [pltpu.HBM(out.shape, out.d...  45.1 us
    all_to_all x5, waiting for transfers between devices, to_chips(): lax.all_to_all(blocks, 'peer', split_axis=0, concat_axis=0, tiled=True, a...  24.5 us
    all_to_all x5, starting transfers between devices, to_chips(): lax.all_to_all(blocks, 'peer', split_axis=0, concat_axis=0, tiled=True, a...  23.2 us
    ppermute x13, starting transfers between devices, swap(): return lax.ppermute(value, 'peer', SIBLING)  21.9 us
    all_to_all x1, blocking collectives, to_chips(): lax.all_to_all(blocks, 'peer', split_axis=0, concat_axis=0, tiled=True, a...  17.6 us
    pallas_call x1, Pallas kernels, local(): pl.pallas_call(grads_kernel, grid=(width // step,), out_shape=[shape(unit...  11.9 us
    ppermute x3, waiting for transfers between devices, local(): lax.ppermute(rest, 'peer', pairs)  10.1 us
    ppermute x2, waiting for transfers between devices, passed_along(): lax.ppermute(value, 'section', [(source, source + steps) for source in ra...  10.1 us
  transfers between devices with their start and end apart: 30, of which 16 were waited for; matrix products, arithmetic and copies ran while one was open for 1% of the time, Pallas kernels for 22%

profile of v2, /device:TPU:7, one launch (start us, length us, event | category | flops | bytes accessed | tf_op | source)
XLA Modules:
  0.0 207.3 jit_solution(14124866046699090141)
XLA Ops:
  7.2 7.6 %all-to-all-start = ((bf16[8,16,5120]{2,1,0:T(8,128)(2,1)}), bf16[8,16,5120]{2,1,0:T(8,128)(2,1)S(1)}, u32[]{:S(2)}, u32[]{:S(2)}) async-start(bf16[8,16,5120]{2,1,0:T(8,128)(2,1)} %bitcast.2), calls=%async_computation | async-start | bytes 2621440 | tf_op jit(solution)/shard_map/all_to_all | solution.py:378
  14.9 1.5 collective-permute-start.4
  16.3 2.4 %collective-permute-start.3 = (bf16[16,5120]{1,0:T(8,128)(2,1)S(1)}, bf16[16,5120]{1,0:T(8,128)(2,1)S(1)}, u32[]{:S(2)}, u32[]{:S(2)}) collective-permute-start(bf16[16,5120]{1,0:T(8,128)(2,1)S(1)} %shard_map.101.own), channel_id=1, source_target_pairs={{0,4},{1,5},{2,6},{3,7},{4,0},{5,1},{6,2},{7,3},{8,12},{9,13},{10,... | collective-permute-start | bytes 491528 | tf_op jit(solution)/shard_map/ppermute | solution.py:442
  18.7 3.1 %collective-permute-start.2 = (bf16[16,5120]{1,0:T(8,128)(2,1)S(1)}, bf16[16,5120]{1,0:T(8,128)(2,1)S(1)}, u32[]{:S(2)}, u32[]{:S(2)}) collective-permute-start(bf16[16,5120]{1,0:T(8,128)(2,1)S(1)} %shard_map.101.own), channel_id=1, source_target_pairs={{1,7},{3,1},{5,3},{7,5},{9,15},{11,9},{13,11},{15,13},{17,23},{19,... | collective-permute-start | bytes 491528 | tf_op jit(solution)/shard_map/ppermute | solution.py:442
  21.8 6.0 %collective-permute-done.4.fourth = bf16[16,5120]{1,0:T(8,128)(2,1)S(1)} collective-permute-done((bf16[16,5120]{1,0:T(8,128)(2,1)S(1)}, bf16[16,5120]{1,0:T(8,128)(2,1)S(1)}, u32[]{:S(2)}, u32[]{:S(2)}) %collective-permute-start.4) | collective-permute-done | bytes 163872 | tf_op jit(solution)/shard_map/ppermute | solution.py:442
  27.8 4.1 %collective-permute-done.3.third = bf16[16,5120]{1,0:T(8,128)(2,1)S(1)} collective-permute-done((bf16[16,5120]{1,0:T(8,128)(2,1)S(1)}, bf16[16,5120]{1,0:T(8,128)(2,1)S(1)}, u32[]{:S(2)}, u32[]{:S(2)}) %collective-permute-start.3) | collective-permute-done | bytes 163872 | tf_op jit(solution)/shard_map/ppermute | solution.py:442
  32.0 3.0 %collective-permute-start.7 = (bf16[32,5120]{1,0:T(8,128)(2,1)S(1)}, bf16[32,5120]{1,0:T(8,128)(2,1)S(1)}, u32[]{:S(2)}, u32[]{:S(2)}) collective-permute-start(bf16[32,5120]{1,0:T(8,128)(2,1)S(1)} %get-tuple-element.77.refs_0_), channel_id=1, source_target_pairs={{0,8},{1,9},{2,10},{3,11},{4,12},{5,13},{6,14},{7,15},{8,0},{9,1},... | collective-permute-start | bytes 983048 | tf_op jit(solution)/shard_map/ppermute | solution.py:445
  35.0 8.9 %shard_map.104 = (bf16[128,5120]{1,0:T(8,128)(2,1)}, bf16[128,5120]{1,0:T(8,128)(2,1)}, f32[2,128,432]{2,1,0:T(8,128)}, bf16[128,432]{1,0:T(8,128)(2,1)}, bf16[128,432]{1,0:T(8,128)(2,1)}) custom-call(bf16[128,5120]{1,0:T(8,128)(2,1)S(1)} %bitcast.23, f32[1,5120]{1,0:T(1,128)S(1)} %copy-done.3, bf16[432,5120]{1,0:T(8,128)(2,1)} %bitcast.40, ...), custom_call_target="tpu_custom_call" | custom-call | flops 3397386240 | bytes 15728640 | tf_op jit(solution)/shard_map/pallas_call | solution.py:354
  43.9 4.0 %all-to-all-start.1 = ((bf16[8,16,5120]{2,1,0:T(8,128)(2,1)}), bf16[8,16,5120]{2,1,0:T(8,128)(2,1)S(1)}, u32[]{:S(2)}, u32[]{:S(2)}) async-start(bf16[8,16,5120]{2,1,0:T(8,128)(2,1)} %bitcast.6), calls=%async_computation.1 | async-start | bytes 2621440 | tf_op jit(solution)/shard_map/all_to_all | solution.py:378
  48.2 13.0 %all-to-all-done.1 = bf16[8,16,5120]{2,1,0:T(8,128)(2,1)S(1)} async-done(((bf16[8,16,5120]{2,1,0:T(8,128)(2,1)}), bf16[8,16,5120]{2,1,0:T(8,128)(2,1)S(1)}, u32[]{:S(2)}, u32[]{:S(2)}) %all-to-all-start.1) | async-done | bytes 1310752 | tf_op jit(solution)/shard_map/all_to_all | solution.py:378
  61.9 2.6 %collective-permute-start.8 = (bf16[16,5120]{1,0:T(8,128)(2,1)S(1)}, bf16[16,5120]{1,0:T(8,128)(2,1)S(1)}, u32[]{:S(2)}, u32[]{:S(2)}) collective-permute-start(bf16[16,5120]{1,0:T(8,128)(2,1)S(1)} %shard_map.105), channel_id=1, source_target_pairs={{0,16},{16,32},{32,48},{48,64},{64,80},{80,96},{96,112},{1,17},{17... | collective-permute-start | bytes 491528 | tf_op jit(solution)/shard_map/ppermute | solution.py:403
  64.5 3.5 %collective-permute-done.8.rows.x = bf16[16,5120]{1,0:T(8,128)(2,1)S(1)} collective-permute-done((bf16[16,5120]{1,0:T(8,128)(2,1)S(1)}, bf16[16,5120]{1,0:T(8,128)(2,1)S(1)}, u32[]{:S(2)}, u32[]{:S(2)}) %collective-permute-start.8) | collective-permute-done | bytes 163872 | tf_op jit(solution)/shard_map/ppermute | solution.py:403
  68.0 5.2 %collective-permute-done.9.refs_3_ = bf16[32,5120]{1,0:T(8,128)(2,1)S(1)} collective-permute-done((bf16[32,5120]{1,0:T(8,128)(2,1)S(1)}, bf16[32,5120]{1,0:T(8,128)(2,1)S(1)}, u32[]{:S(2)}, u32[]{:S(2)}) %collective-permute-start.9) | collective-permute-done | bytes 327712 | tf_op jit(solution)/shard_map/ppermute | solution.py:456
  74.3 3.8 %all-to-all-start.2 = ((bf16[8,16,5120]{2,1,0:T(8,128)(2,1)}), bf16[8,16,5120]{2,1,0:T(8,128)(2,1)S(1)}, u32[]{:S(2)}, u32[]{:S(2)}) async-start(bf16[8,16,5120]{2,1,0:T(8,128)(2,1)} %bitcast.8), calls=%async_computation.2 | async-start | bytes 2621440 | tf_op jit(solution)/shard_map/all_to_all | solution.py:378
  78.6 6.7 %shard_map.107 = (bf16[16,5120]{1,0:T(8,128)(2,1)S(1)}, bf16[128,5120]{1,0:T(8,128)(2,1)}, f32[2,128,432]{2,1,0:T(8,128)}) custom-call(bf16[32,5120]{1,0:T(8,128)(2,1)S(1)} %get-tuple-element.77.refs_0_, bf16[32,5120]{1,0:T(8,128)(2,1)S(1)} %get-tuple-element.80.refs_1_, bf16[32,5120]{1,0:T(8,128)(2,1)S(1)} %collective-permute-done.7.refs_2_, ...), custom_call_target="tpu_custom_call" | custom-call | flops 3397386240 | bytes 7864320 | tf_op jit(solution)/shard_map/pallas_call | solution.py:354
  85.4 5.7 %all-to-all-done.2 = bf16[8,16,5120]{2,1,0:T(8,128)(2,1)S(1)} async-done(((bf16[8,16,5120]{2,1,0:T(8,128)(2,1)}), bf16[8,16,5120]{2,1,0:T(8,128)(2,1)S(1)}, u32[]{:S(2)}, u32[]{:S(2)}) %all-to-all-start.2) | async-done | bytes 1310752 | tf_op jit(solution)/shard_map/all_to_all | solution.py:378
  91.1 8.3 %shard_map.108 = (f32[1,5120]{1,0:T(1,128)S(1)}, bf16[16,5120]{1,0:T(8,128)(2,1)S(1)}, bf16[128,5120]{1,0:T(8,128)(2,1)}, bf16[128,5120]{1,0:T(8,128)(2,1)}, bf1...) custom-call(bf16[128,5120]{1,0:T(8,128)(2,1)S(1)} %bitcast.31, ...), custom_call_target="tpu_custom_call" | custom-call | flops 3397386240 | bytes 10485760 | tf_op jit(solution)/shard_map/pallas_call | solution.py:354
  99.4 3.6 %all-to-all-start.3 = ((bf16[8,16,5120]{2,1,0:T(8,128)(2,1)}), bf16[8,16,5120]{2,1,0:T(8,128)(2,1)S(1)}, u32[]{:S(2)}, u32[]{:S(2)}) async-start(bf16[8,16,5120]{2,1,0:T(8,128)(2,1)} %bitcast.11), calls=%async_computation.3 | async-start | bytes 2621440 | tf_op jit(solution)/shard_map/all_to_all | solution.py:378
  103.0 6.6 %shard_map.110 = (bf16[32,5120]{1,0:T(8,128)(2,1)S(1)}, bf16[32,5120]{1,0:T(8,128)(2,1)}, bf16[32,5120]{1,0:T(8,128)(2,1)S(1)}, bf16[32,5120]{1,0:T(8,128)(2,1)S(1)}) custom-call(s32[128,1]{1,0:T(8,128)S(1)} %add.296.to_target, bf16[128,432]{1,0:T(8,128)(2,1)} %get-tuple-element.87.hidden_a.refs_14_, bf16[128,432]{1,0:T(8,128)(2,1)} %get-tuple-element.119.hidden_b, ...), custom_call_target="tpu_custom_call" | custom-call | flops 2264924160 | bytes 7864320 | tf_op jit(solution)/shard_map/pallas_call | solution.py:354
  110.3 5.8 %all-to-all-done.3 = bf16[8,16,5120]{2,1,0:T(8,128)(2,1)S(1)} async-done(((bf16[8,16,5120]{2,1,0:T(8,128)(2,1)}), bf16[8,16,5120]{2,1,0:T(8,128)(2,1)S(1)}, u32[]{:S(2)}, u32[]{:S(2)}) %all-to-all-start.3) | async-done | bytes 1310752 | tf_op jit(solution)/shard_map/all_to_all | solution.py:378
  117.2 2.1 %collective-permute-start.12 = (bf16[32,5120]{1,0:T(8,128)(2,1)S(1)}, bf16[32,5120]{1,0:T(8,128)(2,1)S(1)}, u32[]{:S(2)}, u32[]{:S(2)}) collective-permute-start(bf16[32,5120]{1,0:T(8,128)(2,1)S(1)} %get-tuple-element.94), channel_id=1, source_target_pairs={{0,6},{1,7},{2,0},{3,1},{4,2},{5,3},{6,4},{7,5},{8,14},{9,15},{10,... | collective-permute-start | bytes 983048 | tf_op jit(solution)/shard_map/ppermute | solution.py:484
  119.3 2.4 %collective-permute-start.10 = (bf16[16,5120]{1,0:T(8,128)(2,1)S(1)}, bf16[16,5120]{1,0:T(8,128)(2,1)S(1)}, u32[]{:S(2)}, u32[]{:S(2)}) collective-permute-start(bf16[16,5120]{1,0:T(8,128)(2,1)S(1)} %shard_map.109), channel_id=1, source_target_pairs={{16,0},{32,16},{48,32},{64,48},{80,64},{96,80},{112,96},{17,1},{33... | collective-permute-start | bytes 491528 | tf_op jit(solution)/shard_map/ppermute | solution.py:403
  121.7 6.6 %collective-permute-done.10.rows.c = bf16[16,5120]{1,0:T(8,128)(2,1)S(1)} collective-permute-done((bf16[16,5120]{1,0:T(8,128)(2,1)S(1)}, bf16[16,5120]{1,0:T(8,128)(2,1)S(1)}, u32[]{:S(2)}, u32[]{:S(2)}) %collective-permute-start.10) | collective-permute-done | bytes 163872 | tf_op jit(solution)/shard_map/ppermute | solution.py:403
  128.5 17.6 %all_to_all.69 = bf16[8,16,5120]{2,1,0:T(8,128)(2,1)S(1)} all-to-all(bf16[8,16,5120]{2,1,0:T(8,128)(2,1)S(1)} %bitcast.27), channel_id=1, replica_groups={{0,2,4,6,8,10,12,14},{1,3,5,7,9,11,13,15},{16,18,20,22,24,26,28,30},{17..., dimensions={0} | all-to-all | bytes 2621440 | tf_op jit(solution)/shard_map/all_to_all | solution.py:378
  147.1 9.2 %shard_map.112 = (bf16[128,5760]{1,0:T(8,128)(2,1)}, bf16[128,5120]{1,0:T(8,128)(2,1)}, bf16[128,432]{1,0:T(8,128)(2,1)}, bf16[128,432]{1,0:T(8,128)(2,1)}) custom-call(bf16[128,5120]{1,0:T(8,128)(2,1)S(1)} %bitcast.24, f32[1,5120]{1,0:T(1,128)S(1)} %copy-done.3, f32[1,5120]{1,0:T(1,128)S(1)} %get-tuple-element.97.gain_two, ...), custom_call_target="tpu_custom_call" | custom-call | flops 3397386240 | bytes 15728640 | tf_op jit(solution)/shard_map/pallas_call | solution.py:354
  156.3 17.6 %collective-permute-start.14 = (bf16[128,5120]{1,0:T(8,128)(2,1)}, bf16[128,5120]{1,0:T(8,128)(2,1)}, u32[]{:S(2)}, u32[]{:S(2)}) collective-permute-start(bf16[128,5120]{1,0:T(8,128)(2,1)} %get-tuple-element.103.normed_in.refs_0_), channel_id=1, source_target_pairs={{0,1},{1,0},{2,3},{3,2},{4,5},{5,4},{6,7},{7,6},{8,9},{9,8},{10,11... | collective-permute-start | bytes 3932168 | tf_op jit(solution)/shard_map/ppermute | solution.py:389
  174.5 4.2 %all-to-all-start.5 = ((bf16[8,16,5760]{2,1,0:T(8,128)(2,1)}), bf16[8,16,5760]{2,1,0:T(8,128)(2,1)S(1)}, u32[]{:S(2)}, u32[]{:S(2)}) async-start(bf16[8,16,5760]{2,1,0:T(8,128)(2,1)} %bitcast.15), calls=%async_computation.5 | async-start | bytes 2949120 | tf_op jit(solution)/shard_map/all_to_all | solution.py:378
  179.4 1.5 collective-permute-done.18.refs_9_
  181.3 1.5 collective-permute-done.19.refs_11_
  185.7 2.6 %collective-permute-start.22 = (bf16[16,5120]{1,0:T(8,128)(2,1)S(1)}, bf16[16,5120]{1,0:T(8,128)(2,1)S(1)}, u32[]{:S(2)}, u32[]{:S(2)}) collective-permute-start(bf16[16,5120]{1,0:T(8,128)(2,1)S(1)} %get-tuple-element.130), channel_id=1, source_target_pairs={{0,8},{1,9},{2,10},{3,11},{4,12},{5,13},{6,14},{7,15},{8,0},{9,1},... | collective-permute-start | bytes 491528 | tf_op jit(solution)/shard_map/ppermute | solution.py:501
  188.4 11.9 %shard_map.113 = (bf16[432,5120]{1,0:T(8,128)(2,1)}, bf16[432,5120]{1,0:T(8,128)(2,1)}) custom-call(bf16[128,5120]{1,0:T(8,128)(2,1)} %get-tuple-element.103.normed_in.refs_0_, bf16[128,5120]{1,0:T(8,128)(2,1)} %collective-permute-done.14.refs_1_, bf16[128,5120]{1,0:T(8,128)(2,1)} %get-tuple-element.105.refs_2_, ...), custom_call_target="tpu_custom_call" | custom-call | flops 4529848320 | bytes 20971520 | tf_op jit(solution)/shard_map/pallas_call | solution.py:508
  200.3 2.6 %collective-permute-done.22.given = bf16[16,5120]{1,0:T(8,128)(2,1)S(1)} collective-permute-done((bf16[16,5120]{1,0:T(8,128)(2,1)S(1)}, bf16[16,5120]{1,0:T(8,128)(2,1)S(1)}, u32[]{:S(2)}, u32[]{:S(2)}) %collective-permute-start.22) | collective-permute-done | bytes 163872 | tf_op jit(solution)/shard_map/ppermute | solution.py:501
  (96 shorter events, 21.3 us)
Async XLA Ops:
  0.6 61.1 %copy-start = (s32[8,16]{1,0:T(8,128)S(1)}, s32[8,16]{1,0:T(8,128)}, u32[]{:S(2)}) copy-start(s32[8,16]{1,0:T(8,128)} %param.11) | copy-start | bytes 1540
  0.6 2.0 collective-permute-start
  2.6 32.3 %collective-permute-start.5 = (bf16[432,5120]{1,0:T(8,128)(2,1)}, bf16[432,5120]{1,0:T(8,128)(2,1)}, u32[]{:S(2)}, u32[]{:S(2)}) collective-permute-start(bf16[432,5120]{1,0:T(8,128)(2,1)} %bitcast.39), channel_id=1, source_target_pairs={{0,1},{1,0},{2,3},{3,2},{4,5},{5,4},{6,7},{7,6},{8,9},{9,8},{10,11... | collective-permute-start | bytes 13271048 | tf_op jit(solution)/shard_map/ppermute | solution.py:389
  3.0 32.0 %collective-permute-start.6 = (bf16[432,5120]{1,0:T(8,128)(2,1)}, bf16[432,5120]{1,0:T(8,128)(2,1)}, u32[]{:S(2)}, u32[]{:S(2)}) collective-permute-start(bf16[432,5120]{1,0:T(8,128)(2,1)} %bitcast.34), channel_id=1, source_target_pairs={{0,1},{1,0},{2,3},{3,2},{4,5},{5,4},{6,7},{7,6},{8,9},{9,8},{10,11... | collective-permute-start | bytes 13271048 | tf_op jit(solution)/shard_map/ppermute | solution.py:389
  4.5 0.7 collective-permute-start.1
  7.2 27.8 %copy-start.3 = (f32[1,5120]{1,0:T(1,128)S(1)}, f32[1,5120]{1,0:T(1,128)}, u32[]{:S(2)}) copy-start(f32[1,5120]{1,0:T(1,128)} %gain.9) | copy-start | bytes 61444
  7.2 24.7 %all-to-all-start = ((bf16[8,16,5120]{2,1,0:T(8,128)(2,1)}), bf16[8,16,5120]{2,1,0:T(8,128)(2,1)S(1)}, u32[]{:S(2)}, u32[]{:S(2)}) async-start(bf16[8,16,5120]{2,1,0:T(8,128)(2,1)} %bitcast.2), calls=%async_computation | async-start | bytes 2621440 | tf_op jit(solution)/shard_map/all_to_all | solution.py:378
  14.9 13.0 %collective-permute-start.4 = (bf16[16,5120]{1,0:T(8,128)(2,1)S(1)}, bf16[16,5120]{1,0:T(8,128)(2,1)S(1)}, u32[]{:S(2)}, u32[]{:S(2)}) collective-permute-start(bf16[16,5120]{1,0:T(8,128)(2,1)S(1)} %shard_map.101.own), channel_id=1, source_target_pairs={{0,2},{1,3},{2,4},{3,5},{4,6},{5,7},{6,0},{7,1},{8,10},{9,11},{10,... | collective-permute-start | bytes 491528 | tf_op jit(solution)/shard_map/ppermute | solution.py:442
  16.3 15.6 %collective-permute-start.3 = (bf16[16,5120]{1,0:T(8,128)(2,1)S(1)}, bf16[16,5120]{1,0:T(8,128)(2,1)S(1)}, u32[]{:S(2)}, u32[]{:S(2)}) collective-permute-start(bf16[16,5120]{1,0:T(8,128)(2,1)S(1)} %shard_map.101.own), channel_id=1, source_target_pairs={{0,4},{1,5},{2,6},{3,7},{4,0},{5,1},{6,2},{7,3},{8,12},{9,13},{10,... | collective-permute-start | bytes 491528 | tf_op jit(solution)/shard_map/ppermute | solution.py:442
  18.7 13.2 %collective-permute-start.2 = (bf16[16,5120]{1,0:T(8,128)(2,1)S(1)}, bf16[16,5120]{1,0:T(8,128)(2,1)S(1)}, u32[]{:S(2)}, u32[]{:S(2)}) collective-permute-start(bf16[16,5120]{1,0:T(8,128)(2,1)S(1)} %shard_map.101.own), channel_id=1, source_target_pairs={{1,7},{3,1},{5,3},{7,5},{9,15},{11,9},{13,11},{15,13},{17,23},{19,... | collective-permute-start | bytes 491528 | tf_op jit(solution)/shard_map/ppermute | solution.py:442
  32.0 11.9 %collective-permute-start.7 = (bf16[32,5120]{1,0:T(8,128)(2,1)S(1)}, bf16[32,5120]{1,0:T(8,128)(2,1)S(1)}, u32[]{:S(2)}, u32[]{:S(2)}) collective-permute-start(bf16[32,5120]{1,0:T(8,128)(2,1)S(1)} %get-tuple-element.77.refs_0_), channel_id=1, source_target_pairs={{0,8},{1,9},{2,10},{3,11},{4,12},{5,13},{6,14},{7,15},{8,0},{9,1},... | collective-permute-start | bytes 983048 | tf_op jit(solution)/shard_map/ppermute | solution.py:445
  43.9 17.3 %all-to-all-start.1 = ((bf16[8,16,5120]{2,1,0:T(8,128)(2,1)}), bf16[8,16,5120]{2,1,0:T(8,128)(2,1)S(1)}, u32[]{:S(2)}, u32[]{:S(2)}) async-start(bf16[8,16,5120]{2,1,0:T(8,128)(2,1)} %bitcast.6), calls=%async_computation.1 | async-start | bytes 2621440 | tf_op jit(solution)/shard_map/all_to_all | solution.py:378
  61.4 11.8 %collective-permute-start.9 = (bf16[32,5120]{1,0:T(8,128)(2,1)S(1)}, bf16[32,5120]{1,0:T(8,128)(2,1)S(1)}, u32[]{:S(2)}, u32[]{:S(2)}) collective-permute-start(bf16[32,5120]{1,0:T(8,128)(2,1)S(1)} %get-tuple-element.80.refs_1_), channel_id=1, source_target_pairs={{0,8},{1,9},{2,10},{3,11},{4,12},{5,13},{6,14},{7,15},{8,0},{9,1},... | collective-permute-start | bytes 983048 | tf_op jit(solution)/shard_map/ppermute | solution.py:456
  61.9 6.1 %collective-permute-start.8 = (bf16[16,5120]{1,0:T(8,128)(2,1)S(1)}, bf16[16,5120]{1,0:T(8,128)(2,1)S(1)}, u32[]{:S(2)}, u32[]{:S(2)}) collective-permute-start(bf16[16,5120]{1,0:T(8,128)(2,1)S(1)} %shard_map.105), channel_id=1, source_target_pairs={{0,16},{16,32},{32,48},{48,64},{64,80},{80,96},{96,112},{1,17},{17... | collective-permute-start | bytes 491528 | tf_op jit(solution)/shard_map/ppermute | solution.py:403
  74.3 16.8 %all-to-all-start.2 = ((bf16[8,16,5120]{2,1,0:T(8,128)(2,1)}), bf16[8,16,5120]{2,1,0:T(8,128)(2,1)S(1)}, u32[]{:S(2)}, u32[]{:S(2)}) async-start(bf16[8,16,5120]{2,1,0:T(8,128)(2,1)} %bitcast.8), calls=%async_computation.2 | async-start | bytes 2621440 | tf_op jit(solution)/shard_map/all_to_all | solution.py:378
  99.4 16.8 %all-to-all-start.3 = ((bf16[8,16,5120]{2,1,0:T(8,128)(2,1)}), bf16[8,16,5120]{2,1,0:T(8,128)(2,1)S(1)}, u32[]{:S(2)}, u32[]{:S(2)}) async-start(bf16[8,16,5120]{2,1,0:T(8,128)(2,1)} %bitcast.11), calls=%async_computation.3 | async-start | bytes 2621440 | tf_op jit(solution)/shard_map/all_to_all | solution.py:378
  116.5 11.9 %collective-permute-start.11 = (bf16[32,5120]{1,0:T(8,128)(2,1)}, bf16[32,5120]{1,0:T(8,128)(2,1)S(1)}, u32[]{:S(2)}, u32[]{:S(2)}) collective-permute-start(bf16[32,5120]{1,0:T(8,128)(2,1)} %get-tuple-element.93), channel_id=1, source_target_pairs={{0,2},{1,3},{2,4},{3,5},{4,6},{5,7},{6,0},{7,1},{8,10},{9,11},{10,... | collective-permute-start | bytes 983048 | tf_op jit(solution)/shard_map/ppermute | solution.py:484
  117.2 11.3 %collective-permute-start.12 = (bf16[32,5120]{1,0:T(8,128)(2,1)S(1)}, bf16[32,5120]{1,0:T(8,128)(2,1)S(1)}, u32[]{:S(2)}, u32[]{:S(2)}) collective-permute-start(bf16[32,5120]{1,0:T(8,128)(2,1)S(1)} %get-tuple-element.94), channel_id=1, source_target_pairs={{0,6},{1,7},{2,0},{3,1},{4,2},{5,3},{6,4},{7,5},{8,14},{9,15},{10,... | collective-permute-start | bytes 983048 | tf_op jit(solution)/shard_map/ppermute | solution.py:484
  119.3 9.0 %collective-permute-start.10 = (bf16[16,5120]{1,0:T(8,128)(2,1)S(1)}, bf16[16,5120]{1,0:T(8,128)(2,1)S(1)}, u32[]{:S(2)}, u32[]{:S(2)}) collective-permute-start(bf16[16,5120]{1,0:T(8,128)(2,1)S(1)} %shard_map.109), channel_id=1, source_target_pairs={{16,0},{32,16},{48,32},{64,48},{80,64},{96,80},{112,96},{17,1},{33... | collective-permute-start | bytes 491528 | tf_op jit(solution)/shard_map/ppermute | solution.py:403
  146.1 10.2 %collective-permute-start.13 = (bf16[32,5120]{1,0:T(8,128)(2,1)S(1)}, bf16[32,5120]{1,0:T(8,128)(2,1)S(1)}, u32[]{:S(2)}, u32[]{:S(2)}) collective-permute-start(bf16[32,5120]{1,0:T(8,128)(2,1)S(1)} %copy-done.6), channel_id=1, source_target_pairs={{0,4},{1,5},{2,6},{3,7},{4,0},{5,1},{6,2},{7,3},{8,12},{9,13},{10,... | collective-permute-start | bytes 983048 | tf_op jit(solution)/shard_map/ppermute | solution.py:488
  156.3 32.0 %collective-permute-start.14 = (bf16[128,5120]{1,0:T(8,128)(2,1)}, bf16[128,5120]{1,0:T(8,128)(2,1)}, u32[]{:S(2)}, u32[]{:S(2)}) collective-permute-start(bf16[128,5120]{1,0:T(8,128)(2,1)} %get-tuple-element.103.normed_in.refs_0_), channel_id=1, source_target_pairs={{0,1},{1,0},{2,3},{3,2},{4,5},{5,4},{6,7},{7,6},{8,9},{9,8},{10,11... | collective-permute-start | bytes 3932168 | tf_op jit(solution)/shard_map/ppermute | solution.py:389
  173.9 14.4 %collective-permute-start.15 = (bf16[128,5120]{1,0:T(8,128)(2,1)}, bf16[128,5120]{1,0:T(8,128)(2,1)}, u32[]{:S(2)}, u32[]{:S(2)}) collective-permute-start(bf16[128,5120]{1,0:T(8,128)(2,1)} %get-tuple-element.105.refs_2_), channel_id=1, source_target_pairs={{0,1},{1,0},{2,3},{3,2},{4,5},{5,4},{6,7},{7,6},{8,9},{9,8},{10,11... | collective-permute-start | bytes 3932168 | tf_op jit(solution)/shard_map/ppermute | solution.py:389
  174.0 14.3 %collective-permute-start.16 = (bf16[128,5120]{1,0:T(8,128)(2,1)}, bf16[128,5120]{1,0:T(8,128)(2,1)}, u32[]{:S(2)}, u32[]{:S(2)}) collective-permute-start(bf16[128,5120]{1,0:T(8,128)(2,1)} %get-tuple-element.107.refs_4_), channel_id=1, source_target_pairs={{0,1},{1,0},{2,3},{3,2},{4,5},{5,4},{6,7},{7,6},{8,9},{9,8},{10,11... | collective-permute-start | bytes 3932168 | tf_op jit(solution)/shard_map/ppermute | solution.py:389
  174.4 13.9 %collective-permute-start.17 = (bf16[128,5120]{1,0:T(8,128)(2,1)}, bf16[128,5120]{1,0:T(8,128)(2,1)}, u32[]{:S(2)}, u32[]{:S(2)}) collective-permute-start(bf16[128,5120]{1,0:T(8,128)(2,1)} %get-tuple-element.109.refs_6_), channel_id=1, source_target_pairs={{0,1},{1,0},{2,3},{3,2},{4,5},{5,4},{6,7},{7,6},{8,9},{9,8},{10,11... | collective-permute-start | bytes 3932168 | tf_op jit(solution)/shard_map/ppermute | solution.py:389
  174.5 29.0 %all-to-all-start.5 = ((bf16[8,16,5760]{2,1,0:T(8,128)(2,1)}), bf16[8,16,5760]{2,1,0:T(8,128)(2,1)S(1)}, u32[]{:S(2)}, u32[]{:S(2)}) async-start(bf16[8,16,5760]{2,1,0:T(8,128)(2,1)} %bitcast.15), calls=%async_computation.5 | async-start | bytes 2949120 | tf_op jit(solution)/shard_map/all_to_all | solution.py:378
  178.7 2.2 %collective-permute-start.18 = (bf16[128,432]{1,0:T(8,128)(2,1)}, bf16[128,432]{1,0:T(8,128)(2,1)S(1)}, u32[]{:S(2)}, u32[]{:S(2)}) collective-permute-start(bf16[128,432]{1,0:T(8,128)(2,1)} %get-tuple-element.112), channel_id=1, source_target_pairs={{0,1},{1,0},{2,3},{3,2},{4,5},{5,4},{6,7},{7,6},{8,9},{9,8},{10,11... | collective-permute-start | bytes 331784 | tf_op jit(solution)/shard_map/ppermute | solution.py:389
  180.9 1.9 collective-permute-start.19
  182.8 1.4 collective-permute-start.20
  184.2 1.6 collective-permute-start.21
  185.7 17.2 %collective-permute-start.22 = (bf16[16,5120]{1,0:T(8,128)(2,1)S(1)}, bf16[16,5120]{1,0:T(8,128)(2,1)S(1)}, u32[]{:S(2)}, u32[]{:S(2)}) collective-permute-start(bf16[16,5120]{1,0:T(8,128)(2,1)S(1)} %get-tuple-element.130), channel_id=1, source_target_pairs={{0,8},{1,9},{2,10},{3,11},{4,12},{5,13},{6,14},{7,15},{8,0},{9,1},... | collective-permute-start | bytes 491528 | tf_op jit(solution)/shard_map/ppermute | solution.py:501
  203.0 3.4 %collective-permute-start.23 = (bf16[16,5120]{1,0:T(8,128)(2,1)S(1)}, bf16[16,5120]{1,0:T(8,128)(2,1)S(1)}, u32[]{:S(2)}, u32[]{:S(2)}) collective-permute-start(bf16[16,5120]{1,0:T(8,128)(2,1)S(1)} %shard_map.116.refs_0_), channel_id=1, source_target_pairs={{0,1},{1,0},{2,3},{3,2},{4,5},{5,4},{6,7},{7,6},{8,9},{9,8},{10,11... | collective-permute-start | bytes 491528 | tf_op jit(solution)/shard_map/ppermute | solution.py:389
  204.6 1.2 collective-permute-start.24
  (10 other events, 65.7 us)

commit v3 on v2

--- a/solution.py
+++ b/solution.py
@@ -145,6 +145,19 @@
     first_pair[ROWS:, :] = even[...] + odd[...]
     second_pair[:ROWS, :] = third[...]
     second_pair[ROWS:, :] = fourth[...]
+
+
+def prepare_kernel(other, index, rows, own_in, wide, share, own, sem, sems):
+    fetch = pltpu.make_async_copy(own_in, own, sem)
+    fetch.start()
+    copies = []
+    for at in range(CHIPS):
+        copies.append(pltpu.make_async_copy(rows, wide.at[at * ROWS : (at + 1) * ROWS, :], sems.at[at]))
+        copies[-1].start()
+    fetch.wait()
+    pick_kernel(own, other, index, share)
+    for copy in copies:
+        copy.wait()
 
 
 def spread_kernel(rows, out):
@@ -207,47 +220,54 @@
     stores.finish()
 
 
-def target_kernel(to_target, hidden_a, hidden_b, down_a, down_b, near, second, third, fourth, wd, sd, hidden, sh):
+def target_kernel(
+    to_target, hidden_a, hidden_b, down_a, down_b, near_out, far_out, wd, sd, proj, hidden, sh, so
+):
     fetches = [pltpu.make_async_copy(ref, hidden.at[at], sh.at[at]) for at, ref in enumerate((hidden_a, hidden_b))]
     for fetch in fetches:
         fetch.start()
     downs = Weights((down_a, down_b), wd, sd)
     downs.start_all()
+    stores = Stores(so)
     sort = one_hot(to_target[...], TALL)
     left = []
     for half, fetch in enumerate(fetches):
         fetch.wait()
         left.append(dot_nn(sort, hidden[half]).astype(BF))
-    for at, cols in enumerate(chunks(near.shape[1])):
+    for at, cols in enumerate(chunks(proj.shape[1])):
         downs.wait(at)
-        term = (dot_nn(left[0], wd[0, :, cols]) + dot_nn(left[1], wd[1, :, cols])).astype(BF)
-        for part, out in enumerate((near, second, third, fourth)):
-            out[:, cols] = term[2 * ROWS * part : 2 * ROWS * (part + 1)]
-
-
-def sum_kernel(near, second, third, fourth, mine, other):
+        proj[:, cols] = (dot_nn(left[0], wd[0, :, cols]) + dot_nn(left[1], wd[1, :, cols])).astype(BF)
+        stores.add(proj.at[: 4 * ROWS, cols], near_out.at[:, cols])
+        stores.add(proj.at[4 * ROWS :, cols], far_out.at[:, cols])
+    stores.finish()
+
+
+def sum_kernel(near, far, mine, second, third, fourth):
     for cols in chunks(near.shape[1]):
-        total = near[:, cols].astype(F32) + second[:, cols].astype(F32)
-        total = total + (third[:, cols].astype(F32) + fourth[:, cols].astype(F32))
+        total = near[:, cols].astype(F32) + far[:, cols].astype(F32)
         mine[:, cols] = total[:ROWS]
-        other[:, cols] = total[ROWS:].astype(BF)
-
-
-def second_out_kernel(own_rows, mine, given, out):
+        for at, out in enumerate((second, third, fourth)):
+            out[:, cols] = total[(at + 1) * ROWS : (at + 2) * ROWS].astype(BF)
+
+
+def second_out_kernel(own_rows, mine, second, third, fourth, out):
     for cols in chunks(out.shape[1]):
-        out[:, cols] = (own_rows[:, cols].astype(F32) + (mine[:, cols] + given[:, cols].astype(F32))).astype(BF)
+        total = mine[:, cols] + second[:, cols].astype(F32) + third[:, cols].astype(F32) + fourth[:, cols].astype(F32)
+        out[:, cols] = (own_rows[:, cols].astype(F32) + total).astype(BF)
 
 
 def first_back_kernel(
-    c, gain, gain_two, slope_in, normed_in, up_a, up_b, down_a, down_b,
-    dn, c_out, d_act_a_out, d_act_b_out,
-    wu, wd, su, sd, d_act, slope, normed, sh, so,
+    c, gain, gain_two, slope_in, normed_in, d_act_two_b, hidden_one_b, hidden_two_b, up_a, up_b, down_a, down_b,
+    dn, c_out, d_act_a_out, thin_out,
+    wu, wd, su, sd, d_act, slope, normed, thin, sh, so,
 ):
     width = c.shape[1]
     downs = Weights((down_a, down_b), wd, sd)
     ups = Weights((up_a, up_b), wu, su)
     downs.start_all()
     fetches = [pltpu.make_async_copy(slope_in, slope, sh.at[0]), pltpu.make_async_copy(normed_in, normed, sh.at[1])]
+    for at, source in enumerate((d_act_two_b, hidden_one_b, hidden_two_b)):
+        fetches.append(pltpu.make_async_copy(source, thin.at[at], sh.at[2 + at]))
     stores = Stores(so)
     stores.add(c, c_out)
     total = [None, None]
@@ -265,7 +285,8 @@
     for half in range(2):
         d_act[half] = (total[half] * slope[half]).astype(BF)
     stores.add(d_act.at[0], d_act_a_out)
-    stores.add(d_act.at[1], d_act_b_out)
+    stores.add(d_act.at[1], thin_out.at[0])
+    stores.add(thin, thin_out.at[1:4])
     gain_pieces = []
     for at, cols in enumerate(chunks(width)):
         ups.wait(at)
@@ -295,8 +316,7 @@
         out[:, cols] = (x[:, cols].astype(F32) + add_blocks(blocks, cols)).astype(BF)
 
 
-def rows_back_kernel(blocks, x, c, gain, *rest):
-    out, spread = rest[0], rest[-1]
+def rows_back_kernel(blocks, x, c, gain, out, spread):
     width = x.shape[1]
     scale = row_scale(x)
     along = jnp.zeros((ROWS, 128), F32)
@@ -310,27 +330,28 @@
     for cols in chunks(width):
         vhat = x[:, cols].astype(F32) * scale
         out[:, cols] = (c[:, cols].astype(F32) + scale * (spread[:, cols] - vhat * mean)).astype(BF)
-    if len(rest) == 3:
-        extra = add_blocks(blocks, slice(width, blocks.shape[1]))
-        line = extra[:8] + extra[8:]
-        rest[1][...] = jnp.concatenate([line[at : at + 1] for at in range(8)], axis=1)
+
+
+def last_kernel(blocks, x, c, gain, out, gain_sum, spread):
+    width = x.shape[1]
+    rows_back_kernel(blocks, x, c, gain, out, spread)
+    extra = add_blocks(blocks, slice(width, blocks.shape[1]))
+    line = extra[:8] + extra[8:]
+    gain_sum[...] = jnp.concatenate([line[at : at + 1] for at in range(8)], axis=1)
 
 
 def grads_kernel(*refs):
-    normed, c, slim = refs[0:4], refs[4:8], refs[8:16]
-    out_up, out_down, left_up, left_down, held, sems = refs[16:22]
+    normed, c, (d_act_one, d_act_two, hidden_one, hidden_two, other) = refs[0:4], refs[4:8], refs[8:13]
+    out_up, out_down, left_up, left_down = refs[13:17]
 
     @pl.when(pl.program_id(0) == 0)
     def _():
-        copies = [pltpu.make_async_copy(ref, held.at[at], sems.at[at]) for at, ref in enumerate(slim)]
-        for copy in copies:
-            copy.start()
-        for at in range(4):
-            rows = slice(at * TALL, (at + 1) * TALL)
-            copies[at].wait()
-            left_up[:, rows] = held[at].T
-            copies[4 + at].wait()
-            left_down[:, rows] = held[4 + at].T
+        for at, own in enumerate((d_act_one, d_act_two)):
+            left_up[:, 2 * at * TALL : (2 * at + 1) * TALL] = own[...].T
+            left_up[:, (2 * at + 1) * TALL : (2 * at + 2) * TALL] = other[at].T
+        for at, own in enumerate((hidden_one, hidden_two)):
+            left_down[:, 2 * at * TALL : (2 * at + 1) * TALL] = own[...].T
+            left_down[:, (2 * at + 1) * TALL : (2 * at + 2) * TALL] = other[2 + at].T
 
     right = jnp.concatenate([ref[...] for ref in normed], axis=0)
     out_up[...] = dot_nn(left_up[...], right).astype(BF)
@@ -380,9 +401,13 @@
     )
 
 
+def spread(rows):
+    width = rows.shape[1]
+    return call(spread_kernel, [in_vmem(TALL, width)], [rows], limit=4, moved=TALL * width * 4)[0]
+
+
 def from_chips(rows):
-    width = rows.shape[1]
-    return to_chips(call(spread_kernel, [in_vmem(TALL, width)], [rows], limit=4, moved=TALL * width * 4)[0])
+    return to_chips(spread(rows))
 
 
 def swap(value):
@@ -428,16 +453,20 @@
     apart_y, apart_z = (wanted // 2 - chip) % 4, (wanted // 8) ^ (chip // 4)
     pick = ((apart_z * 4 + apart_y) * ROWS + (wanted % 2) * CHIPS + chips[:, None]).reshape(TALL, 1)
     cot_index = (jnp.where(pair == core, 0, ROWS)[:, None] + 2 * chips[None, :] + core).reshape(ROWS, 1)
-    owner = (((chip // 4) ^ pair) * 4)[None, :] + ((chip + jnp.arange(4, dtype=jnp.int32)) % 4)[:, None]
+    owner = ((chip // 4) ^ pair)[:, None] * 4 + ((chip + jnp.arange(4, dtype=jnp.int32)) % 4)[None, :]
     to_target = (owner.reshape(CHIPS, 1, 1) * 2 + pair[None, :, None]) ^ mine[None, None, :]
     to_target = (to_target + chips[None, None, :] * ROWS).reshape(TALL, 1)
     own_target = to_target[:ROWS]
     own_pick = (chip * ROWS + slots).reshape(ROWS, 1)
     out_index = (jnp.where(slots % 2 == core, 0, ROWS) + core * CHIPS + slots // 2).reshape(ROWS, 1)
 
-    cot_half = call(pick_kernel, [block], [cot_in, cot_b, cot_index], moved=moved // 4)[0]
+    wide_rows, cot_half = call(
+        prepare_kernel, [in_vmem(TALL, width), block], [cot_b, cot_index], [rows_in, cot_in], [],
+        [kept(ROWS, width), pltpu.SemaphoreType.DMA, dma(CHIPS)], limit=8, moved=moved,
+    )
     even = lax.ppermute(cot_half, "peer", ALONG_Y[3][0::2])
-    x_one = from_chips(after(rows_in, even))
+    wide_rows, even = together(wide_rows, even)
+    x_one = to_chips(wide_rows)
     rest = after(cot_half, even)
     cot_y = [lax.ppermute(rest, "peer", pairs) for pairs in (ALONG_Y[3][1::2], ALONG_Y[2], ALONG_Y[1])]
     cot_a, cot_b = call(join_kernel, [shape(2 * ROWS, width)] * 2, [cot_half, even] + cot_y, moved=moved)
@@ -472,55 +501,55 @@
     )
     blocks = to_chips(d_normed)
     parts = call(
-        target_kernel, [shape(2 * ROWS, width)] * 4, [to_target], [hidden_two, hidden_two_b, down, down_b], [],
-        weight_scratch(units, width, 1) + [kept(2, TALL, units), dma(2)],
+        target_kernel, [], [to_target], [hidden_two, hidden_two_b, down, down_b],
+        [shape(4 * ROWS, width)] * 2,
+        weight_scratch(units, width, 1) + [kept(TALL, width), kept(2, TALL, units), dma(2), dma(2 * steps)],
         limit=20, flops=2 * flops, moved=3 * moved,
     )
+    blocks = after(blocks, *parts)
     d_two = call(
         rows_back_kernel, [block], [blocks, arrived, cot_own, gain], scratch=[kept(ROWS, width, dtype=F32)], moved=moved
     )[0]
     landed = passed_along(d_two, -1)
-    near = together(*parts, d_two)
-    part_up, part_down = lax.ppermute(near[1], "peer", ALONG_Y[1]), lax.ppermute(near[3], "peer", ALONG_Y[3])
-    landed, part_up, part_down = together(landed, part_up, part_down)
     c_all = from_chips(landed)
-    c_all, far = together(c_all, parts[2])
-    part_far = lax.ppermute(far, "peer", ALONG_Y[2])
-    d_normed, c_one, d_act_one, d_act_one_b = call(
+    near, far, c_all = together(*parts, c_all)
+    far = lax.ppermute(far, "peer", ACROSS_Z)
+    d_normed, c_one, d_act_one, thin = call(
         first_back_kernel, [in_vmem(TALL, width + width // 8)], [c_all, gain, gain_two],
-        [slope_one, normed_one, up, up_b, down, down_b], [tall, slim, slim],
+        [slope_one, normed_one, d_act_two_b, hidden_one_b, hidden_two_b, up, up_b, down, down_b],
+        [tall, slim, shape(4, TALL, units)],
         weight_scratch(units, width, 2)
-        + [kept(2, TALL, units), kept(2, TALL, units, dtype=F32), kept(TALL, width), dma(2), dma(3)],
+        + [kept(2, TALL, units), kept(2, TALL, units, dtype=F32), kept(TALL, width), kept(3, TALL, units), dma(5), dma(4)],
         limit=36, flops=3 * flops, moved=6 * moved,
     )
-    d_normed, part_far = together(d_normed, part_far)
+    ready = d_normed
+    d_normed, far = together(d_normed, far)
     blocks = to_chips(d_normed)
-    own_part, other_part = call(
-        sum_kernel, [shape(ROWS, width, dtype=F32), block], [parts[0], part_up, part_far, part_down], moved=moved
-    )
-    given = lax.ppermute(after(other_part, d_normed), "peer", ACROSS_Z)
-    wide, thin = [], []
+    sums = call(sum_kernel, [shape(ROWS, width, dtype=F32), block, block, block], [near, far], moved=moved)
+    sums = [sums[0]] + [lax.ppermute(sums[apart], "peer", ALONG_Y[apart]) for apart in (1, 2, 3)]
+    wide = []
     for value in (normed_one, normed_two, c_one, cot):
-        wide += [value, swap(after(value, d_normed))]
-    for own, other in ((d_act_one, d_act_one_b), (d_act_two, d_act_two_b), (hidden_one, hidden_one_b), (hidden_two, hidden_two_b)):
-        thin += [own, swap(after(other, d_normed))]
-    step = 1024
+        wide += [value, swap(after(value, ready))]
+    slims = [d_act_one, d_act_two, hidden_one, hidden_two, swap(thin)]
+    step = 2560
     grad_up, grad_down = pl.pallas_call(
         grads_kernel,
         grid=(width // step,),
         out_shape=[shape(units, width)] * 2,
-        in_specs=[pl.BlockSpec((TALL, step), lambda i: (0, i))] * 8 + [HBM] * 8,
+        in_specs=[pl.BlockSpec((TALL, step), lambda i: (0, i))] * 8
+        + [pl.BlockSpec((TALL, units), lambda i: (0, 0))] * 4
+        + [pl.BlockSpec((4, TALL, units), lambda i: (0, 0, 0))],
         out_specs=[pl.BlockSpec((units, step), lambda i: (0, i))] * 2,
-        scratch_shapes=[kept(units, 4 * TALL)] * 2 + [kept(8, TALL, units), dma(8)],
-        compiler_params=pltpu.CompilerParams(vmem_limit_bytes=24 * VMEM_MB),
+        scratch_shapes=[kept(units, 4 * TALL)] * 2,
+        compiler_params=pltpu.CompilerParams(vmem_limit_bytes=40 * VMEM_MB),
         cost_estimate=pl.CostEstimate(flops=4 * flops, bytes_accessed=8 * moved, transcendentals=0),
-    )(*[in_hbm(value) for value in wide], *[in_hbm(value) for value in thin])
+    )(*[in_hbm(value) for value in wide], *[in_hbm(value) for value in slims])
 
     d_one, gain_sum = call(
-        rows_back_kernel, [block, shape(1, width, dtype=F32)], [after(blocks, grad_up), rows_in, landed, gain],
+        last_kernel, [block, shape(1, width, dtype=F32)], [after(blocks, grad_up), rows_in, landed, gain],
         scratch=[kept(ROWS, width, dtype=F32)], moved=moved,
     )
-    second = call(second_out_kernel, [block], [after(own_rows, grad_up), own_part, given], moved=moved // 4)[0]
+    second = call(second_out_kernel, [block], [after(own_rows, grad_up)] + sums, moved=moved // 4)[0]
     second = call(pick_kernel, [block], [second, swap(second), out_index])[0]
     grad_gain = gain_sum + swap(gain_sum)
     return (d_one[None], second[None], grad_up[None], grad_down[None], grad_gain)

time: 211 us -> 205 us (0.972); the launches traced: 207 us -> 204 us
  waiting for transfers between devices: 60 us -> 63.2 us
  local copies, waits for them, and re-layouts: 3.3 us -> 0.74 us
  starting transfers between devices: 67.3 us -> 65 us
    ppermute x4, waiting for transfers between devices: 2.75 us -> 9.14 us  [the longest x3 9.14 us: local(): lax.ppermute(sums[apart], 'peer', ALONG_Y[apart])]
    ppermute x13 -> x10, waiting for transfers between devices: 7.41 us -> 3.17 us  [swap(): return lax.ppermute(value, 'peer', SIBLING)]
    ppermute x13 -> x10, starting transfers between devices: 21.9 us -> 18.5 us  [swap(): return lax.ppermute(value, 'peer', SIBLING)]
    unnamed x24 -> x12, local copies, waits for them, and re-layouts: 2.59 us -> 0.03 us
    pallas_call x16 -> x15, Pallas kernels: 45.1 us -> 47.2 us  [call(): pl.pallas_call(kernel, out_shape=list(outs) + [pltpu.HBM(out.shape, out.d...]
  transfers between devices with their start and end apart: 30 -> 27, of which waited for: 16 -> 13; matrix products, arithmetic and copies ran while one was open for 1% -> 1% of each run, Pallas kernels for 22% -> 23%
where the time goes in v3:
time: 205 us; the launch traced here: 204 us
  starting transfers between devices  65 us (32%)
  waiting for transfers between devices  63.2 us (31%)
  Pallas kernels  57.3 us (28%)
  blocking collectives  16 us (8%)
    pallas_call x15, Pallas kernels, call(): pl.pallas_call(kernel, out_shape=list(outs) + [pltpu.HBM(out.shape, out.d...  47.2 us
    all_to_all x5, waiting for transfers between devices, to_chips(): lax.all_to_all(blocks, 'peer', split_axis=0, concat_axis=0, tiled=True, a...  25.3 us
    all_to_all x5, starting transfers between devices, to_chips(): lax.all_to_all(blocks, 'peer', split_axis=0, concat_axis=0, tiled=True, a...  25 us
    ppermute x10, starting transfers between devices, swap(): return lax.ppermute(value, 'peer', SIBLING)  18.5 us
    all_to_all x1, blocking collectives, to_chips(): lax.all_to_all(blocks, 'peer', split_axis=0, concat_axis=0, tiled=True, a...  16 us
    ppermute x2, waiting for transfers between devices, passed_along(): lax.ppermute(value, 'section', [(source, source + steps) for source in ra...  10.4 us
    pallas_call x1, Pallas kernels, local(): pl.pallas_call(grads_kernel, grid=(width // step,), out_shape=[shape(unit...  10 us
    ppermute x3, waiting for transfers between devices, local(): lax.ppermute(rest, 'peer', pairs)  9.97 us
  transfers between devices with their start and end apart: 27, of which 13 were waited for; matrix products, arithmetic and copies ran while one was open for 1% of the time, Pallas kernels for 23%

profile of v3, /device:TPU:7, one launch (start us, length us, event | category | flops | bytes accessed | tf_op | source)
XLA Modules:
  0.0 204.2 jit_solution(7345071135023326878)
XLA Ops:
  3.3 3.1 %shard_map.101 = (bf16[128,5120]{1,0:T(8,128)(2,1)}, bf16[16,5120]{1,0:T(8,128)(2,1)S(1)}) custom-call(bf16[16,5120]{1,0:T(8,128)(2,1)S(1)} %collective-permute-done.other, s32[16,1]{1,0:T(8,128)S(1)} %add.295.index, bf16[16,5120]{1,0:T(8,128)(2,1)} %bitcast.28, bf16[16,5120]{1,0:T(8,128)(2,1)} %bitcast.42), custom_call_target="tpu_custom_call" | custom-call | bytes 2621440 | tf_op jit(solution)/shard_map/pallas_call | solution.py:375
  7.1 7.5 %all-to-all-start = ((bf16[8,16,5120]{2,1,0:T(8,128)(2,1)}), bf16[8,16,5120]{2,1,0:T(8,128)(2,1)S(1)}, u32[]{:S(2)}, u32[]{:S(2)}) async-start(bf16[8,16,5120]{2,1,0:T(8,128)(2,1)} %bitcast.3), calls=%async_computation | async-start | bytes 2621440 | tf_op jit(solution)/shard_map/all_to_all | solution.py:399
  16.1 2.4 %collective-permute-start.3 = (bf16[16,5120]{1,0:T(8,128)(2,1)S(1)}, bf16[16,5120]{1,0:T(8,128)(2,1)S(1)}, u32[]{:S(2)}, u32[]{:S(2)}) collective-permute-start(bf16[16,5120]{1,0:T(8,128)(2,1)S(1)} %get-tuple-element.68.own), channel_id=1, source_target_pairs={{0,4},{1,5},{2,6},{3,7},{4,0},{5,1},{6,2},{7,3},{8,12},{9,13},{10,... | collective-permute-start | bytes 491528 | tf_op jit(solution)/shard_map/ppermute | solution.py:471
  18.5 3.1 %collective-permute-start.2 = (bf16[16,5120]{1,0:T(8,128)(2,1)S(1)}, bf16[16,5120]{1,0:T(8,128)(2,1)S(1)}, u32[]{:S(2)}, u32[]{:S(2)}) collective-permute-start(bf16[16,5120]{1,0:T(8,128)(2,1)S(1)} %get-tuple-element.68.own), channel_id=1, source_target_pairs={{1,7},{3,1},{5,3},{7,5},{9,15},{11,9},{13,11},{15,13},{17,23},{19,... | collective-permute-start | bytes 491528 | tf_op jit(solution)/shard_map/ppermute | solution.py:471
  21.6 5.7 %collective-permute-done.4.fourth = bf16[16,5120]{1,0:T(8,128)(2,1)S(1)} collective-permute-done((bf16[16,5120]{1,0:T(8,128)(2,1)S(1)}, bf16[16,5120]{1,0:T(8,128)(2,1)S(1)}, u32[]{:S(2)}, u32[]{:S(2)}) %collective-permute-start.4) | collective-permute-done | bytes 163872 | tf_op jit(solution)/shard_map/ppermute | solution.py:471
  27.2 4.3 %collective-permute-done.3.third = bf16[16,5120]{1,0:T(8,128)(2,1)S(1)} collective-permute-done((bf16[16,5120]{1,0:T(8,128)(2,1)S(1)}, bf16[16,5120]{1,0:T(8,128)(2,1)S(1)}, u32[]{:S(2)}, u32[]{:S(2)}) %collective-permute-start.3) | collective-permute-done | bytes 163872 | tf_op jit(solution)/shard_map/ppermute | solution.py:471
  31.6 3.0 %collective-permute-start.7 = (bf16[32,5120]{1,0:T(8,128)(2,1)S(1)}, bf16[32,5120]{1,0:T(8,128)(2,1)S(1)}, u32[]{:S(2)}, u32[]{:S(2)}) collective-permute-start(bf16[32,5120]{1,0:T(8,128)(2,1)S(1)} %get-tuple-element.75.refs_0_), channel_id=1, source_target_pairs={{0,8},{1,9},{2,10},{3,11},{4,12},{5,13},{6,14},{7,15},{8,0},{9,1},... | collective-permute-start | bytes 983048 | tf_op jit(solution)/shard_map/ppermute | solution.py:474
  34.6 8.9 %shard_map.103 = (bf16[128,5120]{1,0:T(8,128)(2,1)}, bf16[128,5120]{1,0:T(8,128)(2,1)}, f32[2,128,432]{2,1,0:T(8,128)}, bf16[128,432]{1,0:T(8,128)(2,1)}, bf16[128,432]{1,0:T(8,128)(2,1)}) custom-call(bf16[128,5120]{1,0:T(8,128)(2,1)S(1)} %bitcast.23, f32[1,5120]{1,0:T(1,128)S(1)} %copy-done.3, bf16[432,5120]{1,0:T(8,128)(2,1)} %bitcast.38, ...), custom_call_target="tpu_custom_call" | custom-call | flops 3397386240 | bytes 15728640 | tf_op jit(solution)/shard_map/pallas_call | solution.py:375
  43.5 4.1 %all-to-all-start.1 = ((bf16[8,16,5120]{2,1,0:T(8,128)(2,1)}), bf16[8,16,5120]{2,1,0:T(8,128)(2,1)S(1)}, u32[]{:S(2)}, u32[]{:S(2)}) async-start(bf16[8,16,5120]{2,1,0:T(8,128)(2,1)} %bitcast.7), calls=%async_computation.1 | async-start | bytes 2621440 | tf_op jit(solution)/shard_map/all_to_all | solution.py:399
  47.7 13.2 %all-to-all-done.1 = bf16[8,16,5120]{2,1,0:T(8,128)(2,1)S(1)} async-done(((bf16[8,16,5120]{2,1,0:T(8,128)(2,1)}), bf16[8,16,5120]{2,1,0:T(8,128)(2,1)S(1)}, u32[]{:S(2)}, u32[]{:S(2)}) %all-to-all-start.1) | async-done | bytes 1310752 | tf_op jit(solution)/shard_map/all_to_all | solution.py:399
  61.7 2.5 %collective-permute-start.8 = (bf16[16,5120]{1,0:T(8,128)(2,1)S(1)}, bf16[16,5120]{1,0:T(8,128)(2,1)S(1)}, u32[]{:S(2)}, u32[]{:S(2)}) collective-permute-start(bf16[16,5120]{1,0:T(8,128)(2,1)S(1)} %shard_map.104), channel_id=1, source_target_pairs={{0,16},{16,32},{32,48},{48,64},{64,80},{80,96},{96,112},{1,17},{17... | collective-permute-start | bytes 491528 | tf_op jit(solution)/shard_map/ppermute | solution.py:428
  64.3 3.5 %collective-permute-done.8.rows.x = bf16[16,5120]{1,0:T(8,128)(2,1)S(1)} collective-permute-done((bf16[16,5120]{1,0:T(8,128)(2,1)S(1)}, bf16[16,5120]{1,0:T(8,128)(2,1)S(1)}, u32[]{:S(2)}, u32[]{:S(2)}) %collective-permute-start.8) | collective-permute-done | bytes 163872 | tf_op jit(solution)/shard_map/ppermute | solution.py:428
  67.8 5.2 %collective-permute-done.9.refs_3_ = bf16[32,5120]{1,0:T(8,128)(2,1)S(1)} collective-permute-done((bf16[32,5120]{1,0:T(8,128)(2,1)S(1)}, bf16[32,5120]{1,0:T(8,128)(2,1)S(1)}, u32[]{:S(2)}, u32[]{:S(2)}) %collective-permute-start.9) | collective-permute-done | bytes 327712 | tf_op jit(solution)/shard_map/ppermute | solution.py:485
  74.1 3.8 %all-to-all-start.2 = ((bf16[8,16,5120]{2,1,0:T(8,128)(2,1)}), bf16[8,16,5120]{2,1,0:T(8,128)(2,1)S(1)}, u32[]{:S(2)}, u32[]{:S(2)}) async-start(bf16[8,16,5120]{2,1,0:T(8,128)(2,1)} %bitcast.9), calls=%async_computation.2 | async-start | bytes 2621440 | tf_op jit(solution)/shard_map/all_to_all | solution.py:399
  78.4 6.7 %shard_map.106 = (bf16[16,5120]{1,0:T(8,128)(2,1)S(1)}, bf16[128,5120]{1,0:T(8,128)(2,1)}, f32[2,128,432]{2,1,0:T(8,128)}) custom-call(bf16[32,5120]{1,0:T(8,128)(2,1)S(1)} %get-tuple-element.75.refs_0_, bf16[32,5120]{1,0:T(8,128)(2,1)S(1)} %get-tuple-element.78.refs_1_, bf16[32,5120]{1,0:T(8,128)(2,1)S(1)} %collective-permute-done.7.refs_2_, ...), custom_call_target="tpu_custom_call" | custom-call | flops 3397386240 | bytes 7864320 | tf_op jit(solution)/shard_map/pallas_call | solution.py:375
  85.1 5.7 %all-to-all-done.2 = bf16[8,16,5120]{2,1,0:T(8,128)(2,1)S(1)} async-done(((bf16[8,16,5120]{2,1,0:T(8,128)(2,1)}), bf16[8,16,5120]{2,1,0:T(8,128)(2,1)S(1)}, u32[]{:S(2)}, u32[]{:S(2)}) %all-to-all-start.2) | async-done | bytes 1310752 | tf_op jit(solution)/shard_map/all_to_all | solution.py:399
  90.8 8.3 %shard_map.107 = (f32[1,5120]{1,0:T(1,128)S(1)}, bf16[16,5120]{1,0:T(8,128)(2,1)S(1)}, bf16[128,5120]{1,0:T(8,128)(2,1)}, bf16[128,5120]{1,0:T(8,128)(2,1)}, bf1...) custom-call(bf16[128,5120]{1,0:T(8,128)(2,1)S(1)} %bitcast.31, ...), custom_call_target="tpu_custom_call" | custom-call | flops 3397386240 | bytes 10485760 | tf_op jit(solution)/shard_map/pallas_call | solution.py:375
  99.1 3.6 %all-to-all-start.3 = ((bf16[8,16,5120]{2,1,0:T(8,128)(2,1)}), bf16[8,16,5120]{2,1,0:T(8,128)(2,1)S(1)}, u32[]{:S(2)}, u32[]{:S(2)}) async-start(bf16[8,16,5120]{2,1,0:T(8,128)(2,1)} %bitcast.11), calls=%async_computation.3 | async-start | bytes 2621440 | tf_op jit(solution)/shard_map/all_to_all | solution.py:399
  102.8 6.7 %shard_map.108 = (bf16[64,5120]{1,0:T(8,128)(2,1)}, bf16[64,5120]{1,0:T(8,128)(2,1)}) custom-call(s32[128,1]{1,0:T(8,128)S(1)} %add.294.to_target, bf16[128,432]{1,0:T(8,128)(2,1)} %get-tuple-element.83.hidden_a.refs_11_, bf16[128,432]{1,0:T(8,128)(2,1)} %get-tuple-element.84.hidden_b.hidden_two_b, bf16[432,5120]{1,0:T(8,128)(2,1)} %bitcast.35, ...), custom_call_target="tpu_custom_call" | custom-call | flops 2264924160 | bytes 7864320 | tf_op jit(solution)/shard_map/pallas_call | solution.py:375
  109.5 6.4 %all-to-all-done.3 = bf16[8,16,5120]{2,1,0:T(8,128)(2,1)S(1)} async-done(((bf16[8,16,5120]{2,1,0:T(8,128)(2,1)}), bf16[8,16,5120]{2,1,0:T(8,128)(2,1)S(1)}, u32[]{:S(2)}, u32[]{:S(2)}) %all-to-all-start.3) | async-done | bytes 1310752 | tf_op jit(solution)/shard_map/all_to_all | solution.py:399
  116.3 2.5 %collective-permute-start.10 = (bf16[16,5120]{1,0:T(8,128)(2,1)S(1)}, bf16[16,5120]{1,0:T(8,128)(2,1)S(1)}, u32[]{:S(2)}, u32[]{:S(2)}) collective-permute-start(bf16[16,5120]{1,0:T(8,128)(2,1)S(1)} %shard_map.109), channel_id=1, source_target_pairs={{16,0},{32,16},{48,32},{64,48},{80,64},{96,80},{112,96},{17,1},{33... | collective-permute-start | bytes 491528 | tf_op jit(solution)/shard_map/ppermute | solution.py:428
  118.8 7.0 %collective-permute-done.10.rows.c = bf16[16,5120]{1,0:T(8,128)(2,1)S(1)} collective-permute-done((bf16[16,5120]{1,0:T(8,128)(2,1)S(1)}, bf16[16,5120]{1,0:T(8,128)(2,1)S(1)}, u32[]{:S(2)}, u32[]{:S(2)}) %collective-permute-start.10) | collective-permute-done | bytes 163872 | tf_op jit(solution)/shard_map/ppermute | solution.py:428
  125.9 16.0 %all_to_all.70 = bf16[8,16,5120]{2,1,0:T(8,128)(2,1)S(1)} all-to-all(bf16[8,16,5120]{2,1,0:T(8,128)(2,1)S(1)} %bitcast.27), channel_id=1, replica_groups={{0,2,4,6,8,10,12,14},{1,3,5,7,9,11,13,15},{16,18,20,22,24,26,28,30},{17..., dimensions={0} | all-to-all | bytes 2621440 | tf_op jit(solution)/shard_map/all_to_all | solution.py:399
  142.2 9.5 %shard_map.111 = (bf16[128,5760]{1,0:T(8,128)(2,1)}, bf16[128,5120]{1,0:T(8,128)(2,1)}, bf16[128,432]{1,0:T(8,128)(2,1)}, bf16[4,128,432]{2,1,0:T(8,128)(2,1)}) custom-call(bf16[128,5120]{1,0:T(8,128)(2,1)S(1)} %bitcast.24, f32[1,5120]{1,0:T(1,128)S(1)} %copy-done.3, f32[1,5120]{1,0:T(1,128)S(1)} %get-tuple-element.91.gain_two, ...), custom_call_target="tpu_custom_call" | custom-call | flops 3397386240 | bytes 15728640 | tf_op jit(solution)/shard_map/pallas_call | solution.py:375
  151.7 14.3 %collective-permute-start.12 = (bf16[128,5120]{1,0:T(8,128)(2,1)}, bf16[128,5120]{1,0:T(8,128)(2,1)}, u32[]{:S(2)}, u32[]{:S(2)}) collective-permute-start(bf16[128,5120]{1,0:T(8,128)(2,1)} %get-tuple-element.99.normed_in.refs_0_), channel_id=1, source_target_pairs={{0,1},{1,0},{2,3},{3,2},{4,5},{5,4},{6,7},{7,6},{8,9},{9,8},{10,11... | collective-permute-start | bytes 3932168 | tf_op jit(solution)/shard_map/ppermute | solution.py:414
  166.6 6.1 %all-to-all-start.5 = ((bf16[8,16,5760]{2,1,0:T(8,128)(2,1)}), bf16[8,16,5760]{2,1,0:T(8,128)(2,1)S(1)}, u32[]{:S(2)}, u32[]{:S(2)}) async-start(bf16[8,16,5760]{2,1,0:T(8,128)(2,1)} %bitcast.15), calls=%async_computation.5 | async-start | bytes 2949120 | tf_op jit(solution)/shard_map/all_to_all | solution.py:399
  173.5 1.7 collective-permute-done.16.refs_12_
  175.2 1.7 collective-permute-start.17
  176.9 2.4 %collective-permute-start.18 = (bf16[16,5120]{1,0:T(8,128)(2,1)S(1)}, bf16[16,5120]{1,0:T(8,128)(2,1)S(1)}, u32[]{:S(2)}, u32[]{:S(2)}) collective-permute-start(bf16[16,5120]{1,0:T(8,128)(2,1)S(1)} %get-tuple-element.119), channel_id=1, source_target_pairs={{0,4},{1,5},{2,6},{3,7},{4,0},{5,1},{6,2},{7,3},{8,12},{9,13},{10,... | collective-permute-start | bytes 491528 | tf_op jit(solution)/shard_map/ppermute | solution.py:529
  180.5 10.0 %shard_map.112 = (bf16[432,5120]{1,0:T(8,128)(2,1)}, bf16[432,5120]{1,0:T(8,128)(2,1)}) custom-call(bf16[128,5120]{1,0:T(8,128)(2,1)} %get-tuple-element.99.normed_in.refs_0_, bf16[128,5120]{1,0:T(8,128)(2,1)} %collective-permute-done.12.refs_1_, bf16[128,5120]{1,0:T(8,128)(2,1)} %get-tuple-element.101.refs_2_, ...), custom_call_target="tpu_custom_call" | custom-call | flops 4529848320 | bytes 20971520 | tf_op jit(solution)/shard_map/pallas_call | solution.py:535
  190.5 5.2 %collective-permute-done.17.second = bf16[16,5120]{1,0:T(8,128)(2,1)S(1)} collective-permute-done((bf16[16,5120]{1,0:T(8,128)(2,1)S(1)}, bf16[16,5120]{1,0:T(8,128)(2,1)S(1)}, u32[]{:S(2)}, u32[]{:S(2)}) %collective-permute-start.17) | collective-permute-done | bytes 163872 | tf_op jit(solution)/shard_map/ppermute | solution.py:529
  195.7 3.9 %collective-permute-done.18.third = bf16[16,5120]{1,0:T(8,128)(2,1)S(1)} collective-permute-done((bf16[16,5120]{1,0:T(8,128)(2,1)S(1)}, bf16[16,5120]{1,0:T(8,128)(2,1)S(1)}, u32[]{:S(2)}, u32[]{:S(2)}) %collective-permute-start.18) | collective-permute-done | bytes 163872 | tf_op jit(solution)/shard_map/ppermute | solution.py:529
  (76 shorter events, 15.6 us)
Async XLA Ops:
  0.6 60.8 %copy-start = (s32[8,16]{1,0:T(8,128)S(1)}, s32[8,16]{1,0:T(8,128)}, u32[]{:S(2)}) copy-start(s32[8,16]{1,0:T(8,128)} %param.11) | copy-start | bytes 1540
  0.6 2.0 collective-permute-start
  2.6 32.0 %collective-permute-start.5 = (bf16[432,5120]{1,0:T(8,128)(2,1)}, bf16[432,5120]{1,0:T(8,128)(2,1)}, u32[]{:S(2)}, u32[]{:S(2)}) collective-permute-start(bf16[432,5120]{1,0:T(8,128)(2,1)} %bitcast.37), channel_id=1, source_target_pairs={{0,1},{1,0},{2,3},{3,2},{4,5},{5,4},{6,7},{7,6},{8,9},{9,8},{10,11... | collective-permute-start | bytes 13271048 | tf_op jit(solution)/shard_map/ppermute | solution.py:414
  3.0 31.6 %collective-permute-start.6 = (bf16[432,5120]{1,0:T(8,128)(2,1)}, bf16[432,5120]{1,0:T(8,128)(2,1)}, u32[]{:S(2)}, u32[]{:S(2)}) collective-permute-start(bf16[432,5120]{1,0:T(8,128)(2,1)} %bitcast.32), channel_id=1, source_target_pairs={{0,1},{1,0},{2,3},{3,2},{4,5},{5,4},{6,7},{7,6},{8,9},{9,8},{10,11... | collective-permute-start | bytes 13271048 | tf_op jit(solution)/shard_map/ppermute | solution.py:414
  6.4 0.7 collective-permute-start.1
  7.1 27.5 %copy-start.3 = (f32[1,5120]{1,0:T(1,128)S(1)}, f32[1,5120]{1,0:T(1,128)}, u32[]{:S(2)}) copy-start(f32[1,5120]{1,0:T(1,128)} %gain.9) | copy-start | bytes 61444
  7.1 24.5 %all-to-all-start = ((bf16[8,16,5120]{2,1,0:T(8,128)(2,1)}), bf16[8,16,5120]{2,1,0:T(8,128)(2,1)S(1)}, u32[]{:S(2)}, u32[]{:S(2)}) async-start(bf16[8,16,5120]{2,1,0:T(8,128)(2,1)} %bitcast.3), calls=%async_computation | async-start | bytes 2621440 | tf_op jit(solution)/shard_map/all_to_all | solution.py:399
  14.6 12.6 %collective-permute-start.4 = (bf16[16,5120]{1,0:T(8,128)(2,1)S(1)}, bf16[16,5120]{1,0:T(8,128)(2,1)S(1)}, u32[]{:S(2)}, u32[]{:S(2)}) collective-permute-start(bf16[16,5120]{1,0:T(8,128)(2,1)S(1)} %get-tuple-element.68.own), channel_id=1, source_target_pairs={{0,2},{1,3},{2,4},{3,5},{4,6},{5,7},{6,0},{7,1},{8,10},{9,11},{10,... | collective-permute-start | bytes 491528 | tf_op jit(solution)/shard_map/ppermute | solution.py:471
  16.1 15.5 %collective-permute-start.3 = (bf16[16,5120]{1,0:T(8,128)(2,1)S(1)}, bf16[16,5120]{1,0:T(8,128)(2,1)S(1)}, u32[]{:S(2)}, u32[]{:S(2)}) collective-permute-start(bf16[16,5120]{1,0:T(8,128)(2,1)S(1)} %get-tuple-element.68.own), channel_id=1, source_target_pairs={{0,4},{1,5},{2,6},{3,7},{4,0},{5,1},{6,2},{7,3},{8,12},{9,13},{10,... | collective-permute-start | bytes 491528 | tf_op jit(solution)/shard_map/ppermute | solution.py:471
  18.5 13.1 %collective-permute-start.2 = (bf16[16,5120]{1,0:T(8,128)(2,1)S(1)}, bf16[16,5120]{1,0:T(8,128)(2,1)S(1)}, u32[]{:S(2)}, u32[]{:S(2)}) collective-permute-start(bf16[16,5120]{1,0:T(8,128)(2,1)S(1)} %get-tuple-element.68.own), channel_id=1, source_target_pairs={{1,7},{3,1},{5,3},{7,5},{9,15},{11,9},{13,11},{15,13},{17,23},{19,... | collective-permute-start | bytes 491528 | tf_op jit(solution)/shard_map/ppermute | solution.py:471
  31.6 11.9 %collective-permute-start.7 = (bf16[32,5120]{1,0:T(8,128)(2,1)S(1)}, bf16[32,5120]{1,0:T(8,128)(2,1)S(1)}, u32[]{:S(2)}, u32[]{:S(2)}) collective-permute-start(bf16[32,5120]{1,0:T(8,128)(2,1)S(1)} %get-tuple-element.75.refs_0_), channel_id=1, source_target_pairs={{0,8},{1,9},{2,10},{3,11},{4,12},{5,13},{6,14},{7,15},{8,0},{9,1},... | collective-permute-start | bytes 983048 | tf_op jit(solution)/shard_map/ppermute | solution.py:474
  43.5 17.3 %copy-start.1 = (bf16[1,16,5120]{2,1,0:T(8,128)(2,1)S(1)}, bf16[1,16,5120]{2,1,0:T(8,128)(2,1)}, u32[]{:S(2)}) copy-start(bf16[1,16,5120]{2,1,0:T(8,128)(2,1)} %param.6) | copy-start | bytes 491524
  43.5 17.3 %all-to-all-start.1 = ((bf16[8,16,5120]{2,1,0:T(8,128)(2,1)}), bf16[8,16,5120]{2,1,0:T(8,128)(2,1)S(1)}, u32[]{:S(2)}, u32[]{:S(2)}) async-start(bf16[8,16,5120]{2,1,0:T(8,128)(2,1)} %bitcast.7), calls=%async_computation.1 | async-start | bytes 2621440 | tf_op jit(solution)/shard_map/all_to_all | solution.py:399
  61.0 11.9 %collective-permute-start.9 = (bf16[32,5120]{1,0:T(8,128)(2,1)S(1)}, bf16[32,5120]{1,0:T(8,128)(2,1)S(1)}, u32[]{:S(2)}, u32[]{:S(2)}) collective-permute-start(bf16[32,5120]{1,0:T(8,128)(2,1)S(1)} %get-tuple-element.78.refs_1_), channel_id=1, source_target_pairs={{0,8},{1,9},{2,10},{3,11},{4,12},{5,13},{6,14},{7,15},{8,0},{9,1},... | collective-permute-start | bytes 983048 | tf_op jit(solution)/shard_map/ppermute | solution.py:485
  61.7 6.1 %collective-permute-start.8 = (bf16[16,5120]{1,0:T(8,128)(2,1)S(1)}, bf16[16,5120]{1,0:T(8,128)(2,1)S(1)}, u32[]{:S(2)}, u32[]{:S(2)}) collective-permute-start(bf16[16,5120]{1,0:T(8,128)(2,1)S(1)} %shard_map.104), channel_id=1, source_target_pairs={{0,16},{16,32},{32,48},{48,64},{64,80},{80,96},{96,112},{1,17},{17... | collective-permute-start | bytes 491528 | tf_op jit(solution)/shard_map/ppermute | solution.py:428
  74.1 16.8 %all-to-all-start.2 = ((bf16[8,16,5120]{2,1,0:T(8,128)(2,1)}), bf16[8,16,5120]{2,1,0:T(8,128)(2,1)S(1)}, u32[]{:S(2)}, u32[]{:S(2)}) async-start(bf16[8,16,5120]{2,1,0:T(8,128)(2,1)} %bitcast.9), calls=%async_computation.2 | async-start | bytes 2621440 | tf_op jit(solution)/shard_map/all_to_all | solution.py:399
  99.1 16.8 %all-to-all-start.3 = ((bf16[8,16,5120]{2,1,0:T(8,128)(2,1)}), bf16[8,16,5120]{2,1,0:T(8,128)(2,1)S(1)}, u32[]{:S(2)}, u32[]{:S(2)}) async-start(bf16[8,16,5120]{2,1,0:T(8,128)(2,1)} %bitcast.11), calls=%async_computation.3 | async-start | bytes 2621440 | tf_op jit(solution)/shard_map/all_to_all | solution.py:399
  116.3 9.5 %collective-permute-start.10 = (bf16[16,5120]{1,0:T(8,128)(2,1)S(1)}, bf16[16,5120]{1,0:T(8,128)(2,1)S(1)}, u32[]{:S(2)}, u32[]{:S(2)}) collective-permute-start(bf16[16,5120]{1,0:T(8,128)(2,1)S(1)} %shard_map.109), channel_id=1, source_target_pairs={{16,0},{32,16},{48,32},{64,48},{80,64},{96,80},{112,96},{17,1},{33... | collective-permute-start | bytes 491528 | tf_op jit(solution)/shard_map/ppermute | solution.py:428
  125.9 16.0 %copy-start.4 = (bf16[64,5120]{1,0:T(8,128)(2,1)S(1)}, bf16[64,5120]{1,0:T(8,128)(2,1)}, u32[]{:S(2)}) copy-start(bf16[64,5120]{1,0:T(8,128)(2,1)} %get-tuple-element.97) | copy-start | bytes 1966084
  141.9 24.7 %collective-permute-start.11 = (bf16[64,5120]{1,0:T(8,128)(2,1)S(1)}, bf16[64,5120]{1,0:T(8,128)(2,1)S(1)}, u32[]{:S(2)}, u32[]{:S(2)}) collective-permute-start(bf16[64,5120]{1,0:T(8,128)(2,1)S(1)} %copy-done.4), channel_id=1, source_target_pairs={{0,8},{1,9},{2,10},{3,11},{4,12},{5,13},{6,14},{7,15},{8,0},{9,1},... | collective-permute-start | bytes 1966088 | tf_op jit(solution)/shard_map/ppermute | solution.py:516
  151.7 25.2 %collective-permute-start.12 = (bf16[128,5120]{1,0:T(8,128)(2,1)}, bf16[128,5120]{1,0:T(8,128)(2,1)}, u32[]{:S(2)}, u32[]{:S(2)}) collective-permute-start(bf16[128,5120]{1,0:T(8,128)(2,1)} %get-tuple-element.99.normed_in.refs_0_), channel_id=1, source_target_pairs={{0,1},{1,0},{2,3},{3,2},{4,5},{5,4},{6,7},{7,6},{8,9},{9,8},{10,11... | collective-permute-start | bytes 3932168 | tf_op jit(solution)/shard_map/ppermute | solution.py:414
  166.0 13.3 %collective-permute-start.13 = (bf16[128,5120]{1,0:T(8,128)(2,1)}, bf16[128,5120]{1,0:T(8,128)(2,1)}, u32[]{:S(2)}, u32[]{:S(2)}) collective-permute-start(bf16[128,5120]{1,0:T(8,128)(2,1)} %get-tuple-element.101.refs_2_), channel_id=1, source_target_pairs={{0,1},{1,0},{2,3},{3,2},{4,5},{5,4},{6,7},{7,6},{8,9},{9,8},{10,11... | collective-permute-start | bytes 3932168 | tf_op jit(solution)/shard_map/ppermute | solution.py:414
  166.1 14.4 %collective-permute-start.15 = (bf16[128,5120]{1,0:T(8,128)(2,1)}, bf16[128,5120]{1,0:T(8,128)(2,1)}, u32[]{:S(2)}, u32[]{:S(2)}) collective-permute-start(bf16[128,5120]{1,0:T(8,128)(2,1)} %get-tuple-element.105.refs_6_), channel_id=1, source_target_pairs={{0,1},{1,0},{2,3},{3,2},{4,5},{5,4},{6,7},{7,6},{8,9},{9,8},{10,11... | collective-permute-start | bytes 3932168 | tf_op jit(solution)/shard_map/ppermute | solution.py:414
  166.5 14.0 %collective-permute-start.14 = (bf16[128,5120]{1,0:T(8,128)(2,1)}, bf16[128,5120]{1,0:T(8,128)(2,1)}, u32[]{:S(2)}, u32[]{:S(2)}) collective-permute-start(bf16[128,5120]{1,0:T(8,128)(2,1)} %get-tuple-element.103.refs_4_), channel_id=1, source_target_pairs={{0,1},{1,0},{2,3},{3,2},{4,5},{5,4},{6,7},{7,6},{8,9},{9,8},{10,11... | collective-permute-start | bytes 3932168 | tf_op jit(solution)/shard_map/ppermute | solution.py:414
  166.6 6.8 %copy-start.2 = (bf16[64,5120]{1,0:T(8,128)(2,1)S(1)}, bf16[64,5120]{1,0:T(8,128)(2,1)}, u32[]{:S(2)}) copy-start(bf16[64,5120]{1,0:T(8,128)(2,1)} %get-tuple-element.115.near) | copy-start | bytes 1966084
  166.6 34.8 %all-to-all-start.5 = ((bf16[8,16,5760]{2,1,0:T(8,128)(2,1)}), bf16[8,16,5760]{2,1,0:T(8,128)(2,1)S(1)}, u32[]{:S(2)}, u32[]{:S(2)}) async-start(bf16[8,16,5760]{2,1,0:T(8,128)(2,1)} %bitcast.15), calls=%async_computation.5 | async-start | bytes 2949120 | tf_op jit(solution)/shard_map/all_to_all | solution.py:399
  172.7 2.5 %collective-permute-start.16 = (bf16[4,128,432]{2,1,0:T(8,128)(2,1)}, bf16[4,128,432]{2,1,0:T(8,128)(2,1)S(1)}, u32[]{:S(2)}, u32[]{:S(2)}) collective-permute-start(bf16[4,128,432]{2,1,0:T(8,128)(2,1)} %get-tuple-element.109), channel_id=1, source_target_pairs={{0,1},{1,0},{2,3},{3,2},{4,5},{5,4},{6,7},{7,6},{8,9},{9,8},{10,11... | collective-permute-start | bytes 1327112 | tf_op jit(solution)/shard_map/ppermute | solution.py:414
  175.2 20.5 %collective-permute-start.17 = (bf16[16,5120]{1,0:T(8,128)(2,1)S(1)}, bf16[16,5120]{1,0:T(8,128)(2,1)S(1)}, u32[]{:S(2)}, u32[]{:S(2)}) collective-permute-start(bf16[16,5120]{1,0:T(8,128)(2,1)S(1)} %get-tuple-element.118), channel_id=1, source_target_pairs={{0,2},{1,3},{2,4},{3,5},{4,6},{5,7},{6,0},{7,1},{8,10},{9,11},{10,... | collective-permute-start | bytes 491528 | tf_op jit(solution)/shard_map/ppermute | solution.py:529
  176.9 22.8 %collective-permute-start.18 = (bf16[16,5120]{1,0:T(8,128)(2,1)S(1)}, bf16[16,5120]{1,0:T(8,128)(2,1)S(1)}, u32[]{:S(2)}, u32[]{:S(2)}) collective-permute-start(bf16[16,5120]{1,0:T(8,128)(2,1)S(1)} %get-tuple-element.119), channel_id=1, source_target_pairs={{0,4},{1,5},{2,6},{3,7},{4,0},{5,1},{6,2},{7,3},{8,12},{9,13},{10,... | collective-permute-start | bytes 491528 | tf_op jit(solution)/shard_map/ppermute | solution.py:529
  179.3 20.4 %collective-permute-start.19 = (bf16[16,5120]{1,0:T(8,128)(2,1)S(1)}, bf16[16,5120]{1,0:T(8,128)(2,1)S(1)}, u32[]{:S(2)}, u32[]{:S(2)}) collective-permute-start(bf16[16,5120]{1,0:T(8,128)(2,1)S(1)} %get-tuple-element.120), channel_id=1, source_target_pairs={{0,6},{1,7},{2,0},{3,1},{4,2},{5,3},{6,4},{7,5},{8,14},{9,15},{10,... | collective-permute-start | bytes 491528 | tf_op jit(solution)/shard_map/ppermute | solution.py:529
  199.8 2.7 %collective-permute-start.20 = (bf16[16,5120]{1,0:T(8,128)(2,1)S(1)}, bf16[16,5120]{1,0:T(8,128)(2,1)S(1)}, u32[]{:S(2)}, u32[]{:S(2)}) collective-permute-start(bf16[16,5120]{1,0:T(8,128)(2,1)S(1)} %shard_map.115.refs_0_), channel_id=1, source_target_pairs={{0,1},{1,0},{2,3},{3,2},{4,5},{5,4},{6,7},{7,6},{8,9},{9,8},{10,11... | collective-permute-start | bytes 491528 | tf_op jit(solution)/shard_map/ppermute | solution.py:414
  202.4 1.2 collective-permute-start.21
  (1 other events, 5.3 us)

commit v4 on v3

--- a/solution.py
+++ b/solution.py
@@ -110,8 +110,8 @@
 
 def forward_kernel(
     x, gain, up_a, up_b, down_a, down_b,
-    proj, normed_out, slope_out, hidden_a_out, hidden_b_out,
-    wu, wd, su, sd, normed, slope, hidden, so,
+    proj_out, normed_out, slope_out, hidden_a_out, hidden_b_out,
+    wu, wd, su, sd, proj, normed, slope, hidden, so,
 ):
     ups = Weights((up_a, up_b), wu, su)
     downs = Weights((down_a, down_b), wd, sd)
@@ -129,6 +129,7 @@
     for at, cols in enumerate(chunks(x.shape[1])):
         downs.wait(at)
         proj[:, cols] = (dot_nn(hidden[0], wd[0, :, cols]) + dot_nn(hidden[1], wd[1, :, cols])).astype(BF)
+        stores.add(proj.at[:, cols], proj_out.at[:, cols])
     stores.finish()
 
 
@@ -140,24 +141,26 @@
         out[:, cols] = dot_nn(choose, rows).astype(BF)
 
 
-def join_kernel(own, even, odd, third, fourth, first_pair, second_pair):
+def join_kernel(fourth, third, odd, even, own, first_pair, second_pair):
     first_pair[:ROWS, :] = own[...]
     first_pair[ROWS:, :] = even[...] + odd[...]
     second_pair[:ROWS, :] = third[...]
     second_pair[ROWS:, :] = fourth[...]
 
 
-def prepare_kernel(other, index, rows, own_in, wide, share, own, sem, sems):
-    fetch = pltpu.make_async_copy(own_in, own, sem)
-    fetch.start()
-    copies = []
-    for at in range(CHIPS):
-        copies.append(pltpu.make_async_copy(rows, wide.at[at * ROWS : (at + 1) * ROWS, :], sems.at[at]))
-        copies[-1].start()
-    fetch.wait()
-    pick_kernel(own, other, index, share)
+def finish_kernel(own, other, index, gain_own, gain_other, out, gain_out):
+    pick_kernel(own, other, index, out)
+    gain_out[...] = gain_own[...] + gain_other[...]
+
+
+def prepare_kernel(other, index, rows_in, own_in, wide, share, held, sems):
+    copies = [pltpu.make_async_copy(ref, held.at[at], sems.at[at]) for at, ref in enumerate((rows_in, own_in))]
+    for copy in copies:
+        copy.start()
     for copy in copies:
         copy.wait()
+    pick_kernel(held.at[1], other, index, share)
+    spread_kernel(held.at[0], wide)
 
 
 def spread_kernel(rows, out):
@@ -192,8 +195,8 @@
 
 def second_kernel(
     x, gain, own_target, d_hidden_in, up_a, up_b,
-    gain_term, own_rows, dn, normed_out, d_act_a_out, d_act_b_out, hidden_a_out, hidden_b_out,
-    wu, su, normed, d_act, hidden, d_hidden, sh, so,
+    gain_term, own_rows_out, dn_out, normed_out, d_act_a_out, d_act_b_out, hidden_a_out, hidden_b_out,
+    wu, su, own_rows, dn, normed, d_act, hidden, d_hidden, sh, so,
 ):
     ups = Weights((up_a, up_b), wu, su)
     ups.start_all()
@@ -213,10 +216,13 @@
     stores.add(hidden.at[1], hidden_b_out)
     own = one_hot(own_target[...], TALL)
     for cols in chunks(x.shape[1]):
+        own_rows[:, cols] = dot_nn(own, x[:, cols]).astype(BF)
+    stores.add(own_rows, own_rows_out)
+    for cols in chunks(x.shape[1]):
         term = dot_nn(d_act[0], wu[0, :, cols]) + dot_nn(d_act[1], wu[1, :, cols])
         dn[:, cols] = term.astype(BF)
+        stores.add(dn.at[:, cols], dn_out.at[:, cols])
         gain_term[:, cols] = jnp.sum(term * normed[:, cols].astype(F32), axis=0, keepdims=True) / gain[:, cols]
-        own_rows[:, cols] = dot_nn(own, x[:, cols]).astype(BF)
     stores.finish()
 
 
@@ -258,8 +264,8 @@
 
 def first_back_kernel(
     c, gain, gain_two, slope_in, normed_in, d_act_two_b, hidden_one_b, hidden_two_b, up_a, up_b, down_a, down_b,
-    dn, c_out, d_act_a_out, thin_out,
-    wu, wd, su, sd, d_act, slope, normed, thin, sh, so,
+    dn_out, c_out, d_act_a_out, thin_out,
+    wu, wd, su, sd, dn, d_act, slope, normed, thin, sh, so,
 ):
     width = c.shape[1]
     downs = Weights((down_a, down_b), wd, sd)
@@ -292,6 +298,7 @@
         ups.wait(at)
         term = dot_nn(d_act[0], wu[0, :, cols]) + dot_nn(d_act[1], wu[1, :, cols])
         dn[:, cols] = term.astype(BF)
+        stores.add(dn.at[:, cols], dn_out.at[:, cols])
         product = jnp.sum(term * normed[:, cols].astype(F32), axis=0, keepdims=True)
         gain_pieces.append(product / gain[:, cols] + gain_two[:, cols])
     line = jnp.concatenate(gain_pieces, axis=1)
@@ -301,6 +308,7 @@
     both = jnp.concatenate([high, grid - high], axis=0).astype(BF)
     for block in range(CHIPS):
         dn[block * ROWS : (block + 1) * ROWS, width:] = both
+    stores.add(dn.at[:, width:], dn_out.at[:, width:])
     stores.finish()
 
 
@@ -462,20 +470,21 @@
 
     wide_rows, cot_half = call(
         prepare_kernel, [in_vmem(TALL, width), block], [cot_b, cot_index], [rows_in, cot_in], [],
-        [kept(ROWS, width), pltpu.SemaphoreType.DMA, dma(CHIPS)], limit=8, moved=moved,
+        [kept(2, ROWS, width), dma(2)], limit=8, moved=moved,
     )
     even = lax.ppermute(cot_half, "peer", ALONG_Y[3][0::2])
     wide_rows, even = together(wide_rows, even)
     x_one = to_chips(wide_rows)
     rest = after(cot_half, even)
-    cot_y = [lax.ppermute(rest, "peer", pairs) for pairs in (ALONG_Y[3][1::2], ALONG_Y[2], ALONG_Y[1])]
-    cot_a, cot_b = call(join_kernel, [shape(2 * ROWS, width)] * 2, [cot_half, even] + cot_y, moved=moved)
+    fourth, opposite = lax.ppermute(rest, "peer", ALONG_Y[1]), lax.ppermute(rest, "peer", ALONG_Y[2])
+    odd = lax.ppermute(rest, "peer", ALONG_Y[3][1::2])
+    cot_a, cot_b = call(join_kernel, [shape(2 * ROWS, width)] * 2, [fourth, opposite, odd, even, cot_half], moved=moved)
     x_one, cot_a, cot_b = together(x_one, cot_a, cot_b)
     cot_za = lax.ppermute(cot_a, "peer", ACROSS_Z)
     proj, normed_one, slope_one, hidden_one, hidden_one_b = call(
-        forward_kernel, [in_vmem(TALL, width)], [x_one, gain], [up, up_b, down, down_b], [tall, pair_f32, slim, slim],
+        forward_kernel, [], [x_one, gain], [up, up_b, down, down_b], [tall, tall, pair_f32, slim, slim],
         weight_scratch(units, width, 2)
-        + [kept(TALL, width), kept(2, TALL, units, dtype=F32), kept(2, TALL, units), dma(steps + 3)],
+        + [kept(TALL, width), kept(TALL, width), kept(2, TALL, units, dtype=F32), kept(2, TALL, units), dma(2 * steps + 3)],
         limit=36, flops=3 * flops, moved=6 * moved,
     )
     proj, cot_za = together(proj, cot_za)
@@ -492,11 +501,11 @@
         limit=20, flops=3 * flops, moved=3 * moved,
     )
     gain_two, own_rows, d_normed, normed_two, d_act_two, d_act_two_b, hidden_two, hidden_two_b = call(
-        second_kernel, [shape(1, width, dtype=F32), block, in_vmem(TALL, width)],
-        [x_two, gain, own_target], [d_hidden, up, up_b], [tall, slim, slim, slim, slim],
+        second_kernel, [shape(1, width, dtype=F32)],
+        [x_two, gain, own_target], [d_hidden, up, up_b], [block, tall, tall, slim, slim, slim, slim],
         weight_scratch(units, width, 1)
-        + [kept(TALL, width), kept(2, TALL, units), kept(2, TALL, units), kept(2, TALL, units, dtype=F32),
-           pltpu.SemaphoreType.DMA, dma(steps + 4)],
+        + [kept(ROWS, width), kept(TALL, width), kept(TALL, width), kept(2, TALL, units), kept(2, TALL, units), kept(2, TALL, units, dtype=F32),
+           pltpu.SemaphoreType.DMA, dma(2 * steps + 5)],
         limit=28, flops=3 * flops, moved=4 * moved,
     )
     blocks = to_chips(d_normed)
@@ -515,11 +524,11 @@
     near, far, c_all = together(*parts, c_all)
     far = lax.ppermute(far, "peer", ACROSS_Z)
     d_normed, c_one, d_act_one, thin = call(
-        first_back_kernel, [in_vmem(TALL, width + width // 8)], [c_all, gain, gain_two],
+        first_back_kernel, [], [c_all, gain, gain_two],
         [slope_one, normed_one, d_act_two_b, hidden_one_b, hidden_two_b, up, up_b, down, down_b],
-        [tall, slim, shape(4, TALL, units)],
+        [shape(TALL, width + width // 8), tall, slim, shape(4, TALL, units)],
         weight_scratch(units, width, 2)
-        + [kept(2, TALL, units), kept(2, TALL, units, dtype=F32), kept(TALL, width), kept(3, TALL, units), dma(5), dma(4)],
+        + [kept(TALL, width + width // 8), kept(2, TALL, units), kept(2, TALL, units, dtype=F32), kept(TALL, width), kept(3, TALL, units), dma(5), dma(steps + 5)],
         limit=36, flops=3 * flops, moved=6 * moved,
     )
     ready = d_normed
@@ -549,9 +558,11 @@
         last_kernel, [block, shape(1, width, dtype=F32)], [after(blocks, grad_up), rows_in, landed, gain],
         scratch=[kept(ROWS, width, dtype=F32)], moved=moved,
     )
-    second = call(second_out_kernel, [block], [after(own_rows, grad_up)] + sums, moved=moved // 4)[0]
-    second = call(pick_kernel, [block], [second, swap(second), out_index])[0]
-    grad_gain = gain_sum + swap(gain_sum)
+    second = call(second_out_kernel, [block], [after(own_rows, d_one)] + sums, moved=moved // 4)[0]
+    second, grad_gain = call(
+        finish_kernel, [block, shape(1, width, dtype=F32)],
+        [second, swap(second), out_index, gain_sum, swap(gain_sum)],
+    )
     return (d_one[None], second[None], grad_up[None], grad_down[None], grad_gain)
 
 

time: 205 us -> 202 us (0.985)
    ppermute x3, waiting for transfers between devices: 9.14 us -> 3.98 us  [local(): lax.ppermute(sums[apart], 'peer', ALONG_Y[apart])]
    all_to_all x5, waiting for transfers between devices: 25.3 us -> 29.1 us  [to_chips(): lax.all_to_all(blocks, 'peer', split_axis=0, concat_axis=0, tiled=True, a...]
where the time goes in v4:
time: 202 us
  starting transfers between devices  64.9 us (32%)
  waiting for transfers between devices  62.4 us (31%)
  Pallas kernels  56.2 us (28%)
  blocking collectives  15.9 us (8%)
    pallas_call x15, Pallas kernels, call(): pl.pallas_call(kernel, out_shape=list(outs) + [pltpu.HBM(out.shape, out.d...  46.2 us
    all_to_all x5, waiting for transfers between devices, to_chips(): lax.all_to_all(blocks, 'peer', split_axis=0, concat_axis=0, tiled=True, a...  29.1 us
    all_to_all x5, starting transfers between devices, to_chips(): lax.all_to_all(blocks, 'peer', split_axis=0, concat_axis=0, tiled=True, a...  25 us
    ppermute x10, starting transfers between devices, swap(): return lax.ppermute(value, 'peer', SIBLING)  18.3 us
    all_to_all x1, blocking collectives, to_chips(): lax.all_to_all(blocks, 'peer', split_axis=0, concat_axis=0, tiled=True, a...  15.9 us
    ppermute x2, waiting for transfers between devices, passed_along(): lax.ppermute(value, 'section', [(source, source + steps) for source in ra...  10.8 us
    pallas_call x1, Pallas kernels, local(): pl.pallas_call(grads_kernel, grid=(width // step,), out_shape=[shape(unit...  10 us
    ppermute x1, waiting for transfers between devices, local(): lax.ppermute(rest, 'peer', ALONG_Y[1])  5.67 us
  transfers between devices with their start and end apart: 27, of which 13 were waited for; matrix products, arithmetic and copies ran while one was open for 1% of the time, Pallas kernels for 23%

profile of v4, /device:TPU:7, one launch (start us, length us, event | category | flops | bytes accessed | tf_op | source)
XLA Modules:
  0.0 201.7 jit_solution(17235858622081652575)
XLA Ops:
  3.3 2.3 %shard_map.101 = (bf16[128,5120]{1,0:T(8,128)(2,1)}, bf16[16,5120]{1,0:T(8,128)(2,1)S(1)}) custom-call(bf16[16,5120]{1,0:T(8,128)(2,1)S(1)} %collective-permute-done.other, s32[16,1]{1,0:T(8,128)S(1)} %add.291.index, bf16[16,5120]{1,0:T(8,128)(2,1)} %bitcast.28, bf16[16,5120]{1,0:T(8,128)(2,1)} %bitcast.45), custom_call_target="tpu_custom_call" | custom-call | bytes 2621440 | tf_op jit(solution)/shard_map/pallas_call | solution.py:383
  6.3 7.5 %all-to-all-start = ((bf16[8,16,5120]{2,1,0:T(8,128)(2,1)}), bf16[8,16,5120]{2,1,0:T(8,128)(2,1)S(1)}, u32[]{:S(2)}, u32[]{:S(2)}) async-start(bf16[8,16,5120]{2,1,0:T(8,128)(2,1)} %bitcast.3), calls=%async_computation | async-start | bytes 2621440 | tf_op jit(solution)/shard_map/all_to_all | solution.py:407
  15.3 2.4 %collective-permute-start.3 = (bf16[16,5120]{1,0:T(8,128)(2,1)S(1)}, bf16[16,5120]{1,0:T(8,128)(2,1)S(1)}, u32[]{:S(2)}, u32[]{:S(2)}) collective-permute-start(bf16[16,5120]{1,0:T(8,128)(2,1)S(1)} %get-tuple-element.70.own), channel_id=1, source_target_pairs={{0,4},{1,5},{2,6},{3,7},{4,0},{5,1},{6,2},{7,3},{8,12},{9,13},{10,... | collective-permute-start | bytes 491528 | tf_op jit(solution)/shard_map/ppermute | solution.py:479
  17.7 3.1 %collective-permute-start.4 = (bf16[16,5120]{1,0:T(8,128)(2,1)S(1)}, bf16[16,5120]{1,0:T(8,128)(2,1)S(1)}, u32[]{:S(2)}, u32[]{:S(2)}) collective-permute-start(bf16[16,5120]{1,0:T(8,128)(2,1)S(1)} %get-tuple-element.70.own), channel_id=1, source_target_pairs={{1,7},{3,1},{5,3},{7,5},{9,15},{11,9},{13,11},{15,13},{17,23},{19,... | collective-permute-start | bytes 491528 | tf_op jit(solution)/shard_map/ppermute | solution.py:480
  20.7 5.7 %collective-permute-done.2.fourth = bf16[16,5120]{1,0:T(8,128)(2,1)S(1)} collective-permute-done((bf16[16,5120]{1,0:T(8,128)(2,1)S(1)}, bf16[16,5120]{1,0:T(8,128)(2,1)S(1)}, u32[]{:S(2)}, u32[]{:S(2)}) %collective-permute-start.2) | collective-permute-done | bytes 163872 | tf_op jit(solution)/shard_map/ppermute | solution.py:479
  26.4 4.3 %collective-permute-done.3.third = bf16[16,5120]{1,0:T(8,128)(2,1)S(1)} collective-permute-done((bf16[16,5120]{1,0:T(8,128)(2,1)S(1)}, bf16[16,5120]{1,0:T(8,128)(2,1)S(1)}, u32[]{:S(2)}, u32[]{:S(2)}) %collective-permute-start.3) | collective-permute-done | bytes 163872 | tf_op jit(solution)/shard_map/ppermute | solution.py:479
  30.8 3.0 %collective-permute-start.7 = (bf16[32,5120]{1,0:T(8,128)(2,1)S(1)}, bf16[32,5120]{1,0:T(8,128)(2,1)S(1)}, u32[]{:S(2)}, u32[]{:S(2)}) collective-permute-start(bf16[32,5120]{1,0:T(8,128)(2,1)S(1)} %get-tuple-element.77.refs_0_), channel_id=1, source_target_pairs={{0,8},{1,9},{2,10},{3,11},{4,12},{5,13},{6,14},{7,15},{8,0},{9,1},... | collective-permute-start | bytes 983048 | tf_op jit(solution)/shard_map/ppermute | solution.py:483
  33.8 8.6 %shard_map.103 = (bf16[128,5120]{1,0:T(8,128)(2,1)}, bf16[128,5120]{1,0:T(8,128)(2,1)}, f32[2,128,432]{2,1,0:T(8,128)}, bf16[128,432]{1,0:T(8,128)(2,1)}, bf16[128,432]{1,0:T(8,128)(2,1)}) custom-call(bf16[128,5120]{1,0:T(8,128)(2,1)S(1)} %bitcast.23, f32[1,5120]{1,0:T(1,128)S(1)} %copy-done.3, bf16[432,5120]{1,0:T(8,128)(2,1)} %bitcast.38, ...), custom_call_target="tpu_custom_call" | custom-call | flops 3397386240 | bytes 15728640 | tf_op jit(solution)/shard_map/pallas_call | solution.py:383
  42.5 4.0 %all-to-all-start.1 = ((bf16[8,16,5120]{2,1,0:T(8,128)(2,1)}), bf16[8,16,5120]{2,1,0:T(8,128)(2,1)S(1)}, u32[]{:S(2)}, u32[]{:S(2)}) async-start(bf16[8,16,5120]{2,1,0:T(8,128)(2,1)} %bitcast.42), calls=%async_computation.1 | async-start | bytes 2621440 | tf_op jit(solution)/shard_map/all_to_all | solution.py:407
  46.7 13.0 %all-to-all-done.1 = bf16[8,16,5120]{2,1,0:T(8,128)(2,1)S(1)} async-done(((bf16[8,16,5120]{2,1,0:T(8,128)(2,1)}), bf16[8,16,5120]{2,1,0:T(8,128)(2,1)S(1)}, u32[]{:S(2)}, u32[]{:S(2)}) %all-to-all-start.1) | async-done | bytes 1310752 | tf_op jit(solution)/shard_map/all_to_all | solution.py:407
  60.4 2.6 %collective-permute-start.8 = (bf16[16,5120]{1,0:T(8,128)(2,1)S(1)}, bf16[16,5120]{1,0:T(8,128)(2,1)S(1)}, u32[]{:S(2)}, u32[]{:S(2)}) collective-permute-start(bf16[16,5120]{1,0:T(8,128)(2,1)S(1)} %shard_map.104), channel_id=1, source_target_pairs={{0,16},{16,32},{32,48},{48,64},{64,80},{80,96},{96,112},{1,17},{17... | collective-permute-start | bytes 491528 | tf_op jit(solution)/shard_map/ppermute | solution.py:436
  63.1 3.6 %collective-permute-done.8.rows.x = bf16[16,5120]{1,0:T(8,128)(2,1)S(1)} collective-permute-done((bf16[16,5120]{1,0:T(8,128)(2,1)S(1)}, bf16[16,5120]{1,0:T(8,128)(2,1)S(1)}, u32[]{:S(2)}, u32[]{:S(2)}) %collective-permute-start.8) | collective-permute-done | bytes 163872 | tf_op jit(solution)/shard_map/ppermute | solution.py:436
  66.7 5.2 %collective-permute-done.9.refs_3_ = bf16[32,5120]{1,0:T(8,128)(2,1)S(1)} collective-permute-done((bf16[32,5120]{1,0:T(8,128)(2,1)S(1)}, bf16[32,5120]{1,0:T(8,128)(2,1)S(1)}, u32[]{:S(2)}, u32[]{:S(2)}) %collective-permute-start.9) | collective-permute-done | bytes 327712 | tf_op jit(solution)/shard_map/ppermute | solution.py:494
  73.0 3.8 %all-to-all-start.2 = ((bf16[8,16,5120]{2,1,0:T(8,128)(2,1)}), bf16[8,16,5120]{2,1,0:T(8,128)(2,1)S(1)}, u32[]{:S(2)}, u32[]{:S(2)}) async-start(bf16[8,16,5120]{2,1,0:T(8,128)(2,1)} %bitcast.9), calls=%async_computation.2 | async-start | bytes 2621440 | tf_op jit(solution)/shard_map/all_to_all | solution.py:407
  77.5 6.7 %shard_map.106 = (bf16[16,5120]{1,0:T(8,128)(2,1)S(1)}, bf16[128,5120]{1,0:T(8,128)(2,1)}, f32[2,128,432]{2,1,0:T(8,128)}) custom-call(bf16[32,5120]{1,0:T(8,128)(2,1)S(1)} %get-tuple-element.77.refs_0_, bf16[32,5120]{1,0:T(8,128)(2,1)S(1)} %get-tuple-element.80.refs_1_, bf16[32,5120]{1,0:T(8,128)(2,1)S(1)} %collective-permute-done.7.refs_2_, ...), custom_call_target="tpu_custom_call" | custom-call | flops 3397386240 | bytes 7864320 | tf_op jit(solution)/shard_map/pallas_call | solution.py:383
  84.2 5.6 %all-to-all-done.2 = bf16[8,16,5120]{2,1,0:T(8,128)(2,1)S(1)} async-done(((bf16[8,16,5120]{2,1,0:T(8,128)(2,1)}), bf16[8,16,5120]{2,1,0:T(8,128)(2,1)S(1)}, u32[]{:S(2)}, u32[]{:S(2)}) %all-to-all-start.2) | async-done | bytes 1310752 | tf_op jit(solution)/shard_map/all_to_all | solution.py:407
  89.8 7.8 %shard_map.107 = (f32[1,5120]{1,0:T(1,128)S(1)}, bf16[16,5120]{1,0:T(8,128)(2,1)}, bf16[128,5120]{1,0:T(8,128)(2,1)}, bf16[128,5120]{1,0:T(8,128)(2,1)}, bf16[12...) custom-call(bf16[128,5120]{1,0:T(8,128)(2,1)S(1)} %bitcast.31, ...), custom_call_target="tpu_custom_call" | custom-call | flops 3397386240 | bytes 10485760 | tf_op jit(solution)/shard_map/pallas_call | solution.py:383
  97.6 3.6 %all-to-all-start.3 = ((bf16[8,16,5120]{2,1,0:T(8,128)(2,1)}), bf16[8,16,5120]{2,1,0:T(8,128)(2,1)S(1)}, u32[]{:S(2)}, u32[]{:S(2)}) async-start(bf16[8,16,5120]{2,1,0:T(8,128)(2,1)} %bitcast.43), calls=%async_computation.3 | async-start | bytes 2621440 | tf_op jit(solution)/shard_map/all_to_all | solution.py:407
  101.3 6.7 %shard_map.108 = (bf16[64,5120]{1,0:T(8,128)(2,1)}, bf16[64,5120]{1,0:T(8,128)(2,1)}) custom-call(s32[128,1]{1,0:T(8,128)S(1)} %add.290.to_target, bf16[128,432]{1,0:T(8,128)(2,1)} %get-tuple-element.85.hidden_a.refs_11_, bf16[128,432]{1,0:T(8,128)(2,1)} %get-tuple-element.86.hidden_b.hidden_two_b, bf16[432,5120]{1,0:T(8,128)(2,1)} %bitcast.35, ...), custom_call_target="tpu_custom_call" | custom-call | flops 2264924160 | bytes 7864320 | tf_op jit(solution)/shard_map/pallas_call | solution.py:383
  107.9 6.4 %all-to-all-done.3 = bf16[8,16,5120]{2,1,0:T(8,128)(2,1)S(1)} async-done(((bf16[8,16,5120]{2,1,0:T(8,128)(2,1)}), bf16[8,16,5120]{2,1,0:T(8,128)(2,1)S(1)}, u32[]{:S(2)}, u32[]{:S(2)}) %all-to-all-start.3) | async-done | bytes 1310752 | tf_op jit(solution)/shard_map/all_to_all | solution.py:407
  114.7 2.5 %collective-permute-start.10 = (bf16[16,5120]{1,0:T(8,128)(2,1)S(1)}, bf16[16,5120]{1,0:T(8,128)(2,1)S(1)}, u32[]{:S(2)}, u32[]{:S(2)}) collective-permute-start(bf16[16,5120]{1,0:T(8,128)(2,1)S(1)} %shard_map.109), channel_id=1, source_target_pairs={{16,0},{32,16},{48,32},{64,48},{80,64},{96,80},{112,96},{17,1},{33... | collective-permute-start | bytes 491528 | tf_op jit(solution)/shard_map/ppermute | solution.py:436
  117.2 7.2 %collective-permute-done.10.rows.c = bf16[16,5120]{1,0:T(8,128)(2,1)S(1)} collective-permute-done((bf16[16,5120]{1,0:T(8,128)(2,1)S(1)}, bf16[16,5120]{1,0:T(8,128)(2,1)S(1)}, u32[]{:S(2)}, u32[]{:S(2)}) %collective-permute-start.10) | collective-permute-done | bytes 163872 | tf_op jit(solution)/shard_map/ppermute | solution.py:436
  124.5 15.9 %all_to_all.70 = bf16[8,16,5120]{2,1,0:T(8,128)(2,1)S(1)} all-to-all(bf16[8,16,5120]{2,1,0:T(8,128)(2,1)S(1)} %bitcast.27), channel_id=1, replica_groups={{0,2,4,6,8,10,12,14},{1,3,5,7,9,11,13,15},{16,18,20,22,24,26,28,30},{17..., dimensions={0} | all-to-all | bytes 2621440 | tf_op jit(solution)/shard_map/all_to_all | solution.py:407
  140.7 9.4 %shard_map.111 = (bf16[128,5760]{1,0:T(8,128)(2,1)}, bf16[128,5120]{1,0:T(8,128)(2,1)}, bf16[128,432]{1,0:T(8,128)(2,1)}, bf16[4,128,432]{2,1,0:T(8,128)(2,1)}) custom-call(bf16[128,5120]{1,0:T(8,128)(2,1)S(1)} %bitcast.24, f32[1,5120]{1,0:T(1,128)S(1)} %copy-done.3, f32[1,5120]{1,0:T(1,128)S(1)} %get-tuple-element.93.gain_two, ...), custom_call_target="tpu_custom_call" | custom-call | flops 3397386240 | bytes 15728640 | tf_op jit(solution)/shard_map/pallas_call | solution.py:383
  150.1 14.0 %collective-permute-start.15 = (bf16[128,5120]{1,0:T(8,128)(2,1)}, bf16[128,5120]{1,0:T(8,128)(2,1)}, u32[]{:S(2)}, u32[]{:S(2)}) collective-permute-start(bf16[128,5120]{1,0:T(8,128)(2,1)} %get-tuple-element.107.refs_6_), channel_id=1, source_target_pairs={{0,1},{1,0},{2,3},{3,2},{4,5},{5,4},{6,7},{7,6},{8,9},{9,8},{10,11... | collective-permute-start | bytes 3932168 | tf_op jit(solution)/shard_map/ppermute | solution.py:422
  164.7 6.1 %all-to-all-start.5 = ((bf16[8,16,5760]{2,1,0:T(8,128)(2,1)}), bf16[8,16,5760]{2,1,0:T(8,128)(2,1)S(1)}, u32[]{:S(2)}, u32[]{:S(2)}) async-start(bf16[8,16,5760]{2,1,0:T(8,128)(2,1)} %bitcast.41), calls=%async_computation.5 | async-start | bytes 2949120 | tf_op jit(solution)/shard_map/all_to_all | solution.py:407
  173.4 1.7 collective-permute-start.17
  175.1 2.4 %collective-permute-start.18 = (bf16[16,5120]{1,0:T(8,128)(2,1)}, bf16[16,5120]{1,0:T(8,128)(2,1)S(1)}, u32[]{:S(2)}, u32[]{:S(2)}) collective-permute-start(bf16[16,5120]{1,0:T(8,128)(2,1)} %get-tuple-element.121), channel_id=1, source_target_pairs={{0,4},{1,5},{2,6},{3,7},{4,0},{5,1},{6,2},{7,3},{8,12},{9,13},{10,... | collective-permute-start | bytes 491528 | tf_op jit(solution)/shard_map/ppermute | solution.py:538
  178.6 10.0 %shard_map.112 = (bf16[432,5120]{1,0:T(8,128)(2,1)}, bf16[432,5120]{1,0:T(8,128)(2,1)}) custom-call(bf16[128,5120]{1,0:T(8,128)(2,1)} %get-tuple-element.101.normed_in.refs_0_, bf16[128,5120]{1,0:T(8,128)(2,1)} %collective-permute-done.12.refs_1_, bf16[128,5120]{1,0:T(8,128)(2,1)} %get-tuple-element.103.refs_2_, ...), custom_call_target="tpu_custom_call" | custom-call | flops 4529848320 | bytes 20971520 | tf_op jit(solution)/shard_map/pallas_call | solution.py:544
  188.7 4.1 %all-to-all-done.5 = bf16[8,16,5760]{2,1,0:T(8,128)(2,1)S(1)} async-done(((bf16[8,16,5760]{2,1,0:T(8,128)(2,1)}), bf16[8,16,5760]{2,1,0:T(8,128)(2,1)S(1)}, u32[]{:S(2)}, u32[]{:S(2)}) %all-to-all-start.5) | async-done | bytes 1474592 | tf_op jit(solution)/shard_map/all_to_all | solution.py:407
  193.9 3.9 %collective-permute-done.18.third = bf16[16,5120]{1,0:T(8,128)(2,1)S(1)} collective-permute-done((bf16[16,5120]{1,0:T(8,128)(2,1)}, bf16[16,5120]{1,0:T(8,128)(2,1)S(1)}, u32[]{:S(2)}, u32[]{:S(2)}) %collective-permute-start.18) | collective-permute-done | bytes 163872 | tf_op jit(solution)/shard_map/ppermute | solution.py:538
  197.9 1.6 collective-permute-start.20
  (77 shorter events, 16.0 us)
Async XLA Ops:
  0.6 45.9 %copy-start = (s32[8,16]{1,0:T(8,128)S(1)}, s32[8,16]{1,0:T(8,128)}, u32[]{:S(2)}) copy-start(s32[8,16]{1,0:T(8,128)} %param.11) | copy-start | bytes 1540
  0.6 2.0 collective-permute-start
  2.6 31.1 %collective-permute-start.6 = (bf16[432,5120]{1,0:T(8,128)(2,1)}, bf16[432,5120]{1,0:T(8,128)(2,1)}, u32[]{:S(2)}, u32[]{:S(2)}) collective-permute-start(bf16[432,5120]{1,0:T(8,128)(2,1)} %bitcast.32), channel_id=1, source_target_pairs={{0,1},{1,0},{2,3},{3,2},{4,5},{5,4},{6,7},{7,6},{8,9},{9,8},{10,11... | collective-permute-start | bytes 13271048 | tf_op jit(solution)/shard_map/ppermute | solution.py:422
  3.0 30.8 %collective-permute-start.5 = (bf16[432,5120]{1,0:T(8,128)(2,1)}, bf16[432,5120]{1,0:T(8,128)(2,1)}, u32[]{:S(2)}, u32[]{:S(2)}) collective-permute-start(bf16[432,5120]{1,0:T(8,128)(2,1)} %bitcast.37), channel_id=1, source_target_pairs={{0,1},{1,0},{2,3},{3,2},{4,5},{5,4},{6,7},{7,6},{8,9},{9,8},{10,11... | collective-permute-start | bytes 13271048 | tf_op jit(solution)/shard_map/ppermute | solution.py:422
  5.6 0.7 collective-permute-start.1
  6.3 27.5 %copy-start.3 = (f32[1,5120]{1,0:T(1,128)S(1)}, f32[1,5120]{1,0:T(1,128)}, u32[]{:S(2)}) copy-start(f32[1,5120]{1,0:T(1,128)} %gain.9) | copy-start | bytes 61444
  6.3 24.5 %all-to-all-start = ((bf16[8,16,5120]{2,1,0:T(8,128)(2,1)}), bf16[8,16,5120]{2,1,0:T(8,128)(2,1)S(1)}, u32[]{:S(2)}, u32[]{:S(2)}) async-start(bf16[8,16,5120]{2,1,0:T(8,128)(2,1)} %bitcast.3), calls=%async_computation | async-start | bytes 2621440 | tf_op jit(solution)/shard_map/all_to_all | solution.py:407
  13.8 12.6 %collective-permute-start.2 = (bf16[16,5120]{1,0:T(8,128)(2,1)S(1)}, bf16[16,5120]{1,0:T(8,128)(2,1)S(1)}, u32[]{:S(2)}, u32[]{:S(2)}) collective-permute-start(bf16[16,5120]{1,0:T(8,128)(2,1)S(1)} %get-tuple-element.70.own), channel_id=1, source_target_pairs={{0,2},{1,3},{2,4},{3,5},{4,6},{5,7},{6,0},{7,1},{8,10},{9,11},{10,... | collective-permute-start | bytes 491528 | tf_op jit(solution)/shard_map/ppermute | solution.py:479
  15.3 15.5 %collective-permute-start.3 = (bf16[16,5120]{1,0:T(8,128)(2,1)S(1)}, bf16[16,5120]{1,0:T(8,128)(2,1)S(1)}, u32[]{:S(2)}, u32[]{:S(2)}) collective-permute-start(bf16[16,5120]{1,0:T(8,128)(2,1)S(1)} %get-tuple-element.70.own), channel_id=1, source_target_pairs={{0,4},{1,5},{2,6},{3,7},{4,0},{5,1},{6,2},{7,3},{8,12},{9,13},{10,... | collective-permute-start | bytes 491528 | tf_op jit(solution)/shard_map/ppermute | solution.py:479
  17.7 13.1 %collective-permute-start.4 = (bf16[16,5120]{1,0:T(8,128)(2,1)S(1)}, bf16[16,5120]{1,0:T(8,128)(2,1)S(1)}, u32[]{:S(2)}, u32[]{:S(2)}) collective-permute-start(bf16[16,5120]{1,0:T(8,128)(2,1)S(1)} %get-tuple-element.70.own), channel_id=1, source_target_pairs={{1,7},{3,1},{5,3},{7,5},{9,15},{11,9},{13,11},{15,13},{17,23},{19,... | collective-permute-start | bytes 491528 | tf_op jit(solution)/shard_map/ppermute | solution.py:480
  30.8 11.7 %collective-permute-start.7 = (bf16[32,5120]{1,0:T(8,128)(2,1)S(1)}, bf16[32,5120]{1,0:T(8,128)(2,1)S(1)}, u32[]{:S(2)}, u32[]{:S(2)}) collective-permute-start(bf16[32,5120]{1,0:T(8,128)(2,1)S(1)} %get-tuple-element.77.refs_0_), channel_id=1, source_target_pairs={{0,8},{1,9},{2,10},{3,11},{4,12},{5,13},{6,14},{7,15},{8,0},{9,1},... | collective-permute-start | bytes 983048 | tf_op jit(solution)/shard_map/ppermute | solution.py:483
  42.5 17.3 %copy-start.1 = (bf16[1,16,5120]{2,1,0:T(8,128)(2,1)S(1)}, bf16[1,16,5120]{2,1,0:T(8,128)(2,1)}, u32[]{:S(2)}) copy-start(bf16[1,16,5120]{2,1,0:T(8,128)(2,1)} %param.6) | copy-start | bytes 491524
  42.5 17.3 %all-to-all-start.1 = ((bf16[8,16,5120]{2,1,0:T(8,128)(2,1)}), bf16[8,16,5120]{2,1,0:T(8,128)(2,1)S(1)}, u32[]{:S(2)}, u32[]{:S(2)}) async-start(bf16[8,16,5120]{2,1,0:T(8,128)(2,1)} %bitcast.42), calls=%async_computation.1 | async-start | bytes 2621440 | tf_op jit(solution)/shard_map/all_to_all | solution.py:407
  60.0 11.9 %collective-permute-start.9 = (bf16[32,5120]{1,0:T(8,128)(2,1)S(1)}, bf16[32,5120]{1,0:T(8,128)(2,1)S(1)}, u32[]{:S(2)}, u32[]{:S(2)}) collective-permute-start(bf16[32,5120]{1,0:T(8,128)(2,1)S(1)} %get-tuple-element.80.refs_1_), channel_id=1, source_target_pairs={{0,8},{1,9},{2,10},{3,11},{4,12},{5,13},{6,14},{7,15},{8,0},{9,1},... | collective-permute-start | bytes 983048 | tf_op jit(solution)/shard_map/ppermute | solution.py:494
  60.4 6.3 %collective-permute-start.8 = (bf16[16,5120]{1,0:T(8,128)(2,1)S(1)}, bf16[16,5120]{1,0:T(8,128)(2,1)S(1)}, u32[]{:S(2)}, u32[]{:S(2)}) collective-permute-start(bf16[16,5120]{1,0:T(8,128)(2,1)S(1)} %shard_map.104), channel_id=1, source_target_pairs={{0,16},{16,32},{32,48},{48,64},{64,80},{80,96},{96,112},{1,17},{17... | collective-permute-start | bytes 491528 | tf_op jit(solution)/shard_map/ppermute | solution.py:436
  73.0 16.8 %all-to-all-start.2 = ((bf16[8,16,5120]{2,1,0:T(8,128)(2,1)}), bf16[8,16,5120]{2,1,0:T(8,128)(2,1)S(1)}, u32[]{:S(2)}, u32[]{:S(2)}) async-start(bf16[8,16,5120]{2,1,0:T(8,128)(2,1)} %bitcast.9), calls=%async_computation.2 | async-start | bytes 2621440 | tf_op jit(solution)/shard_map/all_to_all | solution.py:407
  97.6 16.8 %all-to-all-start.3 = ((bf16[8,16,5120]{2,1,0:T(8,128)(2,1)}), bf16[8,16,5120]{2,1,0:T(8,128)(2,1)S(1)}, u32[]{:S(2)}, u32[]{:S(2)}) async-start(bf16[8,16,5120]{2,1,0:T(8,128)(2,1)} %bitcast.43), calls=%async_computation.3 | async-start | bytes 2621440 | tf_op jit(solution)/shard_map/all_to_all | solution.py:407
  114.7 9.7 %collective-permute-start.10 = (bf16[16,5120]{1,0:T(8,128)(2,1)S(1)}, bf16[16,5120]{1,0:T(8,128)(2,1)S(1)}, u32[]{:S(2)}, u32[]{:S(2)}) collective-permute-start(bf16[16,5120]{1,0:T(8,128)(2,1)S(1)} %shard_map.109), channel_id=1, source_target_pairs={{16,0},{32,16},{48,32},{64,48},{80,64},{96,80},{112,96},{17,1},{33... | collective-permute-start | bytes 491528 | tf_op jit(solution)/shard_map/ppermute | solution.py:436
  124.5 15.9 %copy-start.5 = (bf16[64,5120]{1,0:T(8,128)(2,1)S(1)}, bf16[64,5120]{1,0:T(8,128)(2,1)}, u32[]{:S(2)}) copy-start(bf16[64,5120]{1,0:T(8,128)(2,1)} %get-tuple-element.99) | copy-start | bytes 1966084
  140.4 24.3 %collective-permute-start.11 = (bf16[64,5120]{1,0:T(8,128)(2,1)S(1)}, bf16[64,5120]{1,0:T(8,128)(2,1)S(1)}, u32[]{:S(2)}, u32[]{:S(2)}) collective-permute-start(bf16[64,5120]{1,0:T(8,128)(2,1)S(1)} %copy-done.5), channel_id=1, source_target_pairs={{0,8},{1,9},{2,10},{3,11},{4,12},{5,13},{6,14},{7,15},{8,0},{9,1},... | collective-permute-start | bytes 1966088 | tf_op jit(solution)/shard_map/ppermute | solution.py:525
  150.1 25.0 %collective-permute-start.15 = (bf16[128,5120]{1,0:T(8,128)(2,1)}, bf16[128,5120]{1,0:T(8,128)(2,1)}, u32[]{:S(2)}, u32[]{:S(2)}) collective-permute-start(bf16[128,5120]{1,0:T(8,128)(2,1)} %get-tuple-element.107.refs_6_), channel_id=1, source_target_pairs={{0,1},{1,0},{2,3},{3,2},{4,5},{5,4},{6,7},{7,6},{8,9},{9,8},{10,11... | collective-permute-start | bytes 3932168 | tf_op jit(solution)/shard_map/ppermute | solution.py:422
  164.1 13.3 %collective-permute-start.14 = (bf16[128,5120]{1,0:T(8,128)(2,1)}, bf16[128,5120]{1,0:T(8,128)(2,1)}, u32[]{:S(2)}, u32[]{:S(2)}) collective-permute-start(bf16[128,5120]{1,0:T(8,128)(2,1)} %get-tuple-element.105.refs_4_), channel_id=1, source_target_pairs={{0,1},{1,0},{2,3},{3,2},{4,5},{5,4},{6,7},{7,6},{8,9},{9,8},{10,11... | collective-permute-start | bytes 3932168 | tf_op jit(solution)/shard_map/ppermute | solution.py:422
  164.2 14.4 %collective-permute-start.13 = (bf16[128,5120]{1,0:T(8,128)(2,1)}, bf16[128,5120]{1,0:T(8,128)(2,1)}, u32[]{:S(2)}, u32[]{:S(2)}) collective-permute-start(bf16[128,5120]{1,0:T(8,128)(2,1)} %get-tuple-element.103.refs_2_), channel_id=1, source_target_pairs={{0,1},{1,0},{2,3},{3,2},{4,5},{5,4},{6,7},{7,6},{8,9},{9,8},{10,11... | collective-permute-start | bytes 3932168 | tf_op jit(solution)/shard_map/ppermute | solution.py:422
  164.6 14.0 %collective-permute-start.12 = (bf16[128,5120]{1,0:T(8,128)(2,1)}, bf16[128,5120]{1,0:T(8,128)(2,1)}, u32[]{:S(2)}, u32[]{:S(2)}) collective-permute-start(bf16[128,5120]{1,0:T(8,128)(2,1)} %get-tuple-element.101.normed_in.refs_0_), channel_id=1, source_target_pairs={{0,1},{1,0},{2,3},{3,2},{4,5},{5,4},{6,7},{7,6},{8,9},{9,8},{10,11... | collective-permute-start | bytes 3932168 | tf_op jit(solution)/shard_map/ppermute | solution.py:422
  164.7 28.0 %all-to-all-start.5 = ((bf16[8,16,5760]{2,1,0:T(8,128)(2,1)}), bf16[8,16,5760]{2,1,0:T(8,128)(2,1)S(1)}, u32[]{:S(2)}, u32[]{:S(2)}) async-start(bf16[8,16,5760]{2,1,0:T(8,128)(2,1)} %bitcast.41), calls=%async_computation.5 | async-start | bytes 2949120 | tf_op jit(solution)/shard_map/all_to_all | solution.py:407
  170.9 2.5 %collective-permute-start.16 = (bf16[4,128,432]{2,1,0:T(8,128)(2,1)}, bf16[4,128,432]{2,1,0:T(8,128)(2,1)S(1)}, u32[]{:S(2)}, u32[]{:S(2)}) collective-permute-start(bf16[4,128,432]{2,1,0:T(8,128)(2,1)} %get-tuple-element.111), channel_id=1, source_target_pairs={{0,1},{1,0},{2,3},{3,2},{4,5},{5,4},{6,7},{7,6},{8,9},{9,8},{10,11... | collective-permute-start | bytes 1327112 | tf_op jit(solution)/shard_map/ppermute | solution.py:422
  173.4 20.5 %collective-permute-start.17 = (bf16[16,5120]{1,0:T(8,128)(2,1)}, bf16[16,5120]{1,0:T(8,128)(2,1)S(1)}, u32[]{:S(2)}, u32[]{:S(2)}) collective-permute-start(bf16[16,5120]{1,0:T(8,128)(2,1)} %get-tuple-element.120), channel_id=1, source_target_pairs={{0,2},{1,3},{2,4},{3,5},{4,6},{5,7},{6,0},{7,1},{8,10},{9,11},{10,... | collective-permute-start | bytes 491528 | tf_op jit(solution)/shard_map/ppermute | solution.py:538
  175.1 22.8 %collective-permute-start.18 = (bf16[16,5120]{1,0:T(8,128)(2,1)}, bf16[16,5120]{1,0:T(8,128)(2,1)S(1)}, u32[]{:S(2)}, u32[]{:S(2)}) collective-permute-start(bf16[16,5120]{1,0:T(8,128)(2,1)} %get-tuple-element.121), channel_id=1, source_target_pairs={{0,4},{1,5},{2,6},{3,7},{4,0},{5,1},{6,2},{7,3},{8,12},{9,13},{10,... | collective-permute-start | bytes 491528 | tf_op jit(solution)/shard_map/ppermute | solution.py:538
  177.5 20.4 %collective-permute-start.19 = (bf16[16,5120]{1,0:T(8,128)(2,1)}, bf16[16,5120]{1,0:T(8,128)(2,1)S(1)}, u32[]{:S(2)}, u32[]{:S(2)}) collective-permute-start(bf16[16,5120]{1,0:T(8,128)(2,1)} %get-tuple-element.122), channel_id=1, source_target_pairs={{0,6},{1,7},{2,0},{3,1},{4,2},{5,3},{6,4},{7,5},{8,14},{9,15},{10,... | collective-permute-start | bytes 491528 | tf_op jit(solution)/shard_map/ppermute | solution.py:538
  188.7 9.1 %copy-start.4 = (bf16[16,5120]{1,0:T(8,128)(2,1)S(1)}, bf16[16,5120]{1,0:T(8,128)(2,1)}, u32[]{:S(2)}) copy-start(bf16[16,5120]{1,0:T(8,128)(2,1)} %get-tuple-element.116.own_rows) | copy-start | bytes 491524
  197.9 2.8 %collective-permute-start.20 = (bf16[16,5120]{1,0:T(8,128)(2,1)S(1)}, bf16[16,5120]{1,0:T(8,128)(2,1)S(1)}, u32[]{:S(2)}, u32[]{:S(2)}) collective-permute-start(bf16[16,5120]{1,0:T(8,128)(2,1)S(1)} %shard_map.115.own), channel_id=1, source_target_pairs={{0,1},{1,0},{2,3},{3,2},{4,5},{5,4},{6,7},{7,6},{8,9},{9,8},{10,11... | collective-permute-start | bytes 491528 | tf_op jit(solution)/shard_map/ppermute | solution.py:422
  199.5 1.2 collective-permute-start.21
  (2 other events, 12.1 us)

commit v5 on v4

--- a/solution.py
+++ b/solution.py
@@ -121,7 +121,7 @@
     total = normed_times_up(x, scale, gain, normed, normed_out, stores, ups, wu, downs)
     for half in range(2):
         value, slant = silu_parts(total[half])
-        slope[half] = slant
+        slope[half] = slant.astype(BF)
         hidden[half] = value.astype(BF)
     stores.add(slope, slope_out)
     stores.add(hidden.at[0], hidden_a_out)
@@ -188,7 +188,7 @@
             term = dot_nt(piece, wd[half, :, cols])
             total[half] = term if at == 0 else total[half] + term
     for half in range(2):
-        d_hidden[half] = total[half]
+        d_hidden[half] = total[half].astype(BF)
     stores.add(d_hidden, d_hidden_out)
     stores.finish()
 
@@ -209,7 +209,7 @@
     for half in range(2):
         value, slope = silu_parts(total[half])
         hidden[half] = value.astype(BF)
-        d_act[half] = (d_hidden[half] * slope).astype(BF)
+        d_act[half] = (d_hidden[half].astype(F32) * slope).astype(BF)
     stores.add(d_act.at[0], d_act_a_out)
     stores.add(d_act.at[1], d_act_b_out)
     stores.add(hidden.at[0], hidden_a_out)
@@ -275,7 +275,6 @@
     for at, source in enumerate((d_act_two_b, hidden_one_b, hidden_two_b)):
         fetches.append(pltpu.make_async_copy(source, thin.at[at], sh.at[2 + at]))
     stores = Stores(so)
-    stores.add(c, c_out)
     total = [None, None]
     for at, cols in enumerate(chunks(width)):
         downs.wait(at)
@@ -289,8 +288,9 @@
     for fetch in fetches:
         fetch.wait()
     for half in range(2):
-        d_act[half] = (total[half] * slope[half]).astype(BF)
+        d_act[half] = (total[half] * slope[half].astype(F32)).astype(BF)
     stores.add(d_act.at[0], d_act_a_out)
+    stores.add(c, c_out)
     stores.add(d_act.at[1], thin_out.at[0])
     stores.add(thin, thin_out.at[1:4])
     gain_pieces = []
@@ -447,7 +447,7 @@
     moved = 2 * TALL * width * 2
     steps = width // CHUNK
     tall, block, slim = shape(TALL, width), shape(ROWS, width), shape(TALL, units)
-    pair_f32 = shape(2, TALL, units, dtype=F32)
+    both_halves = shape(2, TALL, units)
 
     cot_b = swap(cot_in)
     up_b, down_b = swap(after(up, cot_b)), swap(after(down, cot_b))
@@ -482,9 +482,9 @@
     x_one, cot_a, cot_b = together(x_one, cot_a, cot_b)
     cot_za = lax.ppermute(cot_a, "peer", ACROSS_Z)
     proj, normed_one, slope_one, hidden_one, hidden_one_b = call(
-        forward_kernel, [], [x_one, gain], [up, up_b, down, down_b], [tall, tall, pair_f32, slim, slim],
+        forward_kernel, [], [x_one, gain], [up, up_b, down, down_b], [tall, tall, both_halves, slim, slim],
         weight_scratch(units, width, 2)
-        + [kept(TALL, width), kept(TALL, width), kept(2, TALL, units, dtype=F32), kept(2, TALL, units), dma(2 * steps + 3)],
+        + [kept(TALL, width), kept(TALL, width), kept(2, TALL, units), kept(2, TALL, units), dma(2 * steps + 3)],
         limit=36, flops=3 * flops, moved=6 * moved,
     )
     proj, cot_za = together(proj, cot_za)
@@ -496,15 +496,15 @@
     cot_all = [cot_a, cot_b, cot_za, cot_zb]
     x_two = from_chips(arrived)
     cot_own, cot, d_hidden = call(
-        cot_kernel, [block], cot_all + [pick, own_pick], [down, down_b], [tall, pair_f32],
-        weight_scratch(units, width, 1) + [kept(TALL, width), kept(2, TALL, units, dtype=F32), dma(steps + 1)],
+        cot_kernel, [block], cot_all + [pick, own_pick], [down, down_b], [tall, both_halves],
+        weight_scratch(units, width, 1) + [kept(TALL, width), kept(2, TALL, units), dma(steps + 1)],
         limit=20, flops=3 * flops, moved=3 * moved,
     )
     gain_two, own_rows, d_normed, normed_two, d_act_two, d_act_two_b, hidden_two, hidden_two_b = call(
         second_kernel, [shape(1, width, dtype=F32)],
         [x_two, gain, own_target], [d_hidden, up, up_b], [block, tall, tall, slim, slim, slim, slim],
         weight_scratch(units, width, 1)
-        + [kept(ROWS, width), kept(TALL, width), kept(TALL, width), kept(2, TALL, units), kept(2, TALL, units), kept(2, TALL, units, dtype=F32),
+        + [kept(ROWS, width), kept(TALL, width), kept(TALL, width), kept(2, TALL, units), kept(2, TALL, units), kept(2, TALL, units),
            pltpu.SemaphoreType.DMA, dma(2 * steps + 5)],
         limit=28, flops=3 * flops, moved=4 * moved,
     )
@@ -528,7 +528,7 @@
         [slope_one, normed_one, d_act_two_b, hidden_one_b, hidden_two_b, up, up_b, down, down_b],
         [shape(TALL, width + width // 8), tall, slim, shape(4, TALL, units)],
         weight_scratch(units, width, 2)
-        + [kept(TALL, width + width // 8), kept(2, TALL, units), kept(2, TALL, units, dtype=F32), kept(TALL, width), kept(3, TALL, units), dma(5), dma(steps + 5)],
+        + [kept(TALL, width + width // 8), kept(2, TALL, units), kept(2, TALL, units), kept(TALL, width), kept(3, TALL, units), dma(5), dma(steps + 5)],
         limit=36, flops=3 * flops, moved=6 * moved,
     )
     ready = d_normed

time: 202 us -> 202 us (level)
  no operation moved by 1% of the time
where the time goes in v5:
time: 202 us
  starting transfers between devices  64.8 us (32%)
  waiting for transfers between devices  62.6 us (31%)
  Pallas kernels  56.1 us (28%)
  blocking collectives  15.9 us (8%)
    pallas_call x15, Pallas kernels, call(): pl.pallas_call(kernel, out_shape=list(outs) + [pltpu.HBM(out.shape, out.d...  46 us
    all_to_all x5, waiting for transfers between devices, to_chips(): lax.all_to_all(blocks, 'peer', split_axis=0, concat_axis=0, tiled=True, a...  29.2 us
    all_to_all x5, starting transfers between devices, to_chips(): lax.all_to_all(blocks, 'peer', split_axis=0, concat_axis=0, tiled=True, a...  25 us
    ppermute x10, starting transfers between devices, swap(): return lax.ppermute(value, 'peer', SIBLING)  18.3 us
    all_to_all x1, blocking collectives, to_chips(): lax.all_to_all(blocks, 'peer', split_axis=0, concat_axis=0, tiled=True, a...  15.9 us
    ppermute x2, waiting for transfers between devices, passed_along(): lax.ppermute(value, 'section', [(source, source + steps) for source in ra...  10.9 us
    pallas_call x1, Pallas kernels, local(): pl.pallas_call(grads_kernel, grid=(width // step,), out_shape=[shape(unit...  10 us
    ppermute x1, waiting for transfers between devices, local(): lax.ppermute(rest, 'peer', ALONG_Y[1])  5.67 us
  transfers between devices with their start and end apart: 27, of which 13 were waited for; matrix products, arithmetic and copies ran while one was open for 1% of the time, Pallas kernels for 23%

profile of v5, /device:TPU:7, one launch (start us, length us, event | category | flops | bytes accessed | tf_op | source)
XLA Modules:
  0.0 201.6 jit_solution(6182658634781499862)
XLA Ops:
  3.3 2.3 %shard_map.101 = (bf16[128,5120]{1,0:T(8,128)(2,1)}, bf16[16,5120]{1,0:T(8,128)(2,1)S(1)}) custom-call(bf16[16,5120]{1,0:T(8,128)(2,1)S(1)} %collective-permute-done.other, s32[16,1]{1,0:T(8,128)S(1)} %add.291.index, bf16[16,5120]{1,0:T(8,128)(2,1)} %bitcast.28, bf16[16,5120]{1,0:T(8,128)(2,1)} %bitcast.45), custom_call_target="tpu_custom_call" | custom-call | bytes 2621440 | tf_op jit(solution)/shard_map/pallas_call | solution.py:383
  6.3 7.5 %all-to-all-start = ((bf16[8,16,5120]{2,1,0:T(8,128)(2,1)}), bf16[8,16,5120]{2,1,0:T(8,128)(2,1)S(1)}, u32[]{:S(2)}, u32[]{:S(2)}) async-start(bf16[8,16,5120]{2,1,0:T(8,128)(2,1)} %bitcast.3), calls=%async_computation | async-start | bytes 2621440 | tf_op jit(solution)/shard_map/all_to_all | solution.py:407
  15.3 2.4 %collective-permute-start.3 = (bf16[16,5120]{1,0:T(8,128)(2,1)S(1)}, bf16[16,5120]{1,0:T(8,128)(2,1)S(1)}, u32[]{:S(2)}, u32[]{:S(2)}) collective-permute-start(bf16[16,5120]{1,0:T(8,128)(2,1)S(1)} %get-tuple-element.70.own), channel_id=1, source_target_pairs={{0,4},{1,5},{2,6},{3,7},{4,0},{5,1},{6,2},{7,3},{8,12},{9,13},{10,... | collective-permute-start | bytes 491528 | tf_op jit(solution)/shard_map/ppermute | solution.py:479
  17.7 3.1 %collective-permute-start.4 = (bf16[16,5120]{1,0:T(8,128)(2,1)S(1)}, bf16[16,5120]{1,0:T(8,128)(2,1)S(1)}, u32[]{:S(2)}, u32[]{:S(2)}) collective-permute-start(bf16[16,5120]{1,0:T(8,128)(2,1)S(1)} %get-tuple-element.70.own), channel_id=1, source_target_pairs={{1,7},{3,1},{5,3},{7,5},{9,15},{11,9},{13,11},{15,13},{17,23},{19,... | collective-permute-start | bytes 491528 | tf_op jit(solution)/shard_map/ppermute | solution.py:480
  20.7 5.7 %collective-permute-done.2.fourth = bf16[16,5120]{1,0:T(8,128)(2,1)S(1)} collective-permute-done((bf16[16,5120]{1,0:T(8,128)(2,1)S(1)}, bf16[16,5120]{1,0:T(8,128)(2,1)S(1)}, u32[]{:S(2)}, u32[]{:S(2)}) %collective-permute-start.2) | collective-permute-done | bytes 163872 | tf_op jit(solution)/shard_map/ppermute | solution.py:479
  26.4 4.3 %collective-permute-done.3.third = bf16[16,5120]{1,0:T(8,128)(2,1)S(1)} collective-permute-done((bf16[16,5120]{1,0:T(8,128)(2,1)S(1)}, bf16[16,5120]{1,0:T(8,128)(2,1)S(1)}, u32[]{:S(2)}, u32[]{:S(2)}) %collective-permute-start.3) | collective-permute-done | bytes 163872 | tf_op jit(solution)/shard_map/ppermute | solution.py:479
  30.8 3.0 %collective-permute-start.7 = (bf16[32,5120]{1,0:T(8,128)(2,1)S(1)}, bf16[32,5120]{1,0:T(8,128)(2,1)S(1)}, u32[]{:S(2)}, u32[]{:S(2)}) collective-permute-start(bf16[32,5120]{1,0:T(8,128)(2,1)S(1)} %get-tuple-element.77.refs_0_), channel_id=1, source_target_pairs={{0,8},{1,9},{2,10},{3,11},{4,12},{5,13},{6,14},{7,15},{8,0},{9,1},... | collective-permute-start | bytes 983048 | tf_op jit(solution)/shard_map/ppermute | solution.py:483
  33.8 8.5 %shard_map.103 = (bf16[128,5120]{1,0:T(8,128)(2,1)}, bf16[128,5120]{1,0:T(8,128)(2,1)}, bf16[2,128,432]{2,1,0:T(8,128)(2,1)}, bf16[128,432]{1,0:T(8,128)(2,1)}, bf16[128,432]{1,0:T(8,128)(2,1)}) custom-call(bf16[128,5120]{1,0:T(8,128)(2,1)S(1)} %bitcast.23, f32[1,5120]{1,0:T(1,128)S(1)} %copy-done.3, bf16[432,5120]{1,0:T(8,128)(2,1)} %bitcast.38, ...), custom_call_target="tpu_custom_call" | custom-call | flops 3397386240 | bytes 15728640 | tf_op jit(solution)/shard_map/pallas_call | solution.py:383
  42.3 4.1 %all-to-all-start.1 = ((bf16[8,16,5120]{2,1,0:T(8,128)(2,1)}), bf16[8,16,5120]{2,1,0:T(8,128)(2,1)S(1)}, u32[]{:S(2)}, u32[]{:S(2)}) async-start(bf16[8,16,5120]{2,1,0:T(8,128)(2,1)} %bitcast.42), calls=%async_computation.1 | async-start | bytes 2621440 | tf_op jit(solution)/shard_map/all_to_all | solution.py:407
  46.6 13.0 %all-to-all-done.1 = bf16[8,16,5120]{2,1,0:T(8,128)(2,1)S(1)} async-done(((bf16[8,16,5120]{2,1,0:T(8,128)(2,1)}), bf16[8,16,5120]{2,1,0:T(8,128)(2,1)S(1)}, u32[]{:S(2)}, u32[]{:S(2)}) %all-to-all-start.1) | async-done | bytes 1310752 | tf_op jit(solution)/shard_map/all_to_all | solution.py:407
  60.3 2.5 %collective-permute-start.8 = (bf16[16,5120]{1,0:T(8,128)(2,1)S(1)}, bf16[16,5120]{1,0:T(8,128)(2,1)S(1)}, u32[]{:S(2)}, u32[]{:S(2)}) collective-permute-start(bf16[16,5120]{1,0:T(8,128)(2,1)S(1)} %shard_map.104), channel_id=1, source_target_pairs={{0,16},{16,32},{32,48},{48,64},{64,80},{80,96},{96,112},{1,17},{17... | collective-permute-start | bytes 491528 | tf_op jit(solution)/shard_map/ppermute | solution.py:436
  62.9 3.7 %collective-permute-done.8.rows.x = bf16[16,5120]{1,0:T(8,128)(2,1)S(1)} collective-permute-done((bf16[16,5120]{1,0:T(8,128)(2,1)S(1)}, bf16[16,5120]{1,0:T(8,128)(2,1)S(1)}, u32[]{:S(2)}, u32[]{:S(2)}) %collective-permute-start.8) | collective-permute-done | bytes 163872 | tf_op jit(solution)/shard_map/ppermute | solution.py:436
  66.6 5.2 %collective-permute-done.9.refs_3_ = bf16[32,5120]{1,0:T(8,128)(2,1)S(1)} collective-permute-done((bf16[32,5120]{1,0:T(8,128)(2,1)S(1)}, bf16[32,5120]{1,0:T(8,128)(2,1)S(1)}, u32[]{:S(2)}, u32[]{:S(2)}) %collective-permute-start.9) | collective-permute-done | bytes 327712 | tf_op jit(solution)/shard_map/ppermute | solution.py:494
  72.9 3.8 %all-to-all-start.2 = ((bf16[8,16,5120]{2,1,0:T(8,128)(2,1)}), bf16[8,16,5120]{2,1,0:T(8,128)(2,1)S(1)}, u32[]{:S(2)}, u32[]{:S(2)}) async-start(bf16[8,16,5120]{2,1,0:T(8,128)(2,1)} %bitcast.9), calls=%async_computation.2 | async-start | bytes 2621440 | tf_op jit(solution)/shard_map/all_to_all | solution.py:407
  77.4 6.6 %shard_map.106 = (bf16[16,5120]{1,0:T(8,128)(2,1)S(1)}, bf16[128,5120]{1,0:T(8,128)(2,1)}, bf16[2,128,432]{2,1,0:T(8,128)(2,1)}) custom-call(bf16[32,5120]{1,0:T(8,128)(2,1)S(1)} %get-tuple-element.77.refs_0_, bf16[32,5120]{1,0:T(8,128)(2,1)S(1)} %get-tuple-element.80.refs_1_, bf16[32,5120]{1,0:T(8,128)(2,1)S(1)} %collective-permute-done.7.refs_2_, ...), custom_call_target="tpu_custom_call" | custom-call | flops 3397386240 | bytes 7864320 | tf_op jit(solution)/shard_map/pallas_call | solution.py:383
  84.0 5.6 %all-to-all-done.2 = bf16[8,16,5120]{2,1,0:T(8,128)(2,1)S(1)} async-done(((bf16[8,16,5120]{2,1,0:T(8,128)(2,1)}), bf16[8,16,5120]{2,1,0:T(8,128)(2,1)S(1)}, u32[]{:S(2)}, u32[]{:S(2)}) %all-to-all-start.2) | async-done | bytes 1310752 | tf_op jit(solution)/shard_map/all_to_all | solution.py:407
  89.7 7.8 %shard_map.107 = (f32[1,5120]{1,0:T(1,128)S(1)}, bf16[16,5120]{1,0:T(8,128)(2,1)}, bf16[128,5120]{1,0:T(8,128)(2,1)}, bf16[128,5120]{1,0:T(8,128)(2,1)}, bf16[12...) custom-call(bf16[128,5120]{1,0:T(8,128)(2,1)S(1)} %bitcast.31, ...), custom_call_target="tpu_custom_call" | custom-call | flops 3397386240 | bytes 10485760 | tf_op jit(solution)/shard_map/pallas_call | solution.py:383
  97.5 3.6 %all-to-all-start.3 = ((bf16[8,16,5120]{2,1,0:T(8,128)(2,1)}), bf16[8,16,5120]{2,1,0:T(8,128)(2,1)S(1)}, u32[]{:S(2)}, u32[]{:S(2)}) async-start(bf16[8,16,5120]{2,1,0:T(8,128)(2,1)} %bitcast.43), calls=%async_computation.3 | async-start | bytes 2621440 | tf_op jit(solution)/shard_map/all_to_all | solution.py:407
  101.1 6.6 %shard_map.108 = (bf16[64,5120]{1,0:T(8,128)(2,1)}, bf16[64,5120]{1,0:T(8,128)(2,1)}) custom-call(s32[128,1]{1,0:T(8,128)S(1)} %add.290.to_target, bf16[128,432]{1,0:T(8,128)(2,1)} %get-tuple-element.85.hidden_a.refs_11_, bf16[128,432]{1,0:T(8,128)(2,1)} %get-tuple-element.86.hidden_b.hidden_two_b, bf16[432,5120]{1,0:T(8,128)(2,1)} %bitcast.35, ...), custom_call_target="tpu_custom_call" | custom-call | flops 2264924160 | bytes 7864320 | tf_op jit(solution)/shard_map/pallas_call | solution.py:383
  107.8 6.5 %all-to-all-done.3 = bf16[8,16,5120]{2,1,0:T(8,128)(2,1)S(1)} async-done(((bf16[8,16,5120]{2,1,0:T(8,128)(2,1)}), bf16[8,16,5120]{2,1,0:T(8,128)(2,1)S(1)}, u32[]{:S(2)}, u32[]{:S(2)}) %all-to-all-start.3) | async-done | bytes 1310752 | tf_op jit(solution)/shard_map/all_to_all | solution.py:407
  114.6 2.5 %collective-permute-start.10 = (bf16[16,5120]{1,0:T(8,128)(2,1)S(1)}, bf16[16,5120]{1,0:T(8,128)(2,1)S(1)}, u32[]{:S(2)}, u32[]{:S(2)}) collective-permute-start(bf16[16,5120]{1,0:T(8,128)(2,1)S(1)} %shard_map.109), channel_id=1, source_target_pairs={{16,0},{32,16},{48,32},{64,48},{80,64},{96,80},{112,96},{17,1},{33... | collective-permute-start | bytes 491528 | tf_op jit(solution)/shard_map/ppermute | solution.py:436
  117.1 7.2 %collective-permute-done.10.rows.c = bf16[16,5120]{1,0:T(8,128)(2,1)S(1)} collective-permute-done((bf16[16,5120]{1,0:T(8,128)(2,1)S(1)}, bf16[16,5120]{1,0:T(8,128)(2,1)S(1)}, u32[]{:S(2)}, u32[]{:S(2)}) %collective-permute-start.10) | collective-permute-done | bytes 163872 | tf_op jit(solution)/shard_map/ppermute | solution.py:436
  124.5 15.9 %all_to_all.70 = bf16[8,16,5120]{2,1,0:T(8,128)(2,1)S(1)} all-to-all(bf16[8,16,5120]{2,1,0:T(8,128)(2,1)S(1)} %bitcast.27), channel_id=1, replica_groups={{0,2,4,6,8,10,12,14},{1,3,5,7,9,11,13,15},{16,18,20,22,24,26,28,30},{17..., dimensions={0} | all-to-all | bytes 2621440 | tf_op jit(solution)/shard_map/all_to_all | solution.py:407
  140.6 9.4 %shard_map.111 = (bf16[128,5760]{1,0:T(8,128)(2,1)}, bf16[128,5120]{1,0:T(8,128)(2,1)}, bf16[128,432]{1,0:T(8,128)(2,1)}, bf16[4,128,432]{2,1,0:T(8,128)(2,1)}) custom-call(bf16[128,5120]{1,0:T(8,128)(2,1)S(1)} %bitcast.24, f32[1,5120]{1,0:T(1,128)S(1)} %copy-done.3, f32[1,5120]{1,0:T(1,128)S(1)} %get-tuple-element.93.gain_two, ...), custom_call_target="tpu_custom_call" | custom-call | flops 3397386240 | bytes 15728640 | tf_op jit(solution)/shard_map/pallas_call | solution.py:383
  150.0 14.0 %collective-permute-start.15 = (bf16[128,5120]{1,0:T(8,128)(2,1)}, bf16[128,5120]{1,0:T(8,128)(2,1)}, u32[]{:S(2)}, u32[]{:S(2)}) collective-permute-start(bf16[128,5120]{1,0:T(8,128)(2,1)} %get-tuple-element.107.refs_6_), channel_id=1, source_target_pairs={{0,1},{1,0},{2,3},{3,2},{4,5},{5,4},{6,7},{7,6},{8,9},{9,8},{10,11... | collective-permute-start | bytes 3932168 | tf_op jit(solution)/shard_map/ppermute | solution.py:422
  164.7 6.1 %all-to-all-start.5 = ((bf16[8,16,5760]{2,1,0:T(8,128)(2,1)}), bf16[8,16,5760]{2,1,0:T(8,128)(2,1)S(1)}, u32[]{:S(2)}, u32[]{:S(2)}) async-start(bf16[8,16,5760]{2,1,0:T(8,128)(2,1)} %bitcast.41), calls=%async_computation.5 | async-start | bytes 2949120 | tf_op jit(solution)/shard_map/all_to_all | solution.py:407
  173.3 1.7 collective-permute-start.17
  175.0 2.4 %collective-permute-start.18 = (bf16[16,5120]{1,0:T(8,128)(2,1)}, bf16[16,5120]{1,0:T(8,128)(2,1)S(1)}, u32[]{:S(2)}, u32[]{:S(2)}) collective-permute-start(bf16[16,5120]{1,0:T(8,128)(2,1)} %get-tuple-element.121), channel_id=1, source_target_pairs={{0,4},{1,5},{2,6},{3,7},{4,0},{5,1},{6,2},{7,3},{8,12},{9,13},{10,... | collective-permute-start | bytes 491528 | tf_op jit(solution)/shard_map/ppermute | solution.py:538
  178.6 10.0 %shard_map.112 = (bf16[432,5120]{1,0:T(8,128)(2,1)}, bf16[432,5120]{1,0:T(8,128)(2,1)}) custom-call(bf16[128,5120]{1,0:T(8,128)(2,1)} %get-tuple-element.101.normed_in.refs_0_, bf16[128,5120]{1,0:T(8,128)(2,1)} %collective-permute-done.12.refs_1_, bf16[128,5120]{1,0:T(8,128)(2,1)} %get-tuple-element.103.refs_2_, ...), custom_call_target="tpu_custom_call" | custom-call | flops 4529848320 | bytes 20971520 | tf_op jit(solution)/shard_map/pallas_call | solution.py:544
  188.6 4.1 %all-to-all-done.5 = bf16[8,16,5760]{2,1,0:T(8,128)(2,1)S(1)} async-done(((bf16[8,16,5760]{2,1,0:T(8,128)(2,1)}), bf16[8,16,5760]{2,1,0:T(8,128)(2,1)S(1)}, u32[]{:S(2)}, u32[]{:S(2)}) %all-to-all-start.5) | async-done | bytes 1474592 | tf_op jit(solution)/shard_map/all_to_all | solution.py:407
  193.8 3.9 %collective-permute-done.18.third = bf16[16,5120]{1,0:T(8,128)(2,1)S(1)} collective-permute-done((bf16[16,5120]{1,0:T(8,128)(2,1)}, bf16[16,5120]{1,0:T(8,128)(2,1)S(1)}, u32[]{:S(2)}, u32[]{:S(2)}) %collective-permute-start.18) | collective-permute-done | bytes 163872 | tf_op jit(solution)/shard_map/ppermute | solution.py:538
  197.9 1.6 collective-permute-start.20
  (77 shorter events, 16.1 us)
Async XLA Ops:
  0.6 45.8 %copy-start = (s32[8,16]{1,0:T(8,128)S(1)}, s32[8,16]{1,0:T(8,128)}, u32[]{:S(2)}) copy-start(s32[8,16]{1,0:T(8,128)} %param.11) | copy-start | bytes 1540
  0.6 2.0 collective-permute-start
  2.6 31.1 %collective-permute-start.6 = (bf16[432,5120]{1,0:T(8,128)(2,1)}, bf16[432,5120]{1,0:T(8,128)(2,1)}, u32[]{:S(2)}, u32[]{:S(2)}) collective-permute-start(bf16[432,5120]{1,0:T(8,128)(2,1)} %bitcast.32), channel_id=1, source_target_pairs={{0,1},{1,0},{2,3},{3,2},{4,5},{5,4},{6,7},{7,6},{8,9},{9,8},{10,11... | collective-permute-start | bytes 13271048 | tf_op jit(solution)/shard_map/ppermute | solution.py:422
  3.0 30.8 %collective-permute-start.5 = (bf16[432,5120]{1,0:T(8,128)(2,1)}, bf16[432,5120]{1,0:T(8,128)(2,1)}, u32[]{:S(2)}, u32[]{:S(2)}) collective-permute-start(bf16[432,5120]{1,0:T(8,128)(2,1)} %bitcast.37), channel_id=1, source_target_pairs={{0,1},{1,0},{2,3},{3,2},{4,5},{5,4},{6,7},{7,6},{8,9},{9,8},{10,11... | collective-permute-start | bytes 13271048 | tf_op jit(solution)/shard_map/ppermute | solution.py:422
  5.6 0.7 collective-permute-start.1
  6.3 27.5 %copy-start.3 = (f32[1,5120]{1,0:T(1,128)S(1)}, f32[1,5120]{1,0:T(1,128)}, u32[]{:S(2)}) copy-start(f32[1,5120]{1,0:T(1,128)} %gain.9) | copy-start | bytes 61444
  6.3 24.5 %all-to-all-start = ((bf16[8,16,5120]{2,1,0:T(8,128)(2,1)}), bf16[8,16,5120]{2,1,0:T(8,128)(2,1)S(1)}, u32[]{:S(2)}, u32[]{:S(2)}) async-start(bf16[8,16,5120]{2,1,0:T(8,128)(2,1)} %bitcast.3), calls=%async_computation | async-start | bytes 2621440 | tf_op jit(solution)/shard_map/all_to_all | solution.py:407
  13.8 12.6 %collective-permute-start.2 = (bf16[16,5120]{1,0:T(8,128)(2,1)S(1)}, bf16[16,5120]{1,0:T(8,128)(2,1)S(1)}, u32[]{:S(2)}, u32[]{:S(2)}) collective-permute-start(bf16[16,5120]{1,0:T(8,128)(2,1)S(1)} %get-tuple-element.70.own), channel_id=1, source_target_pairs={{0,2},{1,3},{2,4},{3,5},{4,6},{5,7},{6,0},{7,1},{8,10},{9,11},{10,... | collective-permute-start | bytes 491528 | tf_op jit(solution)/shard_map/ppermute | solution.py:479
  15.3 15.5 %collective-permute-start.3 = (bf16[16,5120]{1,0:T(8,128)(2,1)S(1)}, bf16[16,5120]{1,0:T(8,128)(2,1)S(1)}, u32[]{:S(2)}, u32[]{:S(2)}) collective-permute-start(bf16[16,5120]{1,0:T(8,128)(2,1)S(1)} %get-tuple-element.70.own), channel_id=1, source_target_pairs={{0,4},{1,5},{2,6},{3,7},{4,0},{5,1},{6,2},{7,3},{8,12},{9,13},{10,... | collective-permute-start | bytes 491528 | tf_op jit(solution)/shard_map/ppermute | solution.py:479
  17.7 13.1 %collective-permute-start.4 = (bf16[16,5120]{1,0:T(8,128)(2,1)S(1)}, bf16[16,5120]{1,0:T(8,128)(2,1)S(1)}, u32[]{:S(2)}, u32[]{:S(2)}) collective-permute-start(bf16[16,5120]{1,0:T(8,128)(2,1)S(1)} %get-tuple-element.70.own), channel_id=1, source_target_pairs={{1,7},{3,1},{5,3},{7,5},{9,15},{11,9},{13,11},{15,13},{17,23},{19,... | collective-permute-start | bytes 491528 | tf_op jit(solution)/shard_map/ppermute | solution.py:480
  30.8 11.5 %collective-permute-start.7 = (bf16[32,5120]{1,0:T(8,128)(2,1)S(1)}, bf16[32,5120]{1,0:T(8,128)(2,1)S(1)}, u32[]{:S(2)}, u32[]{:S(2)}) collective-permute-start(bf16[32,5120]{1,0:T(8,128)(2,1)S(1)} %get-tuple-element.77.refs_0_), channel_id=1, source_target_pairs={{0,8},{1,9},{2,10},{3,11},{4,12},{5,13},{6,14},{7,15},{8,0},{9,1},... | collective-permute-start | bytes 983048 | tf_op jit(solution)/shard_map/ppermute | solution.py:483
  42.3 17.3 %copy-start.1 = (bf16[1,16,5120]{2,1,0:T(8,128)(2,1)S(1)}, bf16[1,16,5120]{2,1,0:T(8,128)(2,1)}, u32[]{:S(2)}) copy-start(bf16[1,16,5120]{2,1,0:T(8,128)(2,1)} %param.6) | copy-start | bytes 491524
  42.3 17.3 %all-to-all-start.1 = ((bf16[8,16,5120]{2,1,0:T(8,128)(2,1)}), bf16[8,16,5120]{2,1,0:T(8,128)(2,1)S(1)}, u32[]{:S(2)}, u32[]{:S(2)}) async-start(bf16[8,16,5120]{2,1,0:T(8,128)(2,1)} %bitcast.42), calls=%async_computation.1 | async-start | bytes 2621440 | tf_op jit(solution)/shard_map/all_to_all | solution.py:407
  59.9 11.9 %collective-permute-start.9 = (bf16[32,5120]{1,0:T(8,128)(2,1)S(1)}, bf16[32,5120]{1,0:T(8,128)(2,1)S(1)}, u32[]{:S(2)}, u32[]{:S(2)}) collective-permute-start(bf16[32,5120]{1,0:T(8,128)(2,1)S(1)} %get-tuple-element.80.refs_1_), channel_id=1, source_target_pairs={{0,8},{1,9},{2,10},{3,11},{4,12},{5,13},{6,14},{7,15},{8,0},{9,1},... | collective-permute-start | bytes 983048 | tf_op jit(solution)/shard_map/ppermute | solution.py:494
  60.3 6.3 %collective-permute-start.8 = (bf16[16,5120]{1,0:T(8,128)(2,1)S(1)}, bf16[16,5120]{1,0:T(8,128)(2,1)S(1)}, u32[]{:S(2)}, u32[]{:S(2)}) collective-permute-start(bf16[16,5120]{1,0:T(8,128)(2,1)S(1)} %shard_map.104), channel_id=1, source_target_pairs={{0,16},{16,32},{32,48},{48,64},{64,80},{80,96},{96,112},{1,17},{17... | collective-permute-start | bytes 491528 | tf_op jit(solution)/shard_map/ppermute | solution.py:436
  72.9 16.8 %all-to-all-start.2 = ((bf16[8,16,5120]{2,1,0:T(8,128)(2,1)}), bf16[8,16,5120]{2,1,0:T(8,128)(2,1)S(1)}, u32[]{:S(2)}, u32[]{:S(2)}) async-start(bf16[8,16,5120]{2,1,0:T(8,128)(2,1)} %bitcast.9), calls=%async_computation.2 | async-start | bytes 2621440 | tf_op jit(solution)/shard_map/all_to_all | solution.py:407
  97.5 16.8 %all-to-all-start.3 = ((bf16[8,16,5120]{2,1,0:T(8,128)(2,1)}), bf16[8,16,5120]{2,1,0:T(8,128)(2,1)S(1)}, u32[]{:S(2)}, u32[]{:S(2)}) async-start(bf16[8,16,5120]{2,1,0:T(8,128)(2,1)} %bitcast.43), calls=%async_computation.3 | async-start | bytes 2621440 | tf_op jit(solution)/shard_map/all_to_all | solution.py:407
  114.6 9.7 %collective-permute-start.10 = (bf16[16,5120]{1,0:T(8,128)(2,1)S(1)}, bf16[16,5120]{1,0:T(8,128)(2,1)S(1)}, u32[]{:S(2)}, u32[]{:S(2)}) collective-permute-start(bf16[16,5120]{1,0:T(8,128)(2,1)S(1)} %shard_map.109), channel_id=1, source_target_pairs={{16,0},{32,16},{48,32},{64,48},{80,64},{96,80},{112,96},{17,1},{33... | collective-permute-start | bytes 491528 | tf_op jit(solution)/shard_map/ppermute | solution.py:436
  124.4 15.9 %copy-start.5 = (bf16[64,5120]{1,0:T(8,128)(2,1)S(1)}, bf16[64,5120]{1,0:T(8,128)(2,1)}, u32[]{:S(2)}) copy-start(bf16[64,5120]{1,0:T(8,128)(2,1)} %get-tuple-element.99) | copy-start | bytes 1966084
  140.3 24.3 %collective-permute-start.11 = (bf16[64,5120]{1,0:T(8,128)(2,1)S(1)}, bf16[64,5120]{1,0:T(8,128)(2,1)S(1)}, u32[]{:S(2)}, u32[]{:S(2)}) collective-permute-start(bf16[64,5120]{1,0:T(8,128)(2,1)S(1)} %copy-done.5), channel_id=1, source_target_pairs={{0,8},{1,9},{2,10},{3,11},{4,12},{5,13},{6,14},{7,15},{8,0},{9,1},... | collective-permute-start | bytes 1966088 | tf_op jit(solution)/shard_map/ppermute | solution.py:525
  150.0 24.9 %collective-permute-start.15 = (bf16[128,5120]{1,0:T(8,128)(2,1)}, bf16[128,5120]{1,0:T(8,128)(2,1)}, u32[]{:S(2)}, u32[]{:S(2)}) collective-permute-start(bf16[128,5120]{1,0:T(8,128)(2,1)} %get-tuple-element.107.refs_6_), channel_id=1, source_target_pairs={{0,1},{1,0},{2,3},{3,2},{4,5},{5,4},{6,7},{7,6},{8,9},{9,8},{10,11... | collective-permute-start | bytes 3932168 | tf_op jit(solution)/shard_map/ppermute | solution.py:422
  164.1 13.3 %collective-permute-start.14 = (bf16[128,5120]{1,0:T(8,128)(2,1)}, bf16[128,5120]{1,0:T(8,128)(2,1)}, u32[]{:S(2)}, u32[]{:S(2)}) collective-permute-start(bf16[128,5120]{1,0:T(8,128)(2,1)} %get-tuple-element.105.refs_4_), channel_id=1, source_target_pairs={{0,1},{1,0},{2,3},{3,2},{4,5},{5,4},{6,7},{7,6},{8,9},{9,8},{10,11... | collective-permute-start | bytes 3932168 | tf_op jit(solution)/shard_map/ppermute | solution.py:422
  164.2 14.4 %collective-permute-start.13 = (bf16[128,5120]{1,0:T(8,128)(2,1)}, bf16[128,5120]{1,0:T(8,128)(2,1)}, u32[]{:S(2)}, u32[]{:S(2)}) collective-permute-start(bf16[128,5120]{1,0:T(8,128)(2,1)} %get-tuple-element.103.refs_2_), channel_id=1, source_target_pairs={{0,1},{1,0},{2,3},{3,2},{4,5},{5,4},{6,7},{7,6},{8,9},{9,8},{10,11... | collective-permute-start | bytes 3932168 | tf_op jit(solution)/shard_map/ppermute | solution.py:422
  164.6 14.0 %collective-permute-start.12 = (bf16[128,5120]{1,0:T(8,128)(2,1)}, bf16[128,5120]{1,0:T(8,128)(2,1)}, u32[]{:S(2)}, u32[]{:S(2)}) collective-permute-start(bf16[128,5120]{1,0:T(8,128)(2,1)} %get-tuple-element.101.normed_in.refs_0_), channel_id=1, source_target_pairs={{0,1},{1,0},{2,3},{3,2},{4,5},{5,4},{6,7},{7,6},{8,9},{9,8},{10,11... | collective-permute-start | bytes 3932168 | tf_op jit(solution)/shard_map/ppermute | solution.py:422
  164.7 28.0 %all-to-all-start.5 = ((bf16[8,16,5760]{2,1,0:T(8,128)(2,1)}), bf16[8,16,5760]{2,1,0:T(8,128)(2,1)S(1)}, u32[]{:S(2)}, u32[]{:S(2)}) async-start(bf16[8,16,5760]{2,1,0:T(8,128)(2,1)} %bitcast.41), calls=%async_computation.5 | async-start | bytes 2949120 | tf_op jit(solution)/shard_map/all_to_all | solution.py:407
  170.8 2.5 %collective-permute-start.16 = (bf16[4,128,432]{2,1,0:T(8,128)(2,1)}, bf16[4,128,432]{2,1,0:T(8,128)(2,1)S(1)}, u32[]{:S(2)}, u32[]{:S(2)}) collective-permute-start(bf16[4,128,432]{2,1,0:T(8,128)(2,1)} %get-tuple-element.111), channel_id=1, source_target_pairs={{0,1},{1,0},{2,3},{3,2},{4,5},{5,4},{6,7},{7,6},{8,9},{9,8},{10,11... | collective-permute-start | bytes 1327112 | tf_op jit(solution)/shard_map/ppermute | solution.py:422
  173.3 20.5 %collective-permute-start.17 = (bf16[16,5120]{1,0:T(8,128)(2,1)}, bf16[16,5120]{1,0:T(8,128)(2,1)S(1)}, u32[]{:S(2)}, u32[]{:S(2)}) collective-permute-start(bf16[16,5120]{1,0:T(8,128)(2,1)} %get-tuple-element.120), channel_id=1, source_target_pairs={{0,2},{1,3},{2,4},{3,5},{4,6},{5,7},{6,0},{7,1},{8,10},{9,11},{10,... | collective-permute-start | bytes 491528 | tf_op jit(solution)/shard_map/ppermute | solution.py:538
  175.0 22.8 %collective-permute-start.18 = (bf16[16,5120]{1,0:T(8,128)(2,1)}, bf16[16,5120]{1,0:T(8,128)(2,1)S(1)}, u32[]{:S(2)}, u32[]{:S(2)}) collective-permute-start(bf16[16,5120]{1,0:T(8,128)(2,1)} %get-tuple-element.121), channel_id=1, source_target_pairs={{0,4},{1,5},{2,6},{3,7},{4,0},{5,1},{6,2},{7,3},{8,12},{9,13},{10,... | collective-permute-start | bytes 491528 | tf_op jit(solution)/shard_map/ppermute | solution.py:538
  177.4 20.4 %collective-permute-start.19 = (bf16[16,5120]{1,0:T(8,128)(2,1)}, bf16[16,5120]{1,0:T(8,128)(2,1)S(1)}, u32[]{:S(2)}, u32[]{:S(2)}) collective-permute-start(bf16[16,5120]{1,0:T(8,128)(2,1)} %get-tuple-element.122), channel_id=1, source_target_pairs={{0,6},{1,7},{2,0},{3,1},{4,2},{5,3},{6,4},{7,5},{8,14},{9,15},{10,... | collective-permute-start | bytes 491528 | tf_op jit(solution)/shard_map/ppermute | solution.py:538
  188.6 9.1 %copy-start.4 = (bf16[16,5120]{1,0:T(8,128)(2,1)S(1)}, bf16[16,5120]{1,0:T(8,128)(2,1)}, u32[]{:S(2)}) copy-start(bf16[16,5120]{1,0:T(8,128)(2,1)} %get-tuple-element.116.own_rows) | copy-start | bytes 491524
  197.9 2.8 %collective-permute-start.20 = (bf16[16,5120]{1,0:T(8,128)(2,1)S(1)}, bf16[16,5120]{1,0:T(8,128)(2,1)S(1)}, u32[]{:S(2)}, u32[]{:S(2)}) collective-permute-start(bf16[16,5120]{1,0:T(8,128)(2,1)S(1)} %shard_map.115.own), channel_id=1, source_target_pairs={{0,1},{1,0},{2,3},{3,2},{4,5},{5,4},{6,7},{7,6},{8,9},{9,8},{10,11... | collective-permute-start | bytes 491528 | tf_op jit(solution)/shard_map/ppermute | solution.py:422
  199.5 1.2 collective-permute-start.21
  (2 other events, 12.1 us)
